TPU v7x, 128 devices: a whole 4x4x4 slice. The times are simulated.
128 devices in a mesh: dp: 32 (over z_hi, y, x), head: 2 (over core), tensor: 2 (over z_lo).
Axes of the slice: x: 4, y: 4, z: 4 (z_hi: 2, z_lo: 2; z = z_hi * 2 + z_lo), core: 2. Of those that a mesh axis runs over, the one named last changes fastest.
Arguments:
- tokens: bfloat16 [4096, 2048], P('dp'), may hold values from -6 to 6
- gain_attn: bfloat16 [2048], P('dp'), may hold values from 0.5 to 1.5
- w_query: bfloat16 [2048, 2048], P('dp', 'head'), may hold values from -0.125 to 0.125
- w_key: bfloat16 [2048, 512], P('dp', 'head'), may hold values from -0.125 to 0.125
- w_value: bfloat16 [2048, 512], P('dp', 'head'), may hold values from -0.125 to 0.125
- gain_query: bfloat16 [64], replicated, may hold values from 0.5 to 1.5
- gain_key: bfloat16 [64], replicated, may hold values from 0.5 to 1.5
- w_out: bfloat16 [2048, 2048], P('dp', 'head'), may hold values from -0.75 to 0.75
- gain_ffn: bfloat16 [2048], P('dp'), may hold values from 0.5 to 1.5
- w_gate: bfloat16 [2048, 8192], P('dp', 'tensor'), may hold values from -0.125 to 0.125
- w_up: bfloat16 [2048, 8192], P('dp', 'tensor'), may hold values from -0.125 to 0.125
- w_down: bfloat16 [2048, 8192], P('dp', 'tensor'), may hold values from -0.0625 to 0.0625
- cotangent: bfloat16 [4096, 2048], P('dp'), may hold values from -6 to 6
Outputs:
- output: bfloat16 [4096, 2048], P('dp')
- token_input_gradient: float32 [4096, 2048], P('dp')
- attention_gain_gradient: float32 [2048], P('dp')
- grad_query: float32 [2048, 2048], P('dp', 'head')
- grad_key: float32 [2048, 512], P('dp', 'head')
- grad_value: float32 [2048, 512], P('dp', 'head')
- grad_gain_query: float32 [64], replicated
- grad_gain_key: float32 [64], replicated
- grad_out: float32 [2048, 2048], P('dp', 'head')
- feedforward_gain_gradient: float32 [2048], P('dp')
- grad_gate: float32 [2048, 8192], P('dp', 'tensor')
- grad_up: float32 [2048, 8192], P('dp', 'tensor')
- grad_down: float32 [2048, 8192], P('dp', 'tensor')
All inputs are finite; a program needn't handle non-finite values.
Results may differ from a plain program's by a relative error of at most 0.028.
Values may be sent and summed in bfloat16 or wider, within the bound.
A program may use at most 192 MiB of HBM per device.

v0:
```python
import jax
import jax.numpy as jnp
from jax import lax
from jax.sharding import PartitionSpec as P

eps = 1e-05
theta_base = 1000000.0


def tables(seq, depth):
    half = depth // 2
    position = jnp.arange(seq, dtype=jnp.float32)
    inverse = theta_base ** (-(jnp.arange(half, dtype=jnp.float32) * 2.0) / depth)
    angles = position[:, None] * inverse[None, :]
    return (jnp.cos(angles)[:, None, :], jnp.sin(angles)[:, None, :])


def rotate(value, cosine, sine):
    half = value.shape[-1] // 2
    first = value[..., :half]
    second = value[..., half:]
    return jnp.concatenate(
        [first * cosine - second * sine, second * cosine + first * sine], axis=-1
    )


def head_prep(raw, norm_gain, cosine, sine):
    normed = raw * lax.rsqrt(jnp.mean(raw * raw, axis=-1, keepdims=True) + eps) * norm_gain
    return rotate(normed, cosine, sine)


def over_rows(left, right):
    return lax.dot_general(
        left, right, (((0,), (0,)), ((), ())), preferred_element_type=jnp.float32
    )


def over_cols(left, right):
    return lax.dot_general(
        left, right, (((1,), (1,)), ((), ())), preferred_element_type=jnp.float32
    )


def norm_backward_pass(normalized_gradient, unit_rows, reciprocal_scale, norm_gain):
    scaled_rows = normalized_gradient * norm_gain
    return reciprocal_scale * (
        scaled_rows - unit_rows * jnp.mean(scaled_rows * unit_rows, axis=-1, keepdims=True)
    )


def on_device(
    tokens,
    gain_attn,
    w_query,
    w_key,
    w_value,
    gain_query,
    gain_key,
    w_out,
    gain_ffn,
    w_gate,
    w_up,
    w_down,
    cotangent,
):
    seq = tokens.shape[0]
    depth = gain_query.shape[0]
    scale = depth ** (-0.5)
    attention_gain_value, wq, wk, wv, wo = (
        lax.all_gather(gain_attn, "dp", axis=0, tiled=True),
        lax.all_gather(w_query, "dp", axis=0, tiled=True),
        lax.all_gather(w_key, "dp", axis=0, tiled=True),
        lax.all_gather(w_value, "dp", axis=0, tiled=True),
        lax.all_gather(w_out, "dp", axis=0, tiled=True),
    )
    q_heads = wq.shape[1] // depth
    kv_heads = wk.shape[1] // depth
    group = q_heads // kv_heads
    cosine, sine = tables(seq, depth)
    causal = lax.broadcasted_iota(jnp.int32, (seq, seq), 0) >= lax.broadcasted_iota(
        jnp.int32, (seq, seq), 1
    )
    input_rows = tokens.astype(jnp.float32)
    first_reciprocal_scale = lax.rsqrt(
        jnp.mean(input_rows * input_rows, axis=-1, keepdims=True) + eps
    )
    first_unit_rows = input_rows * first_reciprocal_scale
    first_normed_rows = (first_unit_rows * attention_gain_value.astype(jnp.float32)).astype(
        jnp.bfloat16
    )
    q_raw = jnp.dot(first_normed_rows, wq, preferred_element_type=jnp.float32).reshape(
        seq, q_heads, depth
    )
    k_raw = jnp.dot(first_normed_rows, wk, preferred_element_type=jnp.float32).reshape(
        seq, kv_heads, depth
    )
    v_raw = jnp.dot(first_normed_rows, wv, preferred_element_type=jnp.float32)

    def prepare(raw, norm_gain):
        return head_prep(raw, norm_gain, cosine, sine)

    q_rot, pull_query = jax.vjp(prepare, q_raw, gain_query.astype(jnp.float32))
    k_rot, pull_key = jax.vjp(prepare, k_raw, gain_key.astype(jnp.float32))
    queries = q_rot.astype(jnp.bfloat16).reshape(seq, kv_heads, group, depth)
    keys = k_rot.astype(jnp.bfloat16)
    values = v_raw.astype(jnp.bfloat16).reshape(seq, kv_heads, depth)
    scores = jnp.einsum("skgd,tkd->kgst", queries, keys, preferred_element_type=jnp.float32) * scale
    scores = jnp.where(causal, scores, -1e30)
    top = jnp.max(scores, axis=-1, keepdims=True)
    expo = jnp.exp(scores - top)
    total = jnp.sum(expo, axis=-1, keepdims=True)
    logsum = top + jnp.log(total)
    probs_low = (expo / total).astype(jnp.bfloat16)
    attn = jnp.einsum("kgst,tkd->skgd", probs_low, values, preferred_element_type=jnp.float32)
    attn = attn.reshape(seq, q_heads * depth).astype(jnp.bfloat16)
    branch = lax.psum(over_cols(attn, wo), "head")
    hidden_state = input_rows + branch
    feedforward_gain_value, wg, wu, wd = (
        lax.all_gather(gain_ffn, "dp", axis=0, tiled=True),
        lax.all_gather(w_gate, "dp", axis=0, tiled=True),
        lax.all_gather(w_up, "dp", axis=0, tiled=True),
        lax.all_gather(w_down, "dp", axis=0, tiled=True),
    )
    second_reciprocal_scale = lax.rsqrt(
        jnp.mean(hidden_state * hidden_state, axis=-1, keepdims=True) + eps
    )
    second_unit_rows = hidden_state * second_reciprocal_scale
    second_normed_rows = (second_unit_rows * feedforward_gain_value.astype(jnp.float32)).astype(
        jnp.bfloat16
    )
    gate = jnp.dot(second_normed_rows, wg, preferred_element_type=jnp.float32)
    up_proj = jnp.dot(second_normed_rows, wu, preferred_element_type=jnp.float32)
    sigma = jax.nn.sigmoid(gate)
    swish = gate * sigma
    active = (swish * up_proj).astype(jnp.bfloat16)
    ffn = lax.psum(over_cols(active, wd).astype(jnp.bfloat16), "tensor").astype(jnp.float32)
    output = (hidden_state + ffn).astype(jnp.bfloat16)
    feedforward_gain_value, wg, wu, wd = (
        lax.all_gather(gain_ffn, "dp", axis=0, tiled=True),
        lax.all_gather(w_gate, "dp", axis=0, tiled=True),
        lax.all_gather(w_up, "dp", axis=0, tiled=True),
        lax.all_gather(w_down, "dp", axis=0, tiled=True),
    )
    grad_act = jnp.dot(cotangent, wd, preferred_element_type=jnp.float32)
    grad_gate_v = (grad_act * up_proj * sigma * (1.0 + gate * (1.0 - sigma))).astype(jnp.bfloat16)
    grad_up_v = (grad_act * swish).astype(jnp.bfloat16)
    second_normed_gradient = lax.psum(
        over_cols(grad_gate_v, wg) + over_cols(grad_up_v, wu), "tensor"
    )
    feedforward_gain_gradient = jnp.sum(second_normed_gradient * second_unit_rows, axis=0)
    hidden_gradient = cotangent.astype(jnp.float32) + norm_backward_pass(
        second_normed_gradient,
        second_unit_rows,
        second_reciprocal_scale,
        feedforward_gain_value.astype(jnp.float32),
    )
    grad_down = over_rows(cotangent, active)
    grad_gate = over_rows(second_normed_rows, grad_gate_v)
    grad_up = over_rows(second_normed_rows, grad_up_v)
    attention_gain_value, wq, wk, wv, wo = (
        lax.all_gather(gain_attn, "dp", axis=0, tiled=True),
        lax.all_gather(w_query, "dp", axis=0, tiled=True),
        lax.all_gather(w_key, "dp", axis=0, tiled=True),
        lax.all_gather(w_value, "dp", axis=0, tiled=True),
        lax.all_gather(w_out, "dp", axis=0, tiled=True),
    )
    grad_branch = hidden_gradient.astype(jnp.bfloat16)
    grad_out = over_rows(grad_branch, attn)
    grad_attn = jnp.dot(grad_branch, wo, preferred_element_type=jnp.float32).astype(jnp.bfloat16)
    grad_attn = grad_attn.reshape(seq, kv_heads, group, depth)
    again_scores = (
        jnp.einsum("skgd,tkd->kgst", queries, keys, preferred_element_type=jnp.float32) * scale
    )
    probs = jnp.exp(jnp.where(causal, again_scores, -1e30) - logsum)
    probs_low = probs.astype(jnp.bfloat16)
    grad_probs = jnp.einsum("skgd,tkd->kgst", grad_attn, values, preferred_element_type=jnp.float32)
    grad_values = jnp.einsum(
        "kgst,skgd->tkd", probs_low, grad_attn, preferred_element_type=jnp.float32
    )
    grad_scores = probs * (grad_probs - jnp.sum(probs * grad_probs, axis=-1, keepdims=True))
    grad_scores = grad_scores.astype(jnp.bfloat16)
    grad_queries = (
        jnp.einsum("kgst,tkd->skgd", grad_scores, keys, preferred_element_type=jnp.float32) * scale
    )
    grad_keys = (
        jnp.einsum("kgst,skgd->tkd", grad_scores, queries, preferred_element_type=jnp.float32)
        * scale
    )
    grad_q_raw, grad_gq = pull_query(grad_queries.reshape(seq, q_heads, depth))
    grad_k_raw, grad_gk = pull_key(grad_keys)
    grad_gq, grad_gk = lax.psum((grad_gq, grad_gk), ("dp", "head"))
    grad_q_low = grad_q_raw.reshape(seq, q_heads * depth).astype(jnp.bfloat16)
    grad_k_low = grad_k_raw.reshape(seq, kv_heads * depth).astype(jnp.bfloat16)
    grad_v_low = grad_values.reshape(seq, kv_heads * depth).astype(jnp.bfloat16)
    grad_query = over_rows(first_normed_rows, grad_q_low)
    grad_key = over_rows(first_normed_rows, grad_k_low)
    grad_value = over_rows(first_normed_rows, grad_v_low)
    partial_xn1 = over_cols(grad_q_low, wq) + over_cols(grad_k_low, wk) + over_cols(grad_v_low, wv)
    first_normed_gradient = lax.psum(partial_xn1.astype(jnp.bfloat16), "head").astype(jnp.float32)
    attention_gain_gradient = jnp.sum(first_normed_gradient * first_unit_rows, axis=0)
    token_input_gradient = hidden_gradient + norm_backward_pass(
        first_normed_gradient,
        first_unit_rows,
        first_reciprocal_scale,
        attention_gain_value.astype(jnp.float32),
    )
    shares = (
        lax.psum_scatter(
            attention_gain_gradient.astype(jnp.bfloat16), "dp", scatter_dimension=0, tiled=True
        ).astype(jnp.float32),
        lax.psum_scatter(
            grad_query.astype(jnp.bfloat16), "dp", scatter_dimension=0, tiled=True
        ).astype(jnp.float32),
        lax.psum_scatter(
            grad_key.astype(jnp.bfloat16), "dp", scatter_dimension=0, tiled=True
        ).astype(jnp.float32),
        lax.psum_scatter(
            grad_value.astype(jnp.bfloat16), "dp", scatter_dimension=0, tiled=True
        ).astype(jnp.float32),
        lax.psum_scatter(
            grad_out.astype(jnp.bfloat16), "dp", scatter_dimension=0, tiled=True
        ).astype(jnp.float32),
        lax.psum_scatter(
            feedforward_gain_gradient.astype(jnp.bfloat16), "dp", scatter_dimension=0, tiled=True
        ).astype(jnp.float32),
        lax.psum_scatter(
            grad_gate.astype(jnp.bfloat16), "dp", scatter_dimension=0, tiled=True
        ).astype(jnp.float32),
        lax.psum_scatter(
            grad_up.astype(jnp.bfloat16), "dp", scatter_dimension=0, tiled=True
        ).astype(jnp.float32),
        lax.psum_scatter(
            grad_down.astype(jnp.bfloat16), "dp", scatter_dimension=0, tiled=True
        ).astype(jnp.float32),
    )
    return (
        output,
        token_input_gradient,
        shares[0],
        shares[1],
        shares[2],
        shares[3],
        grad_gq,
        grad_gk,
        shares[4],
        shares[5],
        shares[6],
        shares[7],
        shares[8],
    )


def solution(mesh):
    return jax.shard_map(
        on_device,
        mesh=mesh,
        in_specs=(
            P("dp", None),
            P("dp"),
            P("dp", "head"),
            P("dp", "head"),
            P("dp", "head"),
            P(),
            P(),
            P("dp", "head"),
            P("dp"),
            P("dp", "tensor"),
            P("dp", "tensor"),
            P("dp", "tensor"),
            P("dp", None),
        ),
        out_specs=(
            P("dp", None),
            P("dp", None),
            P("dp"),
            P("dp", "head"),
            P("dp", "head"),
            P("dp", "head"),
            P(),
            P(),
            P("dp", "head"),
            P("dp"),
            P("dp", "tensor"),
            P("dp", "tensor"),
            P("dp", "tensor"),
        ),
        check_vma=False,
    )
```

profile of v0, /device:TPU:0, one launch (start us, length us, event | category | flops | bytes accessed | tf_op | source)
XLA Modules:
  0.0 2402.1 jit_solution(8746365496680299147)
XLA Ops:
  15.1 98.7 %all-reduce.10 = (bf16[2048]{0:T(1024)(128)(2,1)S(1)}, bf16[2048]{0:T(1024)(128)(2,1)S(1)}) all-reduce(bf16[2048]{0:T(1024)(128)(2,1)S(1)} %dynamic-update-slice, bf16[2048]{0:T(1024)(128)(2,1)S(1)} %dynamic-update-slice.1), channel_id=1, replica_groups=mesh['dp'=32,'head'=2,'tensor'=2] {'dp'}, use_global_device_ids=true, to_apply=%add.4 | all-reduce | flops 4096 | bytes 16384
  117.1 30.6 %all-gather.10.cloned.1.call-done = bf16[2048,256]{1,0:T(8,128)(2,1)} async-done(((bf16[64,256]{1,0:T(8,128)(2,1)}), bf16[2048,256]{1,0:T(8,128)(2,1)}) %all-gather.10.cloned.1.call-update) | async-done | bytes 1048592 | tf_op jit(solution)/shard_map/all_gather | solution.py:72
  150.4 79.7 %all-gather.12.cloned.1.call-done = bf16[2048,1024]{1,0:T(8,128)(2,1)} async-done(((bf16[64,1024]{1,0:T(8,128)(2,1)}), bf16[2048,1024]{1,0:T(8,128)(2,1)}) %all-gather.12.cloned.1.call-update) | async-done | bytes 4194320 | tf_op jit(solution)/shard_map/all_gather | solution.py:71
  230.1 4.0 multiply_reduce_fusion.6
  235.8 76.5 %all-gather.14.cloned.1.call-done = bf16[2048,1024]{1,0:T(8,128)(2,1)} async-done(((bf16[64,1024]{1,0:T(8,128)(2,1)}), bf16[2048,1024]{1,0:T(8,128)(2,1)}) %all-gather.14.cloned.1.call-update) | async-done | bytes 4194320 | tf_op jit(solution)/shard_map/all_gather | solution.py:74
  312.3 4.7 fusion.44
  319.3 19.7 all-reduce.16.cloned.1.call-done
  340.7 159.6 %all-gather.18.cloned.1.call-done = bf16[2048,4096]{1,0:T(8,128)(2,1)} async-done(((bf16[64,4096]{1,0:T(8,128)(2,1)}), bf16[2048,4096]{1,0:T(8,128)(2,1)}) %all-gather.18.cloned.1.call-update) | async-done | bytes 16777232 | tf_op jit(solution)/shard_map/all_gather | solution.py:121
  500.3 9.4 fusion.46
  509.7 148.3 %all-gather.16.cloned.1.call-done = bf16[2048,4096]{1,0:T(8,128)(2,1)} async-done(((bf16[64,4096]{1,0:T(8,128)(2,1)}), bf16[2048,4096]{1,0:T(8,128)(2,1)}) %all-gather.16.cloned.1.call-update) | async-done | bytes 16777232 | tf_op jit(solution)/shard_map/all_gather | solution.py:120
  658.0 9.5 fusion.45
  667.5 148.3 %all-gather.20.cloned.1.call-done = bf16[2048,4096]{1,0:T(8,128)(2,1)} async-done(((bf16[64,4096]{1,0:T(8,128)(2,1)}), bf16[2048,4096]{1,0:T(8,128)(2,1)}) %all-gather.20.cloned.1.call-update) | async-done | bytes 16777232 | tf_op jit(solution)/shard_map/all_gather | solution.py:122
  815.7 12.2 multiply_convert_fusion
  828.0 12.9 fusion.47
  840.9 12.9 convolution_add_fusion.1
  853.9 12.6 convolution_convert_fusion.6
  867.0 31.5 %all-reduce.20.cloned.1.call-done = f32[128,2048]{1,0:T(8,128)} async-done(((f32[128,2048]{1,0:T(8,128)}), f32[128,2048]{1,0:T(8,128)}) %all-reduce.20.cloned.1.call-update) | async-done | bytes 1048592 | tf_op jit(solution)/shard_map/psum | solution.py:147
  900.6 37.0 %all-reduce.18.cloned.1.call-done = bf16[128,2048]{1,0:T(8,128)(2,1)} async-done(((bf16[128,2048]{1,0:T(8,128)(2,1)}), bf16[128,2048]{1,0:T(8,128)(2,1)}) %all-reduce.18.cloned.1.call-update) | async-done | bytes 524304 | tf_op jit(solution)/shard_map/psum | solution.py:136
  952.5 3.3 convolution_convert_fusion.2
  955.9 3.4 convolution_convert_fusion.3
  959.4 9.2 convert_bitcast_fusion
  968.6 20.8 copy.72
  990.6 8.2 convolution_convert_fusion
  1000.0 8.1 convolution_convert_fusion.1
  1008.9 171.4 %all-reduce.8 = (f32[64]{0:T(128)}, f32[64]{0:T(128)}) all-reduce(f32[64]{0:T(128)S(1)} %copy-done.38, f32[64]{0:T(128)S(1)} %copy-done.37), channel_id=1, replica_groups=mesh['dp'=32,'head'=2,'tensor'=2] {'dp','head'}, use_global_device_ids=true, to_apply=%region_21.22 | all-reduce | flops 128 | bytes 1024 | tf_op jit(solution)/shard_map/psum | solution.py:191
  1181.7 90.0 %all-reduce.9 = (bf16[2048]{0:T(1024)(128)(2,1)S(1)}, bf16[2048]{0:T(1024)(128)(2,1)S(1)}) all-reduce(bf16[2048]{0:T(1024)(128)(2,1)S(1)} %get-tuple-element.54, bf16[2048]{0:T(1024)(128)(2,1)S(1)} %copy-done.30), channel_id=2, replica_groups=mesh['dp'=32,'head'=2,'tensor'=2] {'dp'}, use_global_device_ids=true, to_apply=%region_16.17.clone | all-reduce | flops 4096 | bytes 16384
  1276.1 70.2 %reduce-scatter.14.cloned.1.call-done = bf16[64,256]{1,0:T(8,128)(2,1)} async-done(((bf16[2048,256]{1,0:T(8,128)(2,1)}), bf16[64,256]{1,0:T(8,128)(2,1)}) %reduce-scatter.14.cloned.1.call-update) | async-done | bytes 32784 | tf_op jit(solution)/shard_map/reduce_scatter | solution.py:217
  1347.7 188.0 %reduce-scatter.16.cloned.1.call-done = bf16[64,1024]{1,0:T(8,128)(2,1)} async-done(((bf16[2048,1024]{1,0:T(8,128)(2,1)}), bf16[64,1024]{1,0:T(8,128)(2,1)}) %reduce-scatter.16.cloned.1.call-update) | async-done | bytes 131088 | tf_op jit(solution)/shard_map/reduce_scatter | solution.py:220
  1537.3 187.6 %reduce-scatter.10.cloned.1.call-done = bf16[64,1024]{1,0:T(8,128)(2,1)} async-done(((bf16[2048,1024]{1,0:T(8,128)(2,1)}), bf16[64,1024]{1,0:T(8,128)(2,1)}) %reduce-scatter.10.cloned.1.call-update) | async-done | bytes 131088 | tf_op jit(solution)/shard_map/reduce_scatter | solution.py:211
  1726.5 219.7 %reduce-scatter.22.cloned.1.call-done = bf16[64,4096]{1,0:T(8,128)(2,1)} async-done(((bf16[2048,4096]{1,0:T(8,128)(2,1)}), bf16[64,4096]{1,0:T(8,128)(2,1)}) %reduce-scatter.22.cloned.1.call-update) | async-done | bytes 524304
  1949.0 221.5 %reduce-scatter.20.cloned.1.call-done = bf16[64,4096]{1,0:T(8,128)(2,1)} async-done(((bf16[2048,4096]{1,0:T(8,128)(2,1)}), bf16[64,4096]{1,0:T(8,128)(2,1)}) %reduce-scatter.20.cloned.1.call-update) | async-done | bytes 524304 | tf_op jit(solution)/shard_map/reduce_scatter | solution.py:229
  2172.5 220.5 %reduce-scatter.18.cloned.1.call-done = bf16[64,4096]{1,0:T(8,128)(2,1)} async-done(((bf16[2048,4096]{1,0:T(8,128)(2,1)}), bf16[64,4096]{1,0:T(8,128)(2,1)}) %reduce-scatter.18.cloned.1.call-update) | async-done | bytes 524304 | tf_op jit(solution)/shard_map/reduce_scatter | solution.py:226
  (182 shorter events, 55.8 us)
Async XLA Ops:
  7.2 222.9 %copy-start = (bf16[128,2048]{1,0:T(8,128)(2,1)S(1)}, bf16[128,2048]{1,0:T(8,128)(2,1)}, u32[]{:S(2)}) copy-start(bf16[128,2048]{1,0:T(8,128)(2,1)} %param.13) | copy-start | bytes 1572868
  7.2 108.0 %all-gather.8.cloned.1.call-start = ((), (), s32[]{:S(2)}) async-start(), calls=%async_computation.7 | async-start | bytes 1081344 | tf_op jit(solution)/shard_map/all_gather | solution.py:73
  7.9 139.8 %all-gather.10.cloned.1.call-start = ((), (), s32[]{:S(2)}) async-start(), calls=%async_computation.8 | async-start | bytes 1081344 | tf_op jit(solution)/shard_map/all_gather | solution.py:72
  8.7 221.4 %all-gather.12.cloned.1.call-start = ((), (), s32[]{:S(2)}) async-start(), calls=%async_computation.9 | async-start | bytes 4325376 | tf_op jit(solution)/shard_map/all_gather | solution.py:71
  9.4 302.9 %all-gather.14.cloned.1.call-start = ((), (), s32[]{:S(2)}) async-start(), calls=%async_computation.10 | async-start | bytes 4325376 | tf_op jit(solution)/shard_map/all_gather | solution.py:74
  10.0 329.1 %all-reduce.16.cloned.1.call-start = ((), (), s32[]{:S(2)}) async-start(), calls=%async_computation.11 | async-start | bytes 2097152 | tf_op jit(solution)/shard_map/psum | solution.py:116
  10.7 223.4 %copy-start.33 = (f32[64]{0:T(128)}, f32[64]{0:T(128)S(1)}, u32[]{:S(2)}) copy-start(f32[64]{0:T(128)S(1)} %convert_element_type.163) | copy-start | bytes 772
  11.4 139.0 %copy-start.35 = (f32[64]{0:T(128)}, f32[64]{0:T(128)S(1)}, u32[]{:S(2)}) copy-start(f32[64]{0:T(128)S(1)} %convert_element_type.162) | copy-start | bytes 772
  115.0 119.0 %copy-start.28 = (f32[128]{0:T(128)}, f32[128]{0:T(128)S(1)}, u32[]{:S(2)}) copy-start(f32[128]{0:T(128)S(1)} %add_rsqrt_fusion.1) | copy-start | bytes 1540
  117.1 118.4 %copy-start.16 = (bf16[128,256]{0,1:T(8,128)(2,1)}, bf16[128,256]{0,1:T(8,128)(2,1)S(1)}, u32[]{:S(2)}) copy-start(bf16[128,256]{0,1:T(8,128)(2,1)S(1)} %copy.53) | copy-start | bytes 196612
  150.4 84.9 %copy-start.18 = (bf16[128,4,32]{0,2,1:T(8,128)(2,1)}, bf16[128,4,32]{0,2,1:T(8,128)(2,1)S(1)}, u32[]{:S(2)}) copy-start(bf16[128,4,32]{0,2,1:T(8,128)(2,1)S(1)} %get-tuple-element.79) | copy-start | bytes 98308
  150.4 84.9 %copy-start.20 = (bf16[128,4,32]{0,2,1:T(8,128)(2,1)}, bf16[128,4,32]{0,2,1:T(8,128)(2,1)S(1)}, u32[]{:S(2)}) copy-start(bf16[128,4,32]{0,2,1:T(8,128)(2,1)S(1)} %get-tuple-element.80) | copy-start | bytes 98308
  234.9 82.1 %copy-start.14 = (bf16[128,16,32]{0,2,1:T(8,128)(2,1)}, bf16[128,16,32]{0,2,1:T(8,128)(2,1)S(1)}, u32[]{:S(2)}) copy-start(bf16[128,16,32]{0,2,1:T(8,128)(2,1)S(1)} %get-tuple-element.76) | copy-start | bytes 393220
  235.3 81.7 %copy-start.24 = (f32[4,4,128]{2,1,0:T(4,128)}, f32[4,4,128]{2,1,0:T(4,128)S(1)}, u32[]{:S(2)}) copy-start(f32[4,4,128]{2,1,0:T(4,128)S(1)} %get-tuple-element.89) | copy-start | bytes 24580
  235.8 104.7 %copy-start.12 = (bf16[4,64,4,128]{3,1,2,0:T(8,128)(2,1)}, bf16[4,64,4,128]{3,1,2,0:T(8,128)(2,1)S(1)}, u32[]{:S(2)}) copy-start(bf16[4,64,4,128]{3,1,2,0:T(8,128)(2,1)S(1)} %convolution_convert_fusion.7) | copy-start | bytes 786436
  317.0 183.3 %all-gather.18.cloned.1.call-start = ((), (), s32[]{:S(2)}) async-start(), calls=%async_computation.13 | async-start | bytes 17301504 | tf_op jit(solution)/shard_map/all_gather | solution.py:121
  317.6 340.4 %all-gather.16.cloned.1.call-start = ((), (), s32[]{:S(2)}) async-start(), calls=%async_computation.12 | async-start | bytes 17301504 | tf_op jit(solution)/shard_map/all_gather | solution.py:120
  318.3 497.4 %all-gather.20.cloned.1.call-start = ((), (), s32[]{:S(2)}) async-start(), calls=%async_computation.14 | async-start | bytes 17301504 | tf_op jit(solution)/shard_map/all_gather | solution.py:122
  319.1 579.4 %all-reduce.20.cloned.1.call-start = ((), (), s32[]{:S(2)}) async-start(), calls=%async_computation.16 | async-start | bytes 2097152 | tf_op jit(solution)/shard_map/psum | solution.py:147
  853.8 83.8 %all-reduce.18.cloned.1.call-start = ((), (), s32[]{:S(2)}) async-start(), calls=%async_computation.15 | async-start | bytes 1048576 | tf_op jit(solution)/shard_map/psum | solution.py:136
  853.9 13.0 copy-start.25
  866.5 313.8 %all-reduce.22.cloned.1.call-start = ((), (), s32[]{:S(2)}) async-start(), calls=%async_computation.17 | async-start | bytes 1048576 | tf_op jit(solution)/shard_map/psum | solution.py:199
  937.7 3.8 copy-start.2
  949.2 325.5 %reduce-scatter.12.cloned.1.call-start = ((), (), s32[]{:S(2)}) async-start(), calls=%async_computation.19 | async-start | bytes 1081344 | tf_op jit(solution)/shard_map/reduce_scatter | solution.py:214
  950.8 395.4 %reduce-scatter.14.cloned.1.call-start = ((), (), s32[]{:S(2)}) async-start(), calls=%async_computation.20 | async-start | bytes 1081344 | tf_op jit(solution)/shard_map/reduce_scatter | solution.py:217
  952.4 583.2 %reduce-scatter.16.cloned.1.call-start = ((), (), s32[]{:S(2)}) async-start(), calls=%async_computation.21 | async-start | bytes 4325376 | tf_op jit(solution)/shard_map/reduce_scatter | solution.py:220
  955.8 3.6 copy-start.7
  955.8 769.0 %reduce-scatter.10.cloned.1.call-start = ((), (), s32[]{:S(2)}) async-start(), calls=%async_computation.18 | async-start | bytes 4325376 | tf_op jit(solution)/shard_map/reduce_scatter | solution.py:211
  959.3 986.8 %reduce-scatter.22.cloned.1.call-start = ((), (), s32[]{:S(2)}) async-start(), calls=%async_computation.24 | async-start | bytes 17301504
  989.4 1181.0 %reduce-scatter.20.cloned.1.call-start = ((), (), s32[]{:S(2)}) async-start(), calls=%async_computation.23 | async-start | bytes 17301504 | tf_op jit(solution)/shard_map/reduce_scatter | solution.py:229
  998.8 1394.2 %reduce-scatter.18.cloned.1.call-start = ((), (), s32[]{:S(2)}) async-start(), calls=%async_computation.22 | async-start | bytes 17301504 | tf_op jit(solution)/shard_map/reduce_scatter | solution.py:226
  1008.2 173.6 %copy-start.30 = (bf16[2048]{0:T(1024)(128)(2,1)S(1)}, bf16[2048]{0:T(1024)(128)(2,1)}, u32[]{:S(2)}) copy-start(bf16[2048]{0:T(1024)(128)(2,1)} %get-tuple-element.52) | copy-start | bytes 12292
  (25 other events, 41.9 us)
Sparse Core Ops, SparseCore 0:
  11.0 69.7 all-gather.7
  83.8 63.8 all-gather.9
  150.7 79.3 all-gather.11
  232.9 79.3 all-gather.13
  317.1 21.8 all-reduce.15
  342.3 157.9 all-gather.17
  503.7 154.2 all-gather.15
  661.4 154.2 all-gather.19
  854.0 44.4 all-reduce.19
  901.3 36.2 all-reduce.17
  949.3 25.2 all-reduce.21
  976.8 186.7 reduce-scatter.11
  1166.1 180.1 reduce-scatter.13
  1348.5 187.1 reduce-scatter.15
  1537.9 186.9 reduce-scatter.9
  1727.1 218.9 reduce-scatter.21
  1948.4 221.9 reduce-scatter.19
  2172.7 220.2 reduce-scatter.17
where the time goes:
time: 2410 us; the launch traced here: 2400 us
  waiting for transfers between devices  1840 us (76%)
  blocking collectives  360 us (15%)
  matrix products  123 us (5%)
  local copies, waits for them, and re-layouts  31.3 us (1%)
  other arithmetic  26.5 us (1%)
    unnamed x19, waiting for transfers between devices  224 us
    reduce_scatter x1, waiting for transfers between devices, on_device(): lax.psum_scatter(grad_up.astype(jnp.bfloat16), 'dp', scatter_dimension=0,...  221 us
    reduce_scatter x1, waiting for transfers between devices, on_device(): lax.psum_scatter(grad_gate.astype(jnp.bfloat16), 'dp', scatter_dimension=...  220 us
    unnamed x2, blocking collectives  189 us
    reduce_scatter x1, waiting for transfers between devices, on_device(): lax.psum_scatter(grad_out.astype(jnp.bfloat16), 'dp', scatter_dimension=0...  188 us
    reduce_scatter x1, waiting for transfers between devices, on_device(): lax.psum_scatter(grad_query.astype(jnp.bfloat16), 'dp', scatter_dimension...  188 us
    psum x1, blocking collectives, on_device(): grad_gq, grad_gk = lax.psum((grad_gq, grad_gk), ('dp', 'head'))  171 us
    all_gather x1, waiting for transfers between devices, on_device(): lax.all_gather(w_up, 'dp', axis=0, tiled=True)  160 us
  transfers between devices with their start and end apart: 18, of which 15 were waited for; matrix products, arithmetic and copies ran while one was open for 5% of the time, Pallas kernels for 0%

commit v1 on v0

v1 whole, which is shorter than its diff:
```python
import functools

import jax
import jax.numpy as jnp
import numpy as np
from jax import lax
from jax.experimental import pallas as pl
from jax.experimental.pallas import tpu as pltpu
from jax.sharding import PartitionSpec as P

BF = jnp.bfloat16
F32 = jnp.float32
MESH = pl.DeviceIdType.MESH
EPS = 1e-05
THETA = 1000000.0
VMEM_BYTES = 60 << 20
ATT_SPLIT = 640


def nn(a, b):
    return lax.dot_general(a, b, (((1,), (0,)), ((), ())), preferred_element_type=F32)


def nt(a, b):
    return lax.dot_general(a, b, (((1,), (1,)), ((), ())), preferred_element_type=F32)


def tn(a, b):
    return lax.dot_general(a, b, (((0,), (0,)), ((), ())), preferred_element_type=F32)


class Place:
    def __init__(self):
        dp = lax.axis_index("dp")
        self.c = lax.axis_index("head")
        self.zl = lax.axis_index("tensor")
        self.zh = lax.div(dp, 16)
        self.y = lax.rem(lax.div(dp, 4), 4)
        self.x = lax.rem(dp, 4)
        self.z = self.zh * 2 + self.zl

    def at(self, zh=None, y=None, x=None, c=None, zl=None):
        zh = self.zh if zh is None else zh
        y = self.y if y is None else y
        x = self.x if x is None else x
        return (zh * 16 + y * 4 + x, self.c if c is None else c, self.zl if zl is None else zl)

    def step(self, axis, by):
        if axis == "x":
            return self.at(x=lax.rem(self.x + by + 4, 4))
        if axis == "y":
            return self.at(y=lax.rem(self.y + by + 4, 4))
        z = lax.rem(self.z + by + 4, 4)
        return self.at(zh=lax.div(z, 2), zl=lax.rem(z, 2))

    def core(self):
        return self.at(c=1 - self.c)

    def zl_pair(self):
        return self.at(zl=1 - self.zl)

    def zh_pair(self):
        return self.at(zh=1 - self.zh)

    def ring(self, axis):
        return {"x": self.x, "y": self.y, "z": self.z}[axis]


class Net:
    def __init__(self, send_sems, recv_sems):
        self.send_sems = send_sems
        self.recv_sems = recv_sems
        self.count = 0
        self.left = []

    def send(self, src, dst, device):
        k = self.count
        assert k < self.send_sems.shape[0]
        self.count += 1
        copy = pltpu.make_async_remote_copy(
            src_ref=src,
            dst_ref=dst,
            send_sem=self.send_sems.at[k],
            recv_sem=self.recv_sems.at[k],
            device_id=device,
            device_id_type=MESH,
        )
        copy.start()
        self.left.append(copy)
        return copy

    def wait_send(self, copy):
        copy.wait_send()
        self.left = [other for other in self.left if other is not copy]

    def drain(self):
        for copy in self.left:
            copy.wait_send()


def greet(devices):
    barrier = pltpu.get_barrier_semaphore()
    for device in devices:
        pl.semaphore_signal(barrier, inc=1, device_id=device, device_id_type=MESH)
    pl.semaphore_wait(barrier, len(devices))


def together(*pipelines):
    live = list(pipelines)
    while live:
        for pipe in list(live):
            try:
                next(pipe)
            except StopIteration:
                live.remove(pipe)
        yield


def interleave(*pipelines):
    for _ in together(*pipelines):
        pass


def local(pairs, sems):
    copies = [pltpu.make_async_copy(s, d, sems.at[i]) for i, (s, d) in enumerate(pairs)]
    for copy in copies:
        copy.start()
    for copy in copies:
        copy.wait()


def add_refs(dst, srcs, rows=32):
    lead, height = dst.shape[:-2], dst.shape[-2]
    rows = min(rows, height)
    per = height // rows
    count = int(np.prod(lead, dtype=np.int64)) * per

    def body(t, carry):
        r = lax.rem(t, per)
        rest = lax.div(t, per)
        index = []
        for size in reversed(lead):
            index.insert(0, lax.rem(rest, size))
            rest = lax.div(rest, size)
        at = tuple(index) + (pl.ds(r * rows, rows), slice(None))
        total = srcs[0][at].astype(F32)
        for src in srcs[1:]:
            total = total + src[at].astype(F32)
        dst[at] = total.astype(dst.dtype)
        return carry

    lax.fori_loop(0, count, body, 0)


def ring_gather(net, place, axis, view):
    i = place.ring(axis)
    before, after = lax.rem(i + 3, 4), lax.rem(i + 1, 4)
    up, down = place.step(axis, 1), place.step(axis, -1)
    u0 = net.send(view(i, 0), view(i, 0), up)
    d1 = net.send(view(i, 1), view(i, 1), down)
    u1 = net.send(view(i, 1), view(i, 1), up)
    d0 = net.send(view(i, 0), view(i, 0), down)
    yield
    u0.wait_recv()
    f0 = net.send(view(before, 0), view(before, 0), up)
    d1.wait_recv()
    f1 = net.send(view(after, 1), view(after, 1), down)
    yield
    for copy in (u1, d0, f0, f1):
        copy.wait_recv()


def ring_reduce(net, place, axis, view, far, near, out):
    i = place.ring(axis)
    before, after, across = lax.rem(i + 3, 4), lax.rem(i + 1, 4), lax.rem(i + 2, 4)
    up, down = place.step(axis, 1), place.step(axis, -1)
    f0 = net.send(view(across, 0), far.at[0], up)
    f1 = net.send(view(across, 1), far.at[1], down)
    u1 = net.send(view(after, 1), near.at[1], up)
    d0 = net.send(view(before, 0), near.at[2], down)
    yield
    f0.wait_recv()
    add_refs(far.at[0], [far.at[0], view(after, 0)])
    u0 = net.send(far.at[0], near.at[0], up)
    f1.wait_recv()
    add_refs(far.at[1], [far.at[1], view(before, 1)])
    d1 = net.send(far.at[1], near.at[3], down)
    yield
    u1.wait_recv()
    d0.wait_recv()
    u0.wait_recv()
    d1.wait_recv()
    add_refs(out(0), [view(i, 0), near.at[0], near.at[2]])
    add_refs(out(1), [view(i, 1), near.at[1], near.at[3]])


def halves(ref, part):
    return ref.at[..., pl.ds(part * 1024, 1024)]


def torus_gather(net, place, buf):
    x, z, c = place.x, place.z, place.c

    def first():
        yield from ring_gather(
            net, place, "x", lambda i, p: buf.at[z, i, c, pl.ds(0, 16), pl.ds(p * 1024, 1024)]
        )
        yield
        yield from ring_gather(
            net, place, "z", lambda i, p: buf.at[i, :, c, pl.ds(0, 16), pl.ds(p * 1024, 1024)]
        )

    def second():
        yield from ring_gather(
            net, place, "z", lambda i, p: buf.at[i, x, c, pl.ds(16, 16), pl.ds(p * 1024, 1024)]
        )
        yield
        yield from ring_gather(
            net, place, "x", lambda i, p: buf.at[:, i, c, pl.ds(16, 16), pl.ds(p * 1024, 1024)]
        )

    yield from together(first(), second())
    swap = net.send(buf.at[:, :, c], buf.at[:, :, c], place.core())
    yield
    swap.wait_recv()


TORUS_SCRATCH = [
    pltpu.VMEM((4, 4, 32, 2048), BF),
    pltpu.VMEM((2, 4, 16, 1024), BF),
    pltpu.VMEM((4, 4, 16, 1024), BF),
    pltpu.VMEM((2, 4, 16, 1024), BF),
    pltpu.VMEM((2, 16, 1024), BF),
    pltpu.VMEM((4, 16, 1024), BF),
    pltpu.VMEM((2, 4, 16, 1024), BF),
    pltpu.VMEM((4, 4, 16, 1024), BF),
    pltpu.VMEM((2, 4, 16, 1024), BF),
    pltpu.VMEM((2, 16, 1024), BF),
    pltpu.VMEM((4, 16, 1024), BF),
]


def torus_reduce(net, place, src, scratch, out):
    both, far_a, near_a, mid_a, far_a2, near_a2, far_b, near_b, mid_b, far_b2, near_b2 = scratch
    x, z, c = place.x, place.z, place.c
    swap = net.send(src.at[:, :, 1 - c], both, place.core())
    yield
    swap.wait_recv()
    add_refs(both, [both, src.at[:, :, c]])

    def first():
        yield from ring_reduce(
            net, place, "z",
            lambda i, p: both.at[i, :, pl.ds(0, 16), pl.ds(p * 1024, 1024)],
            far_a, near_a, lambda p: mid_a.at[p],
        )
        yield
        yield from ring_reduce(
            net, place, "x",
            lambda i, p: mid_a.at[p, i],
            far_a2, near_a2, lambda p: out.at[pl.ds(0, 16), pl.ds(p * 1024, 1024)],
        )

    def second():
        yield from ring_reduce(
            net, place, "x",
            lambda i, p: both.at[:, i, pl.ds(16, 16), pl.ds(p * 1024, 1024)],
            far_b, near_b, lambda p: mid_b.at[p],
        )
        yield
        yield from ring_reduce(
            net, place, "z",
            lambda i, p: mid_b.at[p, i],
            far_b2, near_b2, lambda p: out.at[pl.ds(16, 16), pl.ds(p * 1024, 1024)],
        )

    yield from together(first(), second())


def quad_gather(net, place, buf):
    c, zl = place.c, place.zl
    own = buf.at[pl.ds(c * 64 + zl * 32, 32)]
    one = net.send(own, own, place.zl_pair())
    yield
    one.wait_recv()
    half = buf.at[pl.ds(c * 64, 64)]
    two = net.send(half, half, place.core())
    yield
    two.wait_recv()


def quad_reduce(net, place, src, from_core, from_zl, tmp):
    c, zl = place.c, place.zl
    one = net.send(src.at[pl.ds((1 - c) * 64, 64)], from_core, place.core())
    yield
    one.wait_recv()
    theirs = src[pl.ds(c * 64 + (1 - zl) * 32, 32), :].astype(F32)
    tmp[...] = (theirs + from_core[pl.ds((1 - zl) * 32, 32), :].astype(F32)).astype(BF)
    two = net.send(tmp, from_zl, place.zl_pair())
    yield
    two.wait_recv()


def quad_total(place, src, from_core, from_zl):
    c, zl = place.c, place.zl
    mine = src[pl.ds(c * 64 + zl * 32, 32), :].astype(F32)
    mine = mine + from_core[pl.ds(zl * 32, 32), :].astype(F32)
    return mine + from_zl[...].astype(F32)


def sem_scratch(n):
    return [pltpu.SemaphoreType.DMA((n,)), pltpu.SemaphoreType.DMA((n,))]


def params(collective_id=None):
    if collective_id is None:
        return pltpu.CompilerParams(vmem_limit_bytes=VMEM_BYTES)
    return pltpu.CompilerParams(
        vmem_limit_bytes=VMEM_BYTES, collective_id=collective_id, has_side_effects=True
    )


ANY = pl.BlockSpec(memory_space=pl.ANY)
VM = pl.BlockSpec(memory_space=pltpu.VMEM)


def gather_kernel(
    wq, wk, wv, wo, wg, wu, wd, cot, gains,
    att, ffn, cots, all_gains,
    send_sems, recv_sems, sems,
):
    me = Place()
    zh, y, x, c, zl, z = me.zh, me.y, me.x, me.c, me.zl, me.z
    greet(
        [me.step("x", 1), me.step("x", 2), me.step("x", -1)]
        + [me.step("y", 1), me.step("y", 2), me.step("y", -1)]
        + [me.step("z", 1), me.step("z", 2), me.step("z", -1)]
        + [me.core()]
        + [me.at(zh=1 - zh, x=lax.rem(x + k, 4)) for k in (1, 2, 3)]
    )
    net = Net(send_sems, recv_sems)

    def piece(k):
        return pl.ds(pl.multiple_of(k * 512 + c * 256, 256), 256)

    own = att.at[zh, y, x]
    local(
        [
            (wq.at[:, pl.ds(pl.multiple_of(zl * 512, 512), 512)], own.at[:, pl.ds(0, 512)]),
            (wk.at[:, pl.ds(pl.multiple_of(zl * 128, 128), 128)], own.at[:, pl.ds(512, 128)]),
            (wv.at[:, pl.ds(pl.multiple_of(zl * 128, 128), 128)], own.at[:, pl.ds(640, 128)]),
            (wo.at[:, pl.ds(pl.multiple_of(zl * 512, 512), 512)], own.at[:, pl.ds(768, 512)]),
            (gains, all_gains.at[zh, y, x]),
            (cot.at[pl.ds(c * 64 + zl * 32, 32)], cots.at[z, x, c]),
            (wg.at[:, piece(zh * 4 + x)], ffn.at[0, zh, y, x]),
            (wu.at[:, piece(zh * 4 + x)], ffn.at[1, zh, y, x]),
            (wd.at[:, piece(zh * 4 + x)], ffn.at[2, zh, y, x]),
        ],
        sems,
    )

    def attention():
        swap = net.send(own, own, me.zh_pair())
        yield
        swap.wait_recv()
        a, b = pl.ds(0, ATT_SPLIT), pl.ds(ATT_SPLIT, 1280 - ATT_SPLIT)

        def first():
            yield from ring_gather(net, me, "x", lambda i, p: att.at[p, y, i, :, a])
            yield
            yield from ring_gather(net, me, "y", lambda i, p: att.at[p, i, :, :, a])

        def second():
            yield from ring_gather(net, me, "y", lambda i, p: att.at[p, i, x, :, b])
            yield
            yield from ring_gather(net, me, "x", lambda i, p: att.at[p, :, i, :, b])

        yield from together(first(), second())

    def feed_forward():
        arrivals = []
        for dz in (0, 1):
            for dx in range(4):
                if dz == 0 and dx == 0:
                    continue
                tx = lax.rem(x + dx, 4)
                tz = 1 - zh if dz else zh
                for m, w in enumerate((wg, wu, wd)):
                    arrivals.append(
                        net.send(
                            w.at[:, piece(tz * 4 + tx)],
                            ffn.at[m, zh, y, x],
                            me.at(zh=tz, x=tx),
                        )
                    )
        yield
        for copy in arrivals:
            copy.wait_recv()
        yield from ring_gather(net, me, "y", lambda i, p: ffn.at[:, p, i])

    def small():
        steps = [
            (all_gains.at[zh, y, x], me.zh_pair()),
            (all_gains.at[:, y, x], me.at(x=x + 1 - 2 * lax.rem(x, 2))),
            (all_gains.at[:, y, pl.ds(2 * lax.div(x, 2), 2)], me.step("x", 2)),
            (all_gains.at[:, y], me.at(y=y + 1 - 2 * lax.rem(y, 2))),
            (all_gains.at[:, pl.ds(2 * lax.div(y, 2), 2)], me.step("y", 2)),
        ]
        for block, device in steps:
            copy = net.send(block, block, device)
            yield
            copy.wait_recv()

    interleave(attention(), small(), feed_forward(), torus_gather(net, me, cots))
    net.drain()


def gather_all(wq, wk, wv, wo, wg, wu, wd, cot, gains):
    return pl.pallas_call(
        gather_kernel,
        out_shape=(
            jax.ShapeDtypeStruct((2, 4, 4, 64, 1280), BF),
            jax.ShapeDtypeStruct((3, 2, 4, 4, 64, 256), BF),
            jax.ShapeDtypeStruct((4, 4, 2, 32, 2048), BF),
            jax.ShapeDtypeStruct((2, 4, 4, 16, 128), BF),
        ),
        in_specs=[ANY] * 9,
        out_specs=[ANY] * 4,
        scratch_shapes=sem_scratch(96) + [pltpu.SemaphoreType.DMA((9,))],
        compiler_params=params(1),
        name="gather_all",
    )(wq, wk, wv, wo, wg, wu, wd, cot, gains)


def lanes(shape):
    return lax.broadcasted_iota(jnp.int32, shape, len(shape) - 1)


def partner(v):
    n = v.shape[-1]
    low = lax.rem(lanes(v.shape), 64) < 32
    return jnp.where(low, pltpu.roll(v, n - 32, 1), pltpu.roll(v, 32, 1))


def head_mean(v):
    n = v.shape[-1]
    r = lax.broadcasted_iota(jnp.int32, (n, n), 0)
    same = lax.div(r, 64) == lax.div(lanes((n, n)), 64)
    return lax.dot_general(
        v, jnp.where(same, 1.0 / 64.0, 0.0), (((1,), (0,)), ((), ())),
        precision=lax.Precision.HIGHEST, preferred_element_type=F32,
    )


def half_of(v, which):
    upper = lanes(v.shape) >= 64
    keep = upper if which else jnp.logical_not(upper)
    return jnp.where(keep, v, jnp.zeros_like(v))


def swap_halves(v):
    return pltpu.roll(v.astype(F32), 64, 1).astype(v.dtype)


def attention_forward_kernel(
    x_ref, gain_ref, w_ref, head_gain_ref, cos_ref, sin_ref,
    xn_ref, z_ref, qk_ref, v_ref, p_ref, o_ref, branch_ref,
):
    x = x_ref[...].astype(F32)
    r = lax.rsqrt(jnp.mean(x * x, axis=-1, keepdims=True) + EPS)
    xn = (x * r * gain_ref[...]).astype(BF)
    xn_ref[...] = xn
    raw = nn(xn, w_ref[:, 0:768])
    z = raw[:, 0:640]
    z_ref[...] = z
    v = raw[:, 640:768].astype(BF)
    v_ref[...] = v
    n = z * lax.rsqrt(head_mean(z * z) + EPS) * head_gain_ref[...]
    cos = jnp.concatenate([cos_ref[...]] * 5, axis=1)
    sin = jnp.concatenate([sin_ref[...]] * 5, axis=1)
    qk = (n * cos + partner(n) * sin).astype(BF)
    qk_ref[...] = qk
    k = qk[:, 512:640]
    k_at = {True: k, False: swap_halves(k)}
    v_at = {True: v, False: swap_halves(v)}
    rows = lax.broadcasted_iota(jnp.int32, (128, 128), 0)
    causal = rows >= lanes((128, 128))
    for block in range(4):
        out = None
        for side in range(2):
            h = 2 * block + side
            same = side == h // 4
            q = half_of(qk[:, block * 128:(block + 1) * 128], side)
            s = jnp.where(causal, nt(q, k_at[same]) * 0.125, -1e30)
            e = jnp.exp(s - jnp.max(s, axis=-1, keepdims=True))
            p = e / jnp.sum(e, axis=-1, keepdims=True)
            p_ref[h] = p
            part = nn(p.astype(BF), half_of(v_at[same], side))
            out = part if out is None else out + part
        o_ref[:, block * 128:(block + 1) * 128] = out.astype(BF)
    branch_ref[...] = nt(o_ref[...], w_ref[:, 768:1280]).astype(BF)


def attention_forward(x, gain, w, head_gain, cos, sin):
    return pl.pallas_call(
        attention_forward_kernel,
        out_shape=(
            jax.ShapeDtypeStruct((128, 2048), BF),
            jax.ShapeDtypeStruct((128, 640), F32),
            jax.ShapeDtypeStruct((128, 640), BF),
            jax.ShapeDtypeStruct((128, 128), BF),
            jax.ShapeDtypeStruct((8, 128, 128), F32),
            jax.ShapeDtypeStruct((128, 512), BF),
            jax.ShapeDtypeStruct((128, 2048), BF),
        ),
        in_specs=[VM] * 6,
        out_specs=[VM] * 7,
        compiler_params=params(),
        name="attention_forward",
    )(x, gain, w, head_gain, cos, sin)


def attention_backward_kernel(
    dh_ref, w_ref, head_gain_ref, cos_ref, sin_ref,
    xn_ref, z_ref, qk_ref, v_ref, p_ref, o_ref,
    grad_ref, dxn_ref, dgain_ref, d_ref,
):
    dh = dh_ref[...]
    grad_ref[:, 768:1280] = tn(dh, o_ref[...]).astype(BF)
    do = nn(dh, w_ref[:, 768:1280]).astype(BF)
    qk = qk_ref[...]
    v = v_ref[...]
    k = qk[:, 512:640]
    k_at = {True: k, False: swap_halves(k)}
    v_at = {True: v, False: swap_halves(v)}
    dk = {True: jnp.zeros((128, 128), F32), False: jnp.zeros((128, 128), F32)}
    dv = {True: jnp.zeros((128, 128), F32), False: jnp.zeros((128, 128), F32)}
    for block in range(4):
        dq = None
        for side in range(2):
            h = 2 * block + side
            same = side == h // 4
            p = p_ref[h]
            dob = half_of(do[:, block * 128:(block + 1) * 128], side)
            q = half_of(qk[:, block * 128:(block + 1) * 128], side)
            dp = nt(dob, v_at[same])
            dv[same] = dv[same] + tn(p.astype(BF), dob)
            ds = (p * (dp - jnp.sum(p * dp, axis=-1, keepdims=True))).astype(BF)
            part = nn(ds, half_of(k_at[same], side))
            dq = part if dq is None else dq + part
            dk[same] = dk[same] + tn(ds, q)
        d_ref[:, block * 128:(block + 1) * 128] = dq * 0.125
    d_ref[:, 512:640] = (dk[True] + pltpu.roll(dk[False], 64, 1)) * 0.125
    dvb = (dv[True] + pltpu.roll(dv[False], 64, 1)).astype(BF)
    cos = jnp.concatenate([cos_ref[...]] * 5, axis=1)
    sin = jnp.concatenate([sin_ref[...]] * 5, axis=1)
    dout = d_ref[...]
    dn = dout * cos - partner(dout) * sin
    z = z_ref[...]
    r = lax.rsqrt(head_mean(z * z) + EPS)
    zhat = z * r
    dgain = jnp.sum(dn * zhat, axis=0, keepdims=True)
    pairs = dgain[:, 0:128] + dgain[:, 128:256] + dgain[:, 256:384] + dgain[:, 384:512]
    both = jnp.concatenate([pairs, dgain[:, 512:640]], axis=0)
    both = both + pltpu.roll(both, 64, 1)
    q_row = half_of(both[0:1], 0) + half_of(both[1:2], 1)
    dgain_ref[...] = jnp.concatenate([q_row, jnp.zeros((7, 128), F32)], axis=0)
    dz = dn * head_gain_ref[...]
    dz = r * (dz - zhat * head_mean(dz * zhat))
    low = jnp.concatenate([dz.astype(BF), dvb], axis=1)
    grad_ref[:, 0:768] = tn(xn_ref[...], low).astype(BF)
    dxn_ref[...] = nt(low, w_ref[:, 0:768]).astype(BF)


def attention_backward(dh, w, head_gain, cos, sin, xn, z, qk, v, p, o):
    return pl.pallas_call(
        attention_backward_kernel,
        out_shape=(
            jax.ShapeDtypeStruct((2048, 1280), BF),
            jax.ShapeDtypeStruct((128, 2048), BF),
            jax.ShapeDtypeStruct((8, 128), F32),
        ),
        in_specs=[VM] * 11,
        out_specs=[VM] * 3,
        scratch_shapes=[pltpu.VMEM((128, 640), F32)],
        compiler_params=params(),
        name="attention_backward",
    )(dh, w, head_gain, cos, sin, xn, z, qk, v, p, o)


def hidden_kernel(
    branch, tokens, gain, xn, hidden, from_core, from_zl, tmp, send_sems, recv_sems
):
    me = Place()
    x, z, c, zl = me.x, me.z, me.c, me.zl
    greet(
        [me.step("x", 1), me.step("x", -1), me.step("z", 1), me.step("z", -1), me.core()]
    )
    net = Net(send_sems, recv_sems)
    interleave(quad_reduce(net, me, branch, from_core, from_zl, tmp))
    h = tokens[pl.ds(c * 64 + zl * 32, 32), :].astype(F32)
    h = h + quad_total(me, branch, from_core, from_zl)
    hidden[...] = h
    r = lax.rsqrt(jnp.mean(h * h, axis=-1, keepdims=True) + EPS)
    xn[z, x, c] = (h * r * gain[...]).astype(BF)
    interleave(torus_gather(net, me, xn))
    net.drain()


def hidden_state(branch, tokens, gain):
    return pl.pallas_call(
        hidden_kernel,
        out_shape=(
            jax.ShapeDtypeStruct((4, 4, 2, 32, 2048), BF),
            jax.ShapeDtypeStruct((32, 2048), F32),
        ),
        in_specs=[VM] * 3,
        out_specs=[VM] * 2,
        scratch_shapes=[
            pltpu.VMEM((64, 2048), BF),
            pltpu.VMEM((32, 2048), BF),
            pltpu.VMEM((32, 2048), BF),
        ]
        + sem_scratch(32),
        compiler_params=params(2),
        name="hidden_state",
    )(branch, tokens, gain)


def feed_forward_kernel(x_ref, dy_ref, w_ref, out_ref, dx_ref, grad_ref, acc):
    step = pl.program_id(0)
    x, dy = x_ref[...], dy_ref[...]
    wg, wu, wd = w_ref[0], w_ref[1], w_ref[2]
    g, u, da = nn(x, wg), nn(x, wu), nn(dy, wd)
    sigma = jax.nn.sigmoid(g)
    swish = g * sigma
    ab = (swish * u).astype(BF)
    dg = (da * u * sigma * (1.0 + g * (1.0 - sigma))).astype(BF)
    du = (da * swish).astype(BF)
    out_ref[...] = nt(ab, wd).astype(BF)
    dx_ref[...] = (nt(dg, wg) + nt(du, wu)).astype(BF)
    grads = [tn(x, dg), tn(x, du), tn(dy, ab)]

    @pl.when(step == 0)
    def _():
        for m in range(3):
            acc[m] = grads[m]

    @pl.when(step > 0)
    def _():
        for m in range(3):
            acc[m] += grads[m]

    @pl.when(step == pl.num_programs(0) - 1)
    def _():
        for m in range(3):
            grad_ref[m] = acc[m].astype(BF)


def feed_forward(x, dy, w):
    rows = 512
    block = pl.BlockSpec((rows, 2048), lambda t: (t, 0))
    whole = pl.BlockSpec((3, 2048, 256), lambda t: (0, 0, 0))
    return pl.pallas_call(
        feed_forward_kernel,
        grid=(1024 // rows,),
        out_shape=(
            jax.ShapeDtypeStruct((1024, 2048), BF),
            jax.ShapeDtypeStruct((1024, 2048), BF),
            jax.ShapeDtypeStruct((3, 2048, 256), BF),
        ),
        in_specs=[block, block, whole],
        out_specs=[block, block, whole],
        scratch_shapes=[pltpu.VMEM((3, 2048, 256), F32)],
        compiler_params=params(),
        name="feed_forward",
    )(x, dy, w)


def hidden_grad_kernel(
    part, hidden, cot, gain, dh, dhb, gain_grad, dxn, *rest
):
    scratch, (send_sems, recv_sems) = rest[:-2], rest[-2:]
    me = Place()
    c, zl = me.c, me.zl
    greet(
        [me.step("x", 1), me.step("x", -1), me.step("z", 1), me.step("z", -1), me.core()]
    )
    net = Net(send_sems, recv_sems)
    interleave(torus_reduce(net, me, part, scratch, dxn))
    rows = pl.ds(c * 64 + zl * 32, 32)
    h = hidden[...]
    r = lax.rsqrt(jnp.mean(h * h, axis=-1, keepdims=True) + EPS)
    hat = h * r
    d = dxn[...]
    gain_grad[...] = jnp.sum(d * hat, axis=0, keepdims=True)
    s = d * gain[...]
    total = cot[rows, :].astype(F32) + r * (s - hat * jnp.mean(s * hat, axis=-1, keepdims=True))
    dh[...] = total
    dhb[rows, :] = total.astype(BF)
    interleave(quad_gather(net, me, dhb))
    net.drain()


def hidden_grad(part, hidden, cot, gain):
    return pl.pallas_call(
        hidden_grad_kernel,
        out_shape=(
            jax.ShapeDtypeStruct((32, 2048), F32),
            jax.ShapeDtypeStruct((128, 2048), BF),
            jax.ShapeDtypeStruct((1, 2048), F32),
        ),
        in_specs=[VM] * 4,
        out_specs=[VM] * 3,
        scratch_shapes=[pltpu.VMEM((32, 2048), F32)] + TORUS_SCRATCH + sem_scratch(32),
        compiler_params=params(3),
        name="hidden_grad",
    )(part, hidden, cot, gain)


ATT_A, ATT_B = ATT_SPLIT, 1280 - ATT_SPLIT
FINAL_SCRATCH = [
    pltpu.VMEM((2, 4, 64, ATT_A), BF),
    pltpu.VMEM((4, 4, 64, ATT_A), BF),
    pltpu.VMEM((2, 4, 64, ATT_A), BF),
    pltpu.VMEM((2, 64, ATT_A), BF),
    pltpu.VMEM((4, 64, ATT_A), BF),
    pltpu.VMEM((2, 4, 64, ATT_B), BF),
    pltpu.VMEM((4, 4, 64, ATT_B), BF),
    pltpu.VMEM((2, 4, 64, ATT_B), BF),
    pltpu.VMEM((2, 64, ATT_B), BF),
    pltpu.VMEM((4, 64, ATT_B), BF),
    pltpu.VMEM((2, 64, 1280), BF),
    pltpu.VMEM((64, 1280), BF),
    pltpu.VMEM((2, 3, 4, 64, 256), BF),
    pltpu.VMEM((4, 3, 4, 64, 256), BF),
    pltpu.VMEM((2, 3, 4, 64, 256), BF),
    pltpu.VMEM((64, 2048), BF),
    pltpu.VMEM((32, 2048), BF),
    pltpu.VMEM((32, 2048), BF),
    pltpu.VMEM((7, 8, 640), F32),
    pltpu.VMEM((32, 2048), F32),
]


def final_kernel(
    out_part, grads, ffn_grads, dxn_part, hidden, dh, tokens, gain, ffn_gain_grad, head_gain_grad,
    out, dx, att_grads, gate_grads, gain_sums,
    *rest,
):
    (
        far_a, near_a, mid_a, far_a2, near_a2,
        far_b, near_b, mid_b, far_b2, near_b2,
        both_z, other_z,
        far_f, near_f, mid_f,
        from_core, from_zl, tmp,
        small, total,
    ) = rest[: len(FINAL_SCRATCH)]
    torus = rest[len(FINAL_SCRATCH): len(FINAL_SCRATCH) + len(TORUS_SCRATCH)]
    send_sems, recv_sems, sems = rest[-3:]
    me = Place()
    zh, y, x, c, zl = me.zh, me.y, me.x, me.c, me.zl
    greet(
        [me.step("x", 1), me.step("x", 2), me.step("x", -1)]
        + [me.step("y", 1), me.step("y", 2), me.step("y", -1)]
        + [me.step("z", 1), me.step("z", 2), me.step("z", -1)]
        + [me.core()]
        + [me.at(zh=1 - zh, x=lax.rem(x + k, 4)) for k in (1, 2, 3)]
    )
    net = Net(send_sems, recv_sems)
    rows = pl.ds(c * 64 + zl * 32, 32)

    def tokens_and_gains():
        yield from quad_reduce(net, me, dxn_part, from_core, from_zl, tmp)
        d = quad_total(me, dxn_part, from_core, from_zl)
        t = tokens[rows, :].astype(F32)
        r = lax.rsqrt(jnp.mean(t * t, axis=-1, keepdims=True) + EPS)
        hat = t * r
        s = d * gain[...]
        grad = dh[...] + r * (s - hat * jnp.mean(s * hat, axis=-1, keepdims=True))
        dx[rows, :] = grad.astype(BF)
        gain_grad = jnp.sum(d * hat, axis=0, keepdims=True)
        gain_sums[...] = jnp.zeros((8, 640), F32)
        for k in range(8):
            gain_sums[k:k + 1, 0:256] = gain_grad[:, k * 256:(k + 1) * 256]
            gain_sums[k:k + 1, 256:512] = ffn_gain_grad[:, k * 256:(k + 1) * 256]
        gain_sums[:, 512:640] = head_gain_grad[...]
        spread = quad_gather(net, me, dx)
        next(spread)
        devices = [
            me.core(),
            me.zl_pair(),
            me.zh_pair(),
            me.at(x=x + 1 - 2 * lax.rem(x, 2)),
            me.step("x", 2),
            me.at(y=y + 1 - 2 * lax.rem(y, 2)),
            me.step("y", 2),
        ]
        for k, device in enumerate(devices):
            copy = net.send(gain_sums, small.at[k], device)
            yield
            copy.wait_recv()
            net.wait_send(copy)
            gain_sums[...] = gain_sums[...] + small[k]
            next(spread, None)

    def output():
        yield from torus_reduce(net, me, out_part, torus, total)
        out[rows, :] = (hidden[...] + total[...]).astype(BF)
        yield from quad_gather(net, me, out)

    def attention():
        a, b = pl.ds(0, ATT_A), pl.ds(ATT_A, ATT_B)

        def first():
            yield from ring_reduce(
                net, me, "y", lambda i, p: grads.at[p, i, :, :, a],
                far_a, near_a, lambda p: mid_a.at[p],
            )
            yield
            yield from ring_reduce(
                net, me, "x", lambda i, p: mid_a.at[p, i],
                far_a2, near_a2, lambda p: both_z.at[p, :, a],
            )

        def second():
            yield from ring_reduce(
                net, me, "x", lambda i, p: grads.at[p, :, i, :, b],
                far_b, near_b, lambda p: mid_b.at[p],
            )
            yield
            yield from ring_reduce(
                net, me, "y", lambda i, p: mid_b.at[p, i],
                far_b2, near_b2, lambda p: both_z.at[p, :, b],
            )

        yield from together(first(), second())
        swap = net.send(both_z.at[1 - zh], other_z, me.zh_pair())
        yield
        swap.wait_recv()
        own = att_grads.at[zl]
        add_refs(own, [both_z.at[zh], other_z])
        swap = net.send(own, own, me.zl_pair())
        yield
        swap.wait_recv()

    def feed_forward_grads():
        yield from ring_reduce(
            net, me, "y", lambda i, p: ffn_grads.at[:, p, i],
            far_f, near_f, lambda p: mid_f.at[p],
        )
        mine = zh * 4 + x
        arrivals = []
        for dz in (0, 1):
            for dxx in range(4):
                if dz == 0 and dxx == 0:
                    continue
                tx = lax.rem(x + dxx, 4)
                tz = 1 - zh if dz else zh
                arrivals.append(
                    net.send(
                        mid_f.at[tz, :, tx], gate_grads.at[:, mine, c], me.at(zh=tz, x=tx)
                    )
                )
        keep = pltpu.make_async_copy(mid_f.at[zh, :, x], gate_grads.at[:, mine, c], sems.at[0])
        keep.start()
        yield
        keep.wait()
        for copy in arrivals:
            copy.wait_recv()
        swap = net.send(gate_grads.at[:, :, c], gate_grads.at[:, :, c], me.core())
        yield
        swap.wait_recv()

    interleave(attention(), feed_forward_grads(), output(), tokens_and_gains())
    net.drain()


def final_sums(*args):
    return pl.pallas_call(
        final_kernel,
        out_shape=(
            jax.ShapeDtypeStruct((128, 2048), BF),
            jax.ShapeDtypeStruct((128, 2048), BF),
            jax.ShapeDtypeStruct((2, 64, 1280), BF),
            jax.ShapeDtypeStruct((3, 8, 2, 64, 256), BF),
            jax.ShapeDtypeStruct((8, 640), F32),
        ),
        in_specs=[VM] * 10,
        out_specs=[VM] * 5,
        scratch_shapes=FINAL_SCRATCH
        + TORUS_SCRATCH
        + sem_scratch(96)
        + [pltpu.SemaphoreType.DMA((1,))],
        compiler_params=params(4),
        name="final_sums",
    )(*args)


def rotary_tables():
    position = np.arange(128, dtype=np.float64)[:, None]
    lane = np.arange(128)
    angle = position * THETA ** (-2.0 * (lane % 32) / 64.0)[None, :]
    sign = np.where(lane % 64 < 32, -1.0, 1.0)
    return np.cos(angle).astype(np.float32), (np.sin(angle) * sign).astype(np.float32)


def on_device(
    tokens, gain_attn, w_query, w_key, w_value, gain_query, gain_key, w_out, gain_ffn,
    w_gate, w_up, w_down, cotangent,
):
    cos, sin = (jnp.asarray(t) for t in rotary_tables())
    gains = jnp.zeros((16, 128), BF)
    gains = gains.at[0, 0:64].set(gain_attn).at[0, 64:128].set(gain_ffn)
    att, ffn, cots, all_gains = gather_all(
        w_query, w_key, w_value, w_out, w_gate, w_up, w_down, cotangent, gains
    )
    gain_rows = all_gains[:, :, :, 0, :].reshape(32, 128).astype(F32)
    attn_gain = gain_rows[:, 0:64].reshape(1, 2048)
    ffn_gain = gain_rows[:, 64:128].reshape(1, 2048)
    head_gain = jnp.concatenate([jnp.tile(gain_query, 8), jnp.tile(gain_key, 2)])
    head_gain = head_gain.astype(F32).reshape(1, 640)
    att = att.reshape(2048, 1280)
    xn, z, qk, v, p, o, branch = attention_forward(tokens, attn_gain, att, head_gain, cos, sin)
    xn2, hidden = hidden_state(branch, tokens, ffn_gain)
    out_part, dxn2_part, ffn_grads = feed_forward(
        xn2.reshape(1024, 2048), cots.reshape(1024, 2048), ffn.reshape(3, 2048, 256)
    )
    dh, dhb, ffn_gain_grad = hidden_grad(
        dxn2_part.reshape(4, 4, 2, 32, 2048), hidden, cotangent, ffn_gain
    )
    grads, dxn_part, head_gain_grad = attention_backward(
        dhb, att, head_gain, cos, sin, xn, z, qk, v, p, o
    )
    out, dx, att_grads, gate_grads, gain_sums = final_sums(
        out_part.reshape(4, 4, 2, 32, 2048),
        grads.reshape(2, 4, 4, 64, 1280),
        ffn_grads.reshape(3, 2, 4, 4, 64, 256),
        dxn_part, hidden, dh, tokens, attn_gain, ffn_gain_grad, head_gain_grad,
    )
    dp = lax.axis_index("dp")

    def side_by_side(lo, hi):
        return jnp.concatenate([att_grads[0, :, lo:hi], att_grads[1, :, lo:hi]], axis=1).astype(F32)

    wide = gate_grads.transpose(0, 3, 1, 2, 4).reshape(3, 64, 4096)
    gq = gain_sums[0, 512:576]
    gk = gain_sums[0, 576:640]
    att_gain_grad = lax.dynamic_slice(gain_sums[:, 0:256].reshape(2048), (dp * 64,), (64,))
    ffn_gain_grad = lax.dynamic_slice(gain_sums[:, 256:512].reshape(2048), (dp * 64,), (64,))
    return (
        out,
        dx.astype(F32),
        att_gain_grad,
        side_by_side(0, 512),
        side_by_side(512, 640),
        side_by_side(640, 768),
        gq,
        gk,
        side_by_side(768, 1280),
        ffn_gain_grad,
        wide[0].astype(F32),
        wide[1].astype(F32),
        wide[2].astype(F32),
    )


def solution(mesh):
    return jax.shard_map(
        on_device,
        mesh=mesh,
        in_specs=(
            P("dp", None), P("dp"), P("dp", "head"), P("dp", "head"), P("dp", "head"),
            P(), P(), P("dp", "head"), P("dp"),
            P("dp", "tensor"), P("dp", "tensor"), P("dp", "tensor"), P("dp", None),
        ),
        out_specs=(
            P("dp", None), P("dp", None), P("dp"),
            P("dp", "head"), P("dp", "head"), P("dp", "head"),
            P(), P(), P("dp", "head"), P("dp"),
            P("dp", "tensor"), P("dp", "tensor"), P("dp", "tensor"),
        ),
        check_vma=False,
    )
```

time: 2410 us -> 330 us (0.14)
  waiting for transfers between devices: 1840 us -> 0 us
  blocking collectives: 360 us -> 0 us
  Pallas kernels: 0 us -> 303 us
  matrix products: 123 us -> 0 us
    reduce_scatter x6 -> x0, waiting for transfers between devices: 888 us -> none  [the longest x1 221 us: on_device(): lax.psum_scatter(grad_up.astype(jnp.bfloat16), 'dp', scatter_dimension=0,...]
    all_gather x7 -> x0, waiting for transfers between devices: 643 us -> none  [the longest x1 160 us: on_device(): lax.all_gather(w_up, 'dp', axis=0, tiled=True)]
    pallas_call x0 -> x7, Pallas kernels: none -> 303 us  [the longest x1 101 us: gather_all(): pl.pallas_call(gather_kernel, out_shape=(jax.ShapeDtypeStruct((2, 4, 4, 6...]
    unnamed x19 -> x0, waiting for transfers between devices: 224 us -> none
    unnamed x2 -> x0, blocking collectives: 189 us -> none
    psum x1 -> x0, blocking collectives: 171 us -> none  [on_device(): grad_gq, grad_gk = lax.psum((grad_gq, grad_gk), ('dp', 'head'))]
    dot_general x27 -> x0, matrix products: 123 us -> none  [the longest x7 46.4 us: over_cols(): lax.dot_general(left, right, (((1,), (1,)), ((), ())), preferred_element_...]
    psum x4 -> x0, waiting for transfers between devices: 88.3 us -> none  [the longest x1 37 us: on_device(): lax.psum(over_cols(active, wd).astype(jnp.bfloat16), 'tensor')]
  transfers between devices with their start and end apart: 18 -> 0, of which waited for: 15 -> 0; matrix products, arithmetic and copies ran while one was open for 5% -> 0% of each run, Pallas kernels for 0% -> 0%
where the time goes in v1:
time: 330 us
  Pallas kernels  303 us (92%)
  local copies, waits for them, and re-layouts  16.8 us (5%)
  other arithmetic  9.68 us (3%)
    pallas_call x1, Pallas kernels, gather_all(): pl.pallas_call(gather_kernel, out_shape=(jax.ShapeDtypeStruct((2, 4, 4, 6...  101 us
    pallas_call x1, Pallas kernels, final_sums(): pl.pallas_call(final_kernel, out_shape=(jax.ShapeDtypeStruct((128, 2048),...  98.2 us
    pallas_call x1, Pallas kernels, hidden_state(): pl.pallas_call(hidden_kernel, out_shape=(jax.ShapeDtypeStruct((4, 4, 2, 3...  34.6 us
    pallas_call x1, Pallas kernels, hidden_grad(): pl.pallas_call(hidden_grad_kernel, out_shape=(jax.ShapeDtypeStruct((32, 2...  33.3 us
    pallas_call x1, Pallas kernels, feed_forward(): pl.pallas_call(feed_forward_kernel, grid=(1024 // rows,), out_shape=(jax....  17.8 us
    pallas_call x1, Pallas kernels, attention_backward(): pl.pallas_call(attention_backward_kernel, out_shape=(jax.ShapeDtypeStruct...  10.7 us
    pallas_call x1, Pallas kernels, attention_forward(): pl.pallas_call(attention_forward_kernel, out_shape=(jax.ShapeDtypeStruct(...  7.47 us

profile of v1, /device:TPU:0, one launch (start us, length us, event | category | flops | bytes accessed | tf_op | source)
XLA Modules:
  0.0 329.8 jit_solution(8110429528838791541)
XLA Ops:
  0.7 0.6 fusion.1
  1.2 1.3 and_reduce_fusion
  2.5 2.7 broadcast_select_fusion
  5.2 0.7 scatter.6
  5.9 1.6 scatter.9.gains
  7.5 0.6 copy-done.3
  8.1 100.5 %gather_all.1 = (bf16[2,4,4,64,1280]{4,3,2,1,0:T(8,128)(2,1)}, bf16[3,2,4,4,64,256]{5,4,3,2,1,0:T(8,128)(2,1)}, bf16[4,4,2,32,2048]{4,3,2,1,0:T(8,128)(2,1)}, bf16[2,4,4,16,128]{4,3,2,1,0:T(8,128)(2,1)}) custom-call(bf16[64,1024]{1,0:T(8,128)(2,1)} %wq.1, bf16[64,256]{1,0:T(8,128)(2,1)} %wk.1, bf16[64,256]{1,0:T(8,128)(2,1)} %wv.1, bf16[64,1024]{1,0:T(8,128)(2,1)} %wo.1, ...), custom_call_target="tpu_custom_call" | custom-call | tf_op jit(solution)/shard_map/gather_all/pallas_call | solution.py:419
  108.6 0.9 slice_convert_fusion.3
  109.5 0.7 reshape.178.gain_ref.gain
  110.2 0.7 tile.4
  110.9 0.7 tile.5
  111.7 0.6 maximum_convert_fusion.4.head_gain_ref
  112.3 7.5 %attention_forward.1 = (bf16[128,2048]{1,0:T(8,128)(2,1)}, f32[128,640]{1,0:T(8,128)}, bf16[128,640]{1,0:T(8,128)(2,1)}, bf16[128,128]{1,0:T(8,128)(2,1)}, f32[8...) custom-call(bf16[128,2048]{1,0:T(8,128)(2,1)} %tokens.3, ...), custom_call_target="tpu_custom_call" | custom-call | tf_op jit(solution)/shard_map/attention_forward/pallas_call | solution.py:505
  119.8 0.7 reshape.180.gain
  120.4 34.6 %hidden_state.1 = (bf16[4,4,2,32,2048]{4,3,2,1,0:T(8,128)(2,1)}, f32[32,2048]{1,0:T(8,128)}) custom-call(bf16[128,2048]{1,0:T(8,128)(2,1)} %get-tuple-element.66.branch, bf16[128,2048]{1,0:T(8,128)(2,1)} %tokens.3, f32[1,2048]{1,0:T(1,128)} %reshape.180.gain), custom_call_target="tpu_custom_call" | custom-call | tf_op jit(solution)/shard_map/hidden_state/pallas_call | solution.py:611
  155.1 17.8 %feed_forward.1 = (bf16[1024,2048]{1,0:T(8,128)(2,1)}, bf16[1024,2048]{1,0:T(8,128)(2,1)}, bf16[3,2048,256]{2,1,0:T(8,128)(2,1)}) custom-call(bf16[1024,2048]{1,0:T(8,128)(2,1)} %bitcast.47, bf16[1024,2048]{1,0:T(8,128)(2,1)} %bitcast.46, bf16[3,2048,256]{2,1,0:T(8,128)(2,1)} %bitcast.48), custom_call_target="tpu_custom_call" | custom-call | tf_op jit(solution)/shard_map/feed_forward/pallas_call | solution.py:664
  172.9 33.3 %hidden_grad.1 = (f32[32,2048]{1,0:T(8,128)}, bf16[128,2048]{1,0:T(8,128)(2,1)}, f32[1,2048]{1,0:T(1,128)}) custom-call(bf16[4,4,2,32,2048]{4,3,2,1,0:T(8,128)(2,1)} %bitcast.45, f32[32,2048]{1,0:T(8,128)} %get-tuple-element.72.hidden, bf16[128,2048]{1,0:T(8,128)(2,1)} %cot.3, f32[1,2048]{1,0:T(1,128)} %reshape.180.gain), custom_call_target="tpu_custom_call" | custom-call | tf_op jit(solution)/shard_map/hidden_grad/pallas_call | solution.py:706
  206.2 10.7 %attention_backward.1 = (bf16[2048,1280]{1,0:T(8,128)(2,1)}, bf16[128,2048]{1,0:T(8,128)(2,1)}, f32[8,128]{1,0:T(8,128)}) custom-call(bf16[128,2048]{1,0:T(8,128)(2,1)} %get-tuple-element.73.dh_ref, bf16[2048,1280]{1,0:T(8,128)(2,1)} %bitcast.42, f32[1,640]{1,0:T(1,128)} %maximum_convert_fusion.4.head_gain_ref, f32[128,128]{1,0:T(8,128)} %constant.65.clone.cos_ref, ...), custom_call_target="tpu_custom_call" | custom-call | tf_op jit(solution)/shard_map/attention_backward/pallas_call | solution.py:576
  216.8 98.2 %final_sums.1 = (bf16[128,2048]{1,0:T(8,128)(2,1)}, bf16[128,2048]{1,0:T(8,128)(2,1)}, bf16[2,64,1280]{2,1,0:T(8,128)(2,1)}, bf16[3,8,2,64,256]{4,3,2,1,0:T(8,128)(2,1)}, f32[8,640]{1,0:T(8,128)}) custom-call(bf16[4,4,2,32,2048]{4,3,2,1,0:T(8,128)(2,1)} %bitcast.44, bf16[2,4,4,64,1280]{4,3,2,1,0:T(8,128)(2,1)} %bitcast.43, ...), custom_call_target="tpu_custom_call" | custom-call | tf_op jit(solution)/shard_map/final_sums/pallas_call | solution.py:880
  315.0 1.7 slice_convert_fusion
  316.7 0.8 copy.28
  317.5 1.8 reshape.191
  319.3 0.8 copy.29
  320.1 1.8 reshape.192
  321.9 0.8 copy.30
  322.8 1.8 reshape.193
  324.6 0.7 maximum_convert_fusion.2
  325.3 0.8 maximum_convert_fusion
  326.1 1.1 convert_element_type.52
  327.2 0.6 dynamic_slice.6
  327.8 0.6 dynamic_slice.7
  329.0 0.8 copy.35
  (19 shorter events, 0.9 us)
Async XLA Ops:
  7.5 0.6 copy-start.3
  319.3 5.3 %copy-start.2 = (bf16[2,64,1280]{2,1,0:T(8,128)(2,1)S(1)}, bf16[2,64,1280]{2,1,0:T(8,128)(2,1)}, u32[]{:S(2)}) copy-start(bf16[2,64,1280]{2,1,0:T(8,128)(2,1)} %get-tuple-element.89) | copy-start | bytes 983044
  320.1 6.0 %copy-start = (bf16[128,2048]{1,0:T(8,128)(2,1)S(1)}, bf16[128,2048]{1,0:T(8,128)(2,1)}, u32[]{:S(2)}) copy-start(bf16[128,2048]{1,0:T(8,128)(2,1)} %get-tuple-element.87) | copy-start | bytes 1572868
  321.9 5.2 %copy-start.4 = (f32[8,640]{1,0:T(8,128)S(1)}, f32[8,640]{1,0:T(8,128)}, u32[]{:S(2)}) copy-start(f32[8,640]{1,0:T(8,128)} %get-tuple-element.88) | copy-start | bytes 61444
  321.9 7.0 %copy-start.1 = (bf16[128,2048]{1,0:T(8,128)(2,1)S(1)}, bf16[128,2048]{1,0:T(8,128)(2,1)}, u32[]{:S(2)}) copy-start(bf16[128,2048]{1,0:T(8,128)(2,1)} %get-tuple-element.127) | copy-start | bytes 1572868

commit v2 on v0

v2 whole, which is shorter than its diff:
```python
import types

import jax
import jax.numpy as jnp
import numpy as np
from jax import lax
from jax.experimental import pallas as pl
from jax.experimental.pallas import tpu as pltpu
from jax.sharding import PartitionSpec as P

BF = jnp.bfloat16
F32 = jnp.float32
MESH = pl.DeviceIdType.MESH
EPS = 1e-05
THETA = 1000000.0
VMEM_BYTES = 62 << 20
ATT_GATHER_SPLIT = 768
ATT_SLICES = ((0, 384, "yx"), (384, 384, "xy"), (768, 256, "yx"), (1024, 256, "xy"))


def nn(a, b):
    return lax.dot_general(a, b, (((1,), (0,)), ((), ())), preferred_element_type=F32)


def nt(a, b):
    return lax.dot_general(a, b, (((1,), (1,)), ((), ())), preferred_element_type=F32)


def tn(a, b):
    return lax.dot_general(a, b, (((0,), (0,)), ((), ())), preferred_element_type=F32)


class Place:
    def __init__(self):
        dp = lax.axis_index("dp")
        self.c = lax.axis_index("head")
        self.zl = lax.axis_index("tensor")
        self.zh = lax.div(dp, 16)
        self.y = lax.rem(lax.div(dp, 4), 4)
        self.x = lax.rem(dp, 4)
        self.z = self.zh * 2 + self.zl

    def at(self, zh=None, y=None, x=None, c=None, zl=None):
        zh = self.zh if zh is None else zh
        y = self.y if y is None else y
        x = self.x if x is None else x
        return (zh * 16 + y * 4 + x, self.c if c is None else c, self.zl if zl is None else zl)

    def step(self, axis, by):
        if axis == "x":
            return self.at(x=lax.rem(self.x + by + 4, 4))
        if axis == "y":
            return self.at(y=lax.rem(self.y + by + 4, 4))
        z = lax.rem(self.z + by + 4, 4)
        return self.at(zh=lax.div(z, 2), zl=lax.rem(z, 2))

    def core(self):
        return self.at(c=1 - self.c)

    def zl_pair(self):
        return self.at(zl=1 - self.zl)

    def zh_pair(self):
        return self.at(zh=1 - self.zh)

    def ring(self, axis):
        return {"x": self.x, "y": self.y, "z": self.z}[axis]


class Net:
    def __init__(self, send_sems, recv_sems):
        self.send_sems = send_sems
        self.recv_sems = recv_sems
        self.count = 0
        self.left = []

    def send(self, src, dst, device):
        k = self.count
        assert k < self.send_sems.shape[0]
        self.count += 1
        copy = pltpu.make_async_remote_copy(
            src_ref=src,
            dst_ref=dst,
            send_sem=self.send_sems.at[k],
            recv_sem=self.recv_sems.at[k],
            device_id=device,
            device_id_type=MESH,
        )
        copy.start()
        self.left.append(copy)
        return copy

    def wait_send(self, copy):
        copy.wait_send()
        self.left = [other for other in self.left if other is not copy]

    def drain(self):
        for copy in self.left:
            copy.wait_send()


class Tagged:
    def __init__(self, net):
        self.net = net
        self.copies = []

    def send(self, src, dst, device):
        self.copies.append(self.net.send(src, dst, device))
        return self.copies[-1]

    def drain(self):
        for copy in self.copies:
            self.net.wait_send(copy)


def greet(devices):
    barrier = pltpu.get_barrier_semaphore()
    for device in devices:
        pl.semaphore_signal(barrier, inc=1, device_id=device, device_id_type=MESH)
    pl.semaphore_wait(barrier, len(devices))


def together(*pipelines):
    live = list(pipelines)
    while live:
        for pipe in list(live):
            try:
                next(pipe)
            except StopIteration:
                live.remove(pipe)
        yield


def step(*pipelines):
    for pipe in pipelines:
        next(pipe, None)


def finish(*pipelines):
    for _ in together(*pipelines):
        pass


def local(pairs, sems):
    copies = [pltpu.make_async_copy(s, d, sems.at[i]) for i, (s, d) in enumerate(pairs)]
    for copy in copies:
        copy.start()
    for copy in copies:
        copy.wait()


def add_refs(dst, srcs, rows=32):
    lead, height = dst.shape[:-2], dst.shape[-2]
    rows = min(rows, height)
    per = height // rows
    count = int(np.prod(lead, dtype=np.int64)) * per

    def body(t, carry):
        r = lax.rem(t, per)
        rest = lax.div(t, per)
        index = []
        for size in reversed(lead):
            index.insert(0, lax.rem(rest, size))
            rest = lax.div(rest, size)
        at = tuple(index) + (pl.ds(r * rows, rows), slice(None))
        total = srcs[0][at].astype(F32)
        for src in srcs[1:]:
            total = total + src[at].astype(F32)
        dst[at] = total.astype(dst.dtype)
        return carry

    lax.fori_loop(0, count, body, 0)


def ring_gather(net, place, axis, view, also=None):
    i = place.ring(axis)
    before, after, across = lax.rem(i + 3, 4), lax.rem(i + 1, 4), lax.rem(i + 2, 4)
    up, down = place.step(axis, 1), place.step(axis, -1)
    u0 = net.send(view(i, 0), view(i, 0), up)
    d1 = net.send(view(i, 1), view(i, 1), down)
    u1 = net.send(view(i, 1), view(i, 1), up)
    d0 = net.send(view(i, 0), view(i, 0), down)
    yield
    u0.wait_recv()
    f0 = net.send(view(before, 0), view(before, 0), up)
    d1.wait_recv()
    f1 = net.send(view(after, 1), view(after, 1), down)
    if also is not None:
        also(view(before, 0))
        also(view(after, 1))
    yield
    u1.wait_recv()
    d0.wait_recv()
    if also is not None:
        also(view(before, 1))
        also(view(after, 0))
    f0.wait_recv()
    f1.wait_recv()
    if also is not None:
        also(view(across, 0))
        also(view(across, 1))


def cross_gather(net, place, one, two, view, late=None, also=None):
    ring = [lax.rem(place.ring(one) + k, 4) for k in range(4)]
    other = [lax.rem(place.ring(two) + k, 4) for k in range(4)]
    up = {one: place.step(one, 1), two: place.step(two, 1)}
    down = {one: place.step(one, -1), two: place.step(two, -1)}
    corners = []

    def spread(block, axis):
        return net.send(block, block, up[axis]), net.send(block, block, down[axis])

    def arrived(block):
        if also is not None:
            also(block)
        return block

    def along(axis, part, k, half=None):
        if axis == one:
            return view(part, ring[k], other[0], half)
        return view(part, ring[0], other[k], half)

    def turn(axis, part, k):
        across = two if axis == one else one
        half = 1 if axis == one else 0
        copies = spread(along(axis, part, k, half), across)
        corners.append((axis, part, k, half, across, copies))

    def own(part):
        block = view(part, ring[0], other[0], None)
        return {axis: spread(block, axis) for axis in (one, two)}

    crosses = [own(0)]
    if late is None:
        crosses.append(own(1))
    yield
    if late is not None:
        late.wait_recv()
        crosses.append(own(1))
        yield
    far = []
    for part in (0, 1):
        order = ((0, 3), (1, 1)) if part == 0 else ((1, 1), (0, 3))
        for n, (which, k) in enumerate(order):
            for axis in (one, two):
                crosses[part][axis][which].wait_recv()
                block = arrived(along(axis, part, k))
                if n == 0:
                    on = (up, down)[part][axis]
                    far.append((axis, part, net.send(block, block, on)))
                turn(axis, part, k)
        yield
    for axis, part, copy in far:
        copy.wait_recv()
        arrived(along(axis, part, 2))
        turn(axis, part, 2)
    yield
    last = []
    for n, (axis, part, k, half, across, copies) in enumerate(corners):
        for which, step_ in ((0, 3), (1, 1)):
            copies[which].wait_recv()
            if axis == one:
                block = view(part, ring[k], other[step_], half)
                final = view(part, ring[k], other[2], half)
            else:
                block = view(part, ring[step_], other[k], half)
                final = view(part, ring[2], other[k], half)
            arrived(block)
            if which == part:
                on = (up, down)[part][across]
                last.append((net.send(block, block, on), final))
        if n % 4 == 3:
            yield
    for copy, final in last:
        copy.wait_recv()
        arrived(final)


def ring_reduce(net, place, axis, view, far, near, out):
    i = place.ring(axis)
    before, after, across = lax.rem(i + 3, 4), lax.rem(i + 1, 4), lax.rem(i + 2, 4)
    up, down = place.step(axis, 1), place.step(axis, -1)
    f0 = net.send(view(across, 0), far.at[0], up)
    f1 = net.send(view(across, 1), far.at[1], down)
    u1 = net.send(view(after, 1), near.at[1], up)
    d0 = net.send(view(before, 0), near.at[2], down)
    yield
    f0.wait_recv()
    add_refs(far.at[0], [far.at[0], view(after, 0)])
    u0 = net.send(far.at[0], near.at[0], up)
    f1.wait_recv()
    add_refs(far.at[1], [far.at[1], view(before, 1)])
    d1 = net.send(far.at[1], near.at[3], down)
    yield
    u1.wait_recv()
    d0.wait_recv()
    u0.wait_recv()
    d1.wait_recv()
    add_refs(out(0), [view(i, 0), near.at[0], near.at[2]])
    add_refs(out(1), [view(i, 1), near.at[1], near.at[3]])


def torus_gather(net, place, buf):
    c = place.c
    other = place.core()
    swaps = []

    def also(block):
        swaps.append(net.send(block, block, other))

    def view(part, i, j, half):
        rows = pl.ds(0, 32) if half is None else pl.ds(half * 16, 16)
        return buf.at[i, j, c, rows, pl.ds(part * 1024, 1024)]

    also(buf.at[place.z, place.x, c])
    yield from cross_gather(net, place, "z", "x", view, also=also)
    yield
    for swap in swaps:
        swap.wait_recv()


def torus_buffers():
    return dict(
        both=pltpu.VMEM((4, 4, 32, 2048), BF),
        far_a=pltpu.VMEM((2, 4, 16, 1024), BF),
        near_a=pltpu.VMEM((4, 4, 16, 1024), BF),
        mid_a=pltpu.VMEM((2, 4, 16, 1024), BF),
        far_a2=pltpu.VMEM((2, 16, 1024), BF),
        near_a2=pltpu.VMEM((4, 16, 1024), BF),
        far_b=pltpu.VMEM((2, 4, 16, 1024), BF),
        near_b=pltpu.VMEM((4, 4, 16, 1024), BF),
        mid_b=pltpu.VMEM((2, 4, 16, 1024), BF),
        far_b2=pltpu.VMEM((2, 16, 1024), BF),
        near_b2=pltpu.VMEM((4, 16, 1024), BF),
        total=pltpu.VMEM((32, 2048), F32),
    )


def torus_reduce(net, place, src, swaps, s):
    x, z, c = place.x, place.z, place.c
    both, out = s.both, s.total
    for k, swap in enumerate(swaps):
        swap.wait_recv()
        add_refs(both.at[k], [both.at[k], src.at[k, :, c]])

    def first():
        mid = s.mid_a
        yield from ring_reduce(
            net, place, "z",
            lambda i, p: both.at[i, :, pl.ds(0, 16), pl.ds(p * 1024, 1024)],
            s.far_a, s.near_a, lambda p: mid.at[p],
        )
        yield
        yield from ring_reduce(
            net, place, "x",
            lambda i, p: mid.at[p, i],
            s.far_a2, s.near_a2,
            lambda p: out.at[pl.ds(0, 16), pl.ds(p * 1024, 1024)],
        )

    def second():
        mid = s.mid_b
        yield from ring_reduce(
            net, place, "x",
            lambda i, p: both.at[:, i, pl.ds(16, 16), pl.ds(p * 1024, 1024)],
            s.far_b, s.near_b, lambda p: mid.at[p],
        )
        yield
        yield from ring_reduce(
            net, place, "z",
            lambda i, p: mid.at[p, i],
            s.far_b2, s.near_b2,
            lambda p: out.at[pl.ds(16, 16), pl.ds(p * 1024, 1024)],
        )

    yield from together(first(), second())


def quad_gather(net, place, buf):
    c, zl = place.c, place.zl
    own = buf.at[pl.ds(c * 64 + zl * 32, 32)]
    one = net.send(own, own, place.zl_pair())
    yield
    one.wait_recv()
    half = buf.at[pl.ds(c * 64, 64)]
    two = net.send(half, half, place.core())
    yield
    two.wait_recv()


def quad_reduce(net, place, src, from_core, from_zl, tmp):
    c, zl = place.c, place.zl
    one = net.send(src.at[pl.ds((1 - c) * 64, 64)], from_core, place.core())
    yield
    one.wait_recv()
    theirs = src[pl.ds(c * 64 + (1 - zl) * 32, 32), :].astype(F32)
    tmp[...] = (theirs + from_core[pl.ds((1 - zl) * 32, 32), :].astype(F32)).astype(BF)
    two = net.send(tmp, from_zl, place.zl_pair())
    yield
    two.wait_recv()


def quad_total(place, src, from_core, from_zl):
    c, zl = place.c, place.zl
    mine = src[pl.ds(c * 64 + zl * 32, 32), :].astype(F32)
    mine = mine + from_core[pl.ds(zl * 32, 32), :].astype(F32)
    return mine + from_zl[...].astype(F32)


def sem_scratch(n):
    return [pltpu.SemaphoreType.DMA((n,)), pltpu.SemaphoreType.DMA((n,))]


ANY = pl.BlockSpec(memory_space=pl.ANY)
VM = pl.BlockSpec(memory_space=pltpu.VMEM)


def lanes(shape):
    return lax.broadcasted_iota(jnp.int32, shape, len(shape) - 1)


def partner(v):
    n = v.shape[-1]
    low = lax.rem(lanes(v.shape), 64) < 32
    return jnp.where(low, pltpu.roll(v, n - 32, 1), pltpu.roll(v, 32, 1))


def head_mean(v):
    n = v.shape[-1]
    r = lax.broadcasted_iota(jnp.int32, (n, n), 0)
    same = lax.div(r, 64) == lax.div(lanes((n, n)), 64)
    return lax.dot_general(
        v, jnp.where(same, 1.0 / 64.0, 0.0), (((1,), (0,)), ((), ())),
        precision=lax.Precision.HIGHEST, preferred_element_type=F32,
    )


def half_of(v, which):
    upper = lanes(v.shape) >= 64
    keep = upper if which else jnp.logical_not(upper)
    return jnp.where(keep, v, jnp.zeros_like(v))


def swap_halves(v):
    return pltpu.roll(v.astype(F32), 64, 1).astype(v.dtype)


def rows_rms(v):
    return lax.rsqrt(jnp.mean(v * v, axis=-1, keepdims=True) + EPS)


N_COPIES = 420
N_LOCAL = 8


def input_plan():
    return dict(
        tokens=VM, cot=VM, small=VM, cos=VM, sin=VM,
        wq=ANY, wk=ANY, wv=ANY, wo=ANY, wg=ANY, wu=ANY, wd=ANY,
    )


def output_plan():
    return dict(
        out=jax.ShapeDtypeStruct((128, 2048), BF),
        dx=jax.ShapeDtypeStruct((128, 2048), BF),
        att_grads=jax.ShapeDtypeStruct((2, 64, 1280), BF),
        ffn_grads=jax.ShapeDtypeStruct((3, 8, 2, 64, 256), BF),
        gain_sums=jax.ShapeDtypeStruct((8, 640), F32),
    )


def slice_buffers(n):
    return dict(
        far=pltpu.VMEM((2, 4, 64, n), BF),
        near=pltpu.VMEM((4, 4, 64, n), BF),
        mid=pltpu.VMEM((2, 4, 64, n), BF),
        far2=pltpu.VMEM((2, 64, n), BF),
        near2=pltpu.VMEM((4, 64, n), BF),
    )


def scratch_plan():
    return dict(
        att=pltpu.VMEM((2, 4, 4, 64, 1280), BF),
        gains=pltpu.VMEM((2, 4, 4, 16, 128), BF),
        ffn=pltpu.VMEM((3, 2, 4, 4, 64, 256), BF),
        cots=pltpu.VMEM((4, 4, 2, 32, 2048), BF),
        xn2=pltpu.VMEM((4, 4, 2, 32, 2048), BF),
        xn=pltpu.VMEM((128, 2048), BF),
        z=pltpu.VMEM((128, 640), F32),
        qk=pltpu.VMEM((128, 640), BF),
        v=pltpu.VMEM((128, 128), BF),
        p=pltpu.VMEM((8, 128, 128), F32),
        o=pltpu.VMEM((128, 512), BF),
        branch=pltpu.VMEM((128, 2048), BF),
        hidden=pltpu.VMEM((32, 2048), F32),
        branch_core=pltpu.VMEM((64, 2048), BF),
        branch_zl=pltpu.VMEM((32, 2048), BF),
        branch_tmp=pltpu.VMEM((32, 2048), BF),
        da=pltpu.VMEM((4, 256, 256), F32),
        ab=pltpu.VMEM((4, 256, 256), BF),
        dg=pltpu.VMEM((4, 256, 256), BF),
        du=pltpu.VMEM((4, 256, 256), BF),
        dxn2_part=pltpu.VMEM((4, 4, 2, 32, 2048), BF),
        ffn_part=pltpu.VMEM((3, 2, 4, 4, 64, 256), BF),
        ffn_far=pltpu.VMEM((2, 3, 4, 64, 256), BF),
        ffn_near=pltpu.VMEM((4, 3, 4, 64, 256), BF),
        ffn_mid=pltpu.VMEM((2, 3, 4, 64, 256), BF),
        dh=pltpu.VMEM((32, 2048), F32),
        dhb=pltpu.VMEM((128, 2048), BF),
        ffn_gain_grad=pltpu.VMEM((1, 2048), F32),
        d_heads=pltpu.VMEM((128, 640), F32),
        att_part=pltpu.VMEM((2, 4, 4, 64, 1280), BF),
        dxn_part=pltpu.VMEM((128, 2048), BF),
        dxn_core=pltpu.VMEM((64, 2048), BF),
        dxn_zl=pltpu.VMEM((32, 2048), BF),
        dxn_tmp=pltpu.VMEM((32, 2048), BF),
        both_z=pltpu.VMEM((2, 64, 1280), BF),
        other_z=pltpu.VMEM((64, 1280), BF),
        gain_in=pltpu.VMEM((7, 8, 640), F32),
        dxn2_sum=torus_buffers(),
        out_sum=torus_buffers(),
        slices=[slice_buffers(n) for _, n, _ in ATT_SLICES],
        send_sems=pltpu.SemaphoreType.DMA((N_COPIES,)),
        recv_sems=pltpu.SemaphoreType.DMA((N_COPIES,)),
        sems=pltpu.SemaphoreType.DMA((N_LOCAL,)),
    )


def named(plan):
    if isinstance(plan, dict):
        return types.SimpleNamespace(**{k: named(v) for k, v in plan.items()})
    if isinstance(plan, list):
        return [named(v) for v in plan]
    return plan


def kernel(*refs):
    s = types.SimpleNamespace()
    for plan in (input_plan(), output_plan(), scratch_plan()):
        leaves, tree = jax.tree.flatten(plan)
        part = jax.tree.unflatten(tree, refs[: len(leaves)])
        refs = refs[len(leaves):]
        vars(s).update(vars(named(part)))
    send_sems, recv_sems, sems = s.send_sems, s.recv_sems, s.sems
    me = Place()
    zh, y, x, c, zl, z = me.zh, me.y, me.x, me.c, me.zl, me.z
    greet(
        [me.step("x", 1), me.step("x", 2), me.step("x", -1)]
        + [me.step("y", 1), me.step("y", 2), me.step("y", -1)]
        + [me.step("z", 1), me.step("z", 2), me.step("z", -1)]
        + [me.core()]
        + [me.at(zh=1 - zh, x=lax.rem(x + k, 4)) for k in (1, 2, 3)]
    )
    net = Net(send_sems, recv_sems)
    att, ffn = s.att, s.ffn
    rows = pl.ds(c * 64 + zl * 32, 32)


    def piece(k):
        return pl.ds(pl.multiple_of(k * 512 + c * 256, 256), 256)

    own = att.at[zh, y, x]
    wide = pl.ds(pl.multiple_of(zl * 512, 512), 512)
    narrow = pl.ds(pl.multiple_of(zl * 128, 128), 128)
    mine = zh * 4 + x
    pairs = [
        (s.wq.at[:, wide], own.at[:, pl.ds(0, 512)]),
        (s.wk.at[:, narrow], own.at[:, pl.ds(512, 128)]),
        (s.wv.at[:, narrow], own.at[:, pl.ds(640, 128)]),
        (s.wo.at[:, wide], own.at[:, pl.ds(768, 512)]),
    ] + [(w.at[:, piece(mine)], ffn.at[m, zh, y, x]) for m, w in enumerate((s.wg, s.wu, s.wd))]
    copies = [pltpu.make_async_copy(a, b, sems.at[k]) for k, (a, b) in enumerate(pairs)]
    for copy in copies:
        copy.start()
    s.cots[z, x, c] = s.cot[rows, :]
    s.gains[zh, y, x] = s.small[...]

    def gather_attention():
        swap = net.send(own, own, me.zh_pair())
        halves = (
            pl.ds(0, ATT_GATHER_SPLIT),
            pl.ds(ATT_GATHER_SPLIT, 1280 - ATT_GATHER_SPLIT),
        )

        def view(part, i, j, half):
            block = att.at[1 - zh if part else zh, i, j]
            return block if half is None else block.at[:, halves[half]]

        yield from cross_gather(net, me, "y", "x", view, late=swap)

    def gather_ffn():
        arrivals = []
        for dz in (0, 1):
            for dx in range(4):
                if dz == 0 and dx == 0:
                    continue
                tx = lax.rem(x + dx, 4)
                tz = 1 - zh if dz else zh
                for m, w in enumerate((s.wg, s.wu, s.wd)):
                    arrivals.append(
                        net.send(
                            w.at[:, piece(tz * 4 + tx)],
                            ffn.at[m, zh, y, x],
                            me.at(zh=tz, x=tx),
                        )
                    )
        yield
        for copy in copies[4:]:
            copy.wait()
        for copy in arrivals:
            copy.wait_recv()
        yield from ring_gather(net, me, "y", lambda i, p: ffn.at[:, p, i])

    def gather_gains():
        gains = s.gains
        steps = [
            (gains.at[zh, y, x], me.zh_pair()),
            (gains.at[:, y, x], me.at(x=x + 1 - 2 * lax.rem(x, 2))),
            (gains.at[:, y, pl.ds(2 * lax.div(x, 2), 2)], me.step("x", 2)),
            (gains.at[:, y], me.at(y=y + 1 - 2 * lax.rem(y, 2))),
            (gains.at[:, pl.ds(2 * lax.div(y, 2), 2)], me.step("y", 2)),
        ]
        for block, device in steps:
            copy = net.send(block, block, device)
            yield
            copy.wait_recv()

    def gain_row(k):
        blocks = []
        for pair in range(16):
            a, b = 2 * pair, 2 * pair + 1
            total = None
            for d in (a, b):
                block = s.gains[d // 16, d // 4 % 4, d % 4].astype(F32)
                total = block if total is None else total + block
            blocks.append(total[k:k + 1, :])
        return jnp.concatenate(blocks, axis=1)

    for copy in copies[:4]:
        copy.wait()
    attention = gather_attention()
    step(attention)
    gains = gather_gains()
    step(gains, attention)
    weights = gather_ffn()
    step(weights)
    for _ in range(2):
        step(gains, attention)
    finish(gains)
    t = s.tokens[...].astype(F32)
    s.xn[...] = (t * rows_rms(t) * gain_row(0)).astype(BF)
    finish(attention)


    cots = torus_gather(net, me, s.cots)
    step(weights, cots)
    raw = nn(s.xn[...], att[:, :, :, :, 0:768].reshape(2048, 768))
    z_raw = raw[:, 0:640]
    s.z[...] = z_raw
    v = raw[:, 640:768].astype(BF)
    s.v[...] = v
    step(cots)
    both_gains = s.small[...].astype(F32)[2:3, :]
    turned = pltpu.roll(both_gains, 64, 1)
    low = lanes((1, 128)) < 64
    gain_q = jnp.where(low, both_gains, turned)
    gain_k = jnp.where(low, turned, both_gains)
    head_gain = jnp.concatenate([gain_q] * 4 + [gain_k], axis=1)
    cos = jnp.concatenate([s.cos[...]] * 5, axis=1)
    sin = jnp.concatenate([s.sin[...]] * 5, axis=1)
    n = z_raw * lax.rsqrt(head_mean(z_raw * z_raw) + EPS) * head_gain
    s.qk[...] = (n * cos + partner(n) * sin).astype(BF)
    step(cots)
    k = s.qk[:, 512:640]
    k_at = {True: k, False: swap_halves(k)}
    v_at = {True: v, False: swap_halves(v)}
    causal = lax.broadcasted_iota(jnp.int32, (128, 128), 0) >= lanes((128, 128))
    for block in range(4):
        out = None
        for side in range(2):
            h = 2 * block + side
            same = side == h // 4
            q = half_of(s.qk[:, block * 128:(block + 1) * 128], side)
            score = jnp.where(causal, nt(q, k_at[same]) * 0.125, -1e30)
            e = jnp.exp(score - jnp.max(score, axis=-1, keepdims=True))
            p = e / jnp.sum(e, axis=-1, keepdims=True)
            s.p[h] = p
            part = nn(p.astype(BF), half_of(v_at[same], side))
            out = part if out is None else out + part
        s.o[:, block * 128:(block + 1) * 128] = out.astype(BF)
    s.branch[...] = nt(s.o[...], att[:, :, :, :, 768:1280].reshape(2048, 512)).astype(BF)
    quad = quad_reduce(
        net, me, s.branch, s.branch_core, s.branch_zl, s.branch_tmp
    )
    step(quad, cots)
    finish(quad)
    hidden = s.tokens[rows, :].astype(F32)
    hidden = hidden + quad_total(me, s.branch, s.branch_core, s.branch_zl)
    s.hidden[...] = hidden
    s.xn2[z, x, c] = (hidden * rows_rms(hidden) * gain_row(1)).astype(BF)
    normed_net = Tagged(net)
    normed = torus_gather(normed_net, me, s.xn2)
    step(normed, weights)
    for _ in range(3):
        step(normed, cots)
    finish(cots)
    step(normed)
    finish(weights)


    def weight(m):
        return ffn[m].reshape(2048, 256)

    for k in range(4):
        s.da[k] = nn(s.cots[k].reshape(256, 2048), weight(2))
        step(normed)
    finish(normed)
    swaps = []
    for k in range(4):
        xk = s.xn2[k].reshape(256, 2048)
        g, u, da = nn(xk, weight(0)), nn(xk, weight(1)), s.da[k]
        sigma = jax.nn.sigmoid(g)
        swish = g * sigma
        s.ab[k] = (swish * u).astype(BF)
        dg = (da * u * sigma * (1.0 + g * (1.0 - sigma))).astype(BF)
        du = (da * swish).astype(BF)
        s.dg[k] = dg
        s.du[k] = du
        part = (nt(dg, weight(0)) + nt(du, weight(1))).astype(BF)
        s.dxn2_part[k] = part.reshape(4, 2, 32, 2048)
        swaps.append(
            net.send(s.dxn2_part.at[k, :, 1 - c], s.dxn2_sum.both.at[k], me.core())
        )


    dxn2 = torus_reduce(net, me, s.dxn2_part, swaps, s.dxn2_sum)
    step(dxn2)

    def weight_grads(first, last):
        def one(d, carry):
            cols = pl.ds(pl.multiple_of(d * 256, 256), 256)
            at = (lax.div(d, 4), lax.rem(d, 4))
            xd = s.xn2[:, :, :, :, cols].reshape(1024, 256)
            dyd = s.cots[:, :, :, :, cols].reshape(1024, 256)
            for m, left, right in ((0, xd, s.dg), (1, xd, s.du), (2, dyd, s.ab)):
                grad = tn(left, right[...].reshape(1024, 256))
                s.ffn_part[(m,) + at] = grad.astype(BF).reshape(4, 64, 256)
            return carry

        lax.fori_loop(first, last, one, 0)

    def reduce_ffn_grads():
        part, mid, grads = s.ffn_part, s.ffn_mid, s.ffn_grads
        yield from ring_reduce(
            net, me, "y", lambda i, p: part.at[:, p, i],
            s.ffn_far, s.ffn_near, lambda p: mid.at[p],
        )
        arrivals = []
        for dz in (0, 1):
            for dx in range(4):
                if dz == 0 and dx == 0:
                    continue
                tx = lax.rem(x + dx, 4)
                tz = 1 - zh if dz else zh
                arrivals.append(
                    net.send(mid.at[tz, :, tx], grads.at[:, mine, c], me.at(zh=tz, x=tx))
                )
        keep = pltpu.make_async_copy(mid.at[zh, :, x], grads.at[:, mine, c], sems.at[7])
        keep.start()
        yield
        keep.wait()
        for copy in arrivals:
            copy.wait_recv()
        swap = net.send(grads.at[:, :, c], grads.at[:, :, c], me.core())
        yield
        swap.wait_recv()

    weight_grads(0, 4)
    step(dxn2)
    weight_grads(4, 8)
    ffn_grads = reduce_ffn_grads()
    step(ffn_grads, dxn2)
    swaps = []
    normed_net.drain()
    for k in range(4):
        part = nt(s.ab[k], weight(2)).astype(BF)
        s.xn2[k] = part.reshape(4, 2, 32, 2048)
        swaps.append(net.send(s.xn2.at[k, :, 1 - c], s.out_sum.both.at[k], me.core()))
        if k % 2 == 1:
            step(dxn2)
    step(ffn_grads)
    finish(dxn2)
    hidden = s.hidden[...]
    r = rows_rms(hidden)
    hat = hidden * r
    d = s.dxn2_sum.total[...]
    s.ffn_gain_grad[...] = jnp.sum(d * hat, axis=0, keepdims=True)
    scaled = d * gain_row(1)
    dh = s.cot[rows, :].astype(F32)
    dh = dh + r * (scaled - hat * jnp.mean(scaled * hat, axis=-1, keepdims=True))
    s.dh[...] = dh
    s.dhb[rows, :] = dh.astype(BF)
    spread = quad_gather(net, me, s.dhb)
    step(spread)

    def finish_output():
        yield from torus_reduce(net, me, s.xn2, swaps, s.out_sum)
        s.out[rows, :] = (s.hidden[...] + s.out_sum.total[...]).astype(BF)
        yield from quad_gather(net, me, s.out)

    output = finish_output()
    step(spread)
    step(output)
    finish(spread)


    def reduce_att_grads(k):
        start, width, order = ATT_SLICES[k]
        cols = pl.ds(start, width)
        part, mid, both_z = s.att_part, s.slices[k].mid, s.both_z
        one, two = order
        if one == "y":
            view = lambda i, p: part.at[p, i, :, :, cols]
        else:
            view = lambda i, p: part.at[p, :, i, :, cols]
        yield from ring_reduce(
            net, me, one, view, s.slices[k].far, s.slices[k].near, lambda p: mid.at[p]
        )
        yield
        yield from ring_reduce(
            net, me, two, lambda i, p: mid.at[p, i],
            s.slices[k].far2, s.slices[k].near2, lambda p: both_z.at[p, :, cols],
        )
        other = s.other_z.at[:, cols]
        swap = net.send(both_z.at[1 - zh, :, cols], other, me.zh_pair())
        yield
        swap.wait_recv()
        done = s.att_grads.at[zl, :, cols]
        add_refs(done, [both_z.at[zh, :, cols], other])
        swap = net.send(done, done, me.zl_pair())
        yield
        swap.wait_recv()

    dhb = s.dhb[...]
    grad = tn(dhb, s.o[...]).astype(BF)
    s.att_part[:, :, :, :, 768:1280] = grad.reshape(2, 4, 4, 64, 512)
    slices = [reduce_att_grads(k) for k in range(4)]
    step(slices[2], slices[3])
    do = nn(dhb, att[:, :, :, :, 768:1280].reshape(2048, 512)).astype(BF)
    step(output, ffn_grads)
    v = s.v[...]
    k = s.qk[:, 512:640]
    k_at = {True: k, False: swap_halves(k)}
    v_at = {True: v, False: swap_halves(v)}
    zero = jnp.zeros((128, 128), F32)
    dk = {True: zero, False: zero}
    dv = {True: zero, False: zero}
    for block in range(4):
        dq = None
        for side in range(2):
            h = 2 * block + side
            same = side == h // 4
            p = s.p[h]
            dob = half_of(do[:, block * 128:(block + 1) * 128], side)
            q = half_of(s.qk[:, block * 128:(block + 1) * 128], side)
            dp = nt(dob, v_at[same])
            dv[same] = dv[same] + tn(p.astype(BF), dob)
            ds = (p * (dp - jnp.sum(p * dp, axis=-1, keepdims=True))).astype(BF)
            part = nn(ds, half_of(k_at[same], side))
            dq = part if dq is None else dq + part
            dk[same] = dk[same] + tn(ds, q)
        s.d_heads[:, block * 128:(block + 1) * 128] = dq * 0.125
    s.d_heads[:, 512:640] = (dk[True] + pltpu.roll(dk[False], 64, 1)) * 0.125
    dvb = (dv[True] + pltpu.roll(dv[False], 64, 1)).astype(BF)
    step(output, ffn_grads, slices[2], slices[3])
    dout = s.d_heads[...]
    dn = dout * cos - partner(dout) * sin
    z_raw = s.z[...]
    r = lax.rsqrt(head_mean(z_raw * z_raw) + EPS)
    zhat = z_raw * r
    dgain = jnp.sum(dn * zhat, axis=0, keepdims=True)
    q_pairs = dgain[:, 0:128] + dgain[:, 128:256] + dgain[:, 256:384] + dgain[:, 384:512]
    q_pairs = q_pairs + pltpu.roll(q_pairs, 64, 1)
    k_pairs = dgain[:, 512:640]
    k_pairs = k_pairs + pltpu.roll(k_pairs, 64, 1)
    dz = dn * head_gain
    dz = r * (dz - zhat * head_mean(dz * zhat))
    low_grads = jnp.concatenate([dz.astype(BF), dvb], axis=1)
    back = nt(low_grads, att[:, :, :, :, 0:768].reshape(2048, 768))
    s.dxn_part[...] = back.astype(BF)
    quad = quad_reduce(net, me, s.dxn_part, s.dxn_core, s.dxn_zl, s.dxn_tmp)
    step(quad, output, ffn_grads)
    grad = tn(s.xn[...], low_grads).astype(BF)
    s.att_part[:, :, :, :, 0:768] = grad.reshape(2, 4, 4, 64, 768)
    step(slices[0], slices[1])


    def tokens_and_gains():
        yield from quad
        d = quad_total(me, s.dxn_part, s.dxn_core, s.dxn_zl)
        t = s.tokens[rows, :].astype(F32)
        r = rows_rms(t)
        hat = t * r
        scaled = d * gain_row(0)
        total = s.dh[...]
        total = total + r * (scaled - hat * jnp.mean(scaled * hat, axis=-1, keepdims=True))
        s.dx[rows, :] = total.astype(BF)
        gain_grad = jnp.sum(d * hat, axis=0, keepdims=True)
        sums = s.gain_sums
        for k in range(8):
            part = slice(k * 256, (k + 1) * 256)
            sums[k:k + 1, 0:256] = gain_grad[:, part]
            sums[k:k + 1, 256:512] = s.ffn_gain_grad[:, part]
        row = lax.broadcasted_iota(jnp.int32, (8, 128), 0)
        head_grad = jnp.where(lanes((8, 128)) < 64, q_pairs, k_pairs)
        sums[:, 512:640] = jnp.where(row == 0, head_grad, 0.0)
        spread = quad_gather(net, me, s.dx)
        step(spread)
        devices = [
            me.core(),
            me.zl_pair(),
            me.zh_pair(),
            me.at(x=x + 1 - 2 * lax.rem(x, 2)),
            me.step("x", 2),
            me.at(y=y + 1 - 2 * lax.rem(y, 2)),
            me.step("y", 2),
        ]
        for k, device in enumerate(devices):
            copy = net.send(sums, s.gain_in.at[k], device)
            yield
            copy.wait_recv()
            net.wait_send(copy)
            sums[...] = sums[...] + s.gain_in[k]
            step(spread)

    rest = tokens_and_gains()
    finish(rest, slices[2], slices[3], slices[0], slices[1], output, ffn_grads)
    net.drain()


def everything(**args):
    in_specs, in_tree = jax.tree.flatten(input_plan())
    out_shapes, out_tree = jax.tree.flatten(output_plan())
    results = pl.pallas_call(
        kernel,
        out_shape=tuple(out_shapes),
        in_specs=in_specs,
        out_specs=[VM] * len(out_shapes),
        scratch_shapes=jax.tree.leaves(scratch_plan()),
        compiler_params=pltpu.CompilerParams(
            vmem_limit_bytes=VMEM_BYTES, collective_id=1, has_side_effects=True
        ),
        name="everything",
    )(*in_tree.flatten_up_to(args))
    return named(jax.tree.unflatten(out_tree, results))


def finish_kernel(
    out_in, dx_in, att, ffn, sums,
    out, dx, gq, gk, gv, go, gate, up, down, attn_gain, ffn_gain, gain_q, gain_k,
):
    out[...] = out_in[...]
    dx[...] = dx_in[...].astype(F32)
    for zl in range(2):
        for ref, start, width in ((gq, 0, 512), (gk, 512, 128), (gv, 640, 128), (go, 768, 512)):
            ref[:, zl * width:(zl + 1) * width] = att[zl, :, start:start + width].astype(F32)
    for m, ref in enumerate((gate, up, down)):
        for k in range(8):
            for c in range(2):
                start = k * 512 + c * 256
                ref[:, start:start + 256] = ffn[m, k, c].astype(F32)
    dp = lax.axis_index("dp")
    row = sums[pl.ds(lax.div(dp, 4), 1), :]
    shift = lax.rem(4 - lax.rem(dp, 4), 4) * 64
    attn_gain[...] = pltpu.roll(row[:, 0:256], shift, 1)[:, 0:64]
    ffn_gain[...] = pltpu.roll(row[:, 256:512], shift, 1)[:, 0:64]
    gain_q[...] = sums[0:1, 512:576]
    gain_k[...] = sums[0:1, 576:640]


def rows_block(*shape):
    n = len(shape)
    return pl.BlockSpec(shape, lambda t: (0,) * (n - 2) + (t, 0))


def whole_block(*shape):
    return pl.BlockSpec(shape, lambda t: (0,) * len(shape))


def finished(r):
    tall = rows_block(32, 2048)
    full, half, wide = (rows_block(16, n) for n in (1024, 256, 4096))
    one = whole_block(1, 64)
    sizes = [(64, 1024), (64, 256), (64, 256), (64, 1024)] + [(64, 4096)] * 3 + [(1, 64)] * 4
    return pl.pallas_call(
        finish_kernel,
        grid=(4,),
        out_shape=(
            jax.ShapeDtypeStruct((128, 2048), BF),
            jax.ShapeDtypeStruct((128, 2048), F32),
        )
        + tuple(jax.ShapeDtypeStruct(size, F32) for size in sizes),
        in_specs=[
            tall, tall, rows_block(2, 16, 1280), rows_block(3, 8, 2, 16, 256), whole_block(8, 640),
        ],
        out_specs=[tall, tall, full, half, half, full, wide, wide, wide, one, one, one, one],
        name="finished",
    )(r.out, r.dx, r.att_grads, r.ffn_grads, r.gain_sums)


def rotary_tables():
    position = np.arange(128, dtype=np.float64)[:, None]
    lane = np.arange(128)
    angle = position * THETA ** (-2.0 * (lane % 32) / 64.0)[None, :]
    sign = np.where(lane % 64 < 32, -1.0, 1.0)
    return np.cos(angle).astype(np.float32), (np.sin(angle) * sign).astype(np.float32)


def on_device(
    tokens, gain_attn, w_query, w_key, w_value, gain_query, gain_key, w_out, gain_ffn,
    w_gate, w_up, w_down, cotangent,
):
    cos, sin = (jnp.asarray(t) for t in rotary_tables())
    dp = lax.axis_index("dp")
    odd = lax.rem(dp, 2)
    lane = lax.broadcasted_iota(jnp.int32, (2, 128), 1)
    two = jnp.stack([gain_attn, gain_ffn])
    placed = jnp.where(lax.div(lane, 64) == odd, jnp.concatenate([two, two], axis=1), 0)
    heads = jnp.concatenate([gain_query, gain_key]).reshape(1, 128)
    small = jnp.concatenate([placed.astype(BF), heads, jnp.zeros((13, 128), BF)], axis=0)
    r = everything(
        tokens=tokens, cot=cotangent, small=small, cos=cos, sin=sin,
        wq=w_query, wk=w_key, wv=w_value, wo=w_out, wg=w_gate, wu=w_up, wd=w_down,
    )
    out, dx, gq, gk, gv, go, gate, up, down, attn, ffn, gain_q, gain_k = finished(r)
    attn, ffn, gain_q, gain_k = (v.reshape(64) for v in (attn, ffn, gain_q, gain_k))
    return out, dx, attn, gq, gk, gv, gain_q, gain_k, go, ffn, gate, up, down


def solution(mesh):
    return jax.shard_map(
        on_device,
        mesh=mesh,
        in_specs=(
            P("dp", None), P("dp"), P("dp", "head"), P("dp", "head"), P("dp", "head"),
            P(), P(), P("dp", "head"), P("dp"),
            P("dp", "tensor"), P("dp", "tensor"), P("dp", "tensor"), P("dp", None),
        ),
        out_specs=(
            P("dp", None), P("dp", None), P("dp"),
            P("dp", "head"), P("dp", "head"), P("dp", "head"),
            P(), P(), P("dp", "head"), P("dp"),
            P("dp", "tensor"), P("dp", "tensor"), P("dp", "tensor"),
        ),
        check_vma=False,
    )
```

time: 2410 us -> 210 us (0.09)
  waiting for transfers between devices: 1840 us -> 0 us
  blocking collectives: 360 us -> 0 us
  Pallas kernels: 0 us -> 207 us
  matrix products: 123 us -> 0 us
  local copies, waits for them, and re-layouts: 31.3 us -> 0.08 us
  other arithmetic: 26.5 us -> 2.24 us
    reduce_scatter x6 -> x0, waiting for transfers between devices: 888 us -> none  [the longest x1 221 us: on_device(): lax.psum_scatter(grad_up.astype(jnp.bfloat16), 'dp', scatter_dimension=0,...]
    all_gather x7 -> x0, waiting for transfers between devices: 643 us -> none  [the longest x1 160 us: on_device(): lax.all_gather(w_up, 'dp', axis=0, tiled=True)]
    unnamed x19 -> x0, waiting for transfers between devices: 224 us -> none
    pallas_call x0 -> x2, Pallas kernels: none -> 207 us  [the longest x1 202 us: everything(): pl.pallas_call(kernel, out_shape=tuple(out_shapes), in_specs=in_specs, ou...]
    unnamed x2 -> x0, blocking collectives: 189 us -> none
    psum x1 -> x0, blocking collectives: 171 us -> none  [on_device(): grad_gq, grad_gk = lax.psum((grad_gq, grad_gk), ('dp', 'head'))]
    dot_general x27 -> x0, matrix products: 123 us -> none  [the longest x7 46.4 us: over_cols(): lax.dot_general(left, right, (((1,), (1,)), ((), ())), preferred_element_...]
    psum x4 -> x0, waiting for transfers between devices: 88.3 us -> none  [the longest x1 37 us: on_device(): lax.psum(over_cols(active, wd).astype(jnp.bfloat16), 'tensor')]
  transfers between devices with their start and end apart: 18 -> 0, of which waited for: 15 -> 0; matrix products, arithmetic and copies ran while one was open for 5% -> 0% of each run, Pallas kernels for 0% -> 0%
where the time goes in v2:
time: 210 us
  Pallas kernels  207 us (99%)
  other arithmetic  2.24 us (1%)
    pallas_call x1, Pallas kernels, everything(): pl.pallas_call(kernel, out_shape=tuple(out_shapes), in_specs=in_specs, ou...  202 us
    pallas_call x1, Pallas kernels, finished(): pl.pallas_call(finish_kernel, grid=(4,), out_shape=(jax.ShapeDtypeStruct(...  4.71 us

profile of v2, /device:TPU:0, one launch (start us, length us, event | category | flops | bytes accessed | tf_op | source)
XLA Modules:
  0.0 209.8 jit_solution(7422069824070180428)
XLA Ops:
  0.7 0.8 broadcast_select_fusion
  1.5 0.7 maximum_bitcast_fusion
  2.2 0.1 pad.2.clone
  2.3 0.7 maximum_maximum_fusion.refs_3_
  3.0 201.9 %everything.1 = (bf16[2,64,1280]{2,1,0:T(8,128)(2,1)}, bf16[128,2048]{1,0:T(8,128)(2,1)}, bf16[3,8,2,64,256]{4,3,2,1,0:T(8,128)(2,1)}, f32[8,640]{1,0:T(8,128)}, bf16[128,2048]{1,0:T(8,128)(2,1)}) custom-call(f32[128,128]{1,0:T(8,128)} %constant.26.clone.refs_0_, bf16[128,2048]{1,0:T(8,128)(2,1)} %refs_1_.1, f32[128,128]{1,0:T(8,128)} %constant.27.clone.refs_2_, ...), custom_call_target="tpu_custom_call" | custom-call | tf_op jit(solution)/shard_map/everything/pallas_call | solution.py:947
  204.9 4.7 %finished.1 = (bf16[128,2048]{1,0:T(8,128)(2,1)}, f32[128,2048]{1,0:T(8,128)}, f32[64,1024]{1,0:T(8,128)}, f32[64,256]{1,0:T(8,128)}, f32[64,256]{1,0:T(8,128)},...) custom-call(bf16[128,2048]{1,0:T(8,128)(2,1)} %get-tuple-element.31., ...), custom_call_target="tpu_custom_call" | custom-call | tf_op jit(solution)/shard_map/finished/pallas_call | solution.py:998
  (2 shorter events, 0.0 us)

commit v3 on v2

--- a/solution.py
+++ b/solution.py
@@ -14,7 +14,7 @@
 EPS = 1e-05
 THETA = 1000000.0
 VMEM_BYTES = 62 << 20
-ATT_GATHER_SPLIT = 768
+ATT_GATHER_SPLIT = 896
 ATT_SLICES = ((0, 384, "yx"), (384, 384, "xy"), (768, 256, "yx"), (1024, 256, "xy"))
 
 
@@ -67,36 +67,63 @@
         return {"x": self.x, "y": self.y, "z": self.z}[axis]
 
 
+class Copy:
+    def __init__(self, copy):
+        self.copy = copy
+        self.left = True
+
+    def wait_recv(self):
+        self.copy.wait_recv()
+
+    def wait_send(self):
+        if self.left:
+            self.copy.wait_send()
+            self.left = False
+
+
+class Group:
+    def __init__(self, sem):
+        self.sem = sem
+
+    def wait(self, like):
+        pltpu.make_async_copy(like, like, self.sem).wait()
+
+
 class Net:
     def __init__(self, send_sems, recv_sems):
         self.send_sems = send_sems
         self.recv_sems = recv_sems
-        self.count = 0
-        self.left = []
-
-    def send(self, src, dst, device):
-        k = self.count
-        assert k < self.send_sems.shape[0]
-        self.count += 1
+        self.slots = [None] * send_sems.shape[0]
+        self.sends = 0
+        self.groups = 0
+
+    def group(self):
+        k = self.groups
+        assert k < self.recv_sems.shape[0], k
+        self.groups += 1
+        return Group(self.recv_sems.at[k])
+
+    def send(self, src, dst, device, group=None):
+        slot = self.sends % len(self.slots)
+        self.sends += 1
+        if self.slots[slot] is not None:
+            self.slots[slot].wait_send()
         copy = pltpu.make_async_remote_copy(
             src_ref=src,
             dst_ref=dst,
-            send_sem=self.send_sems.at[k],
-            recv_sem=self.recv_sems.at[k],
+            send_sem=self.send_sems.at[slot],
+            recv_sem=(group or self.group()).sem,
             device_id=device,
             device_id_type=MESH,
         )
         copy.start()
-        self.left.append(copy)
-        return copy
-
-    def wait_send(self, copy):
-        copy.wait_send()
-        self.left = [other for other in self.left if other is not copy]
+        self.slots[slot] = Copy(copy)
+        return self.slots[slot]
 
     def drain(self):
-        for copy in self.left:
-            copy.wait_send()
+        for copy in self.slots:
+            if copy is not None:
+                copy.wait_send()
 
 
 class Tagged:
@@ -104,13 +131,16 @@
         self.net = net
         self.copies = []
 
-    def send(self, src, dst, device):
-        self.copies.append(self.net.send(src, dst, device))
+    def group(self):
+        return self.net.group()
+
+    def send(self, src, dst, device, group=None):
+        self.copies.append(self.net.send(src, dst, device, group))
         return self.copies[-1]
 
     def drain(self):
         for copy in self.copies:
-            self.net.wait_send(copy)
+            copy.wait_send()
 
 
 def greet(devices):
@@ -172,44 +202,58 @@
     lax.fori_loop(0, count, body, 0)
 
 
-def ring_gather(net, place, axis, view, also=None):
+def ring_gather(net, place, axis, view, like):
+    i = place.ring(axis)
+    before, after = lax.rem(i + 3, 4), lax.rem(i + 1, 4)
+    up, down = place.step(axis, 1), place.step(axis, -1)
+    rest = net.group()
+    u0 = net.send(view(i, 0), view(i, 0), up)
+    d1 = net.send(view(i, 1), view(i, 1), down)
+    net.send(view(i, 1), view(i, 1), up, rest)
+    net.send(view(i, 0), view(i, 0), down, rest)
+    yield
+    u0.wait_recv()
+    net.send(view(before, 0), view(before, 0), up, rest)
+    d1.wait_recv()
+    net.send(view(after, 1), view(after, 1), down, rest)
+    yield
+    rest.wait(like)
+
+
+def ring_reduce(net, place, axis, view, far, near, out):
     i = place.ring(axis)
     before, after, across = lax.rem(i + 3, 4), lax.rem(i + 1, 4), lax.rem(i + 2, 4)
     up, down = place.step(axis, 1), place.step(axis, -1)
-    u0 = net.send(view(i, 0), view(i, 0), up)
-    d1 = net.send(view(i, 1), view(i, 1), down)
-    u1 = net.send(view(i, 1), view(i, 1), up)
-    d0 = net.send(view(i, 0), view(i, 0), down)
-    yield
-    u0.wait_recv()
-    f0 = net.send(view(before, 0), view(before, 0), up)
-    d1.wait_recv()
-    f1 = net.send(view(after, 1), view(after, 1), down)
-    if also is not None:
-        also(view(before, 0))
-        also(view(after, 1))
-    yield
-    u1.wait_recv()
-    d0.wait_recv()
-    if also is not None:
-        also(view(before, 1))
-        also(view(after, 0))
-    f0.wait_recv()
-    f1.wait_recv()
-    if also is not None:
-        also(view(across, 0))
-        also(view(across, 1))
-
-
-def cross_gather(net, place, one, two, view, late=None, also=None):
+    fars, nears = net.group(), net.group()
+    net.send(view(across, 0), far.at[0], up, fars)
+    net.send(view(across, 1), far.at[1], down, fars)
+    yield
+    net.send(view(after, 1), near.at[1], up, nears)
+    net.send(view(before, 0), near.at[2], down, nears)
+    yield
+    fars.wait(far)
+    add_refs(far.at[0], [far.at[0], view(after, 0)])
+    net.send(far.at[0], near.at[0], up, nears)
+    add_refs(far.at[1], [far.at[1], view(before, 1)])
+    net.send(far.at[1], near.at[3], down, nears)
+    yield
+    nears.wait(near)
+    add_refs(out(0), [view(i, 0), near.at[0], near.at[2]])
+    add_refs(out(1), [view(i, 1), near.at[1], near.at[3]])
+
+
+def cross_gather(net, place, one, two, view, likes, late=None, also=None, only=None):
     ring = [lax.rem(place.ring(one) + k, 4) for k in range(4)]
     other = [lax.rem(place.ring(two) + k, 4) for k in range(4)]
     up = {one: place.step(one, 1), two: place.step(two, 1)}
     down = {one: place.step(one, -1), two: place.step(two, -1)}
     corners = []
-
-    def spread(block, axis):
-        return net.send(block, block, up[axis]), net.send(block, block, down[axis])
+    last = [net.group(), net.group()]
+    finals = [[], []]
+
+    def spread(block, axis, group):
+        net.send(block, block, up[axis], group)
+        net.send(block, block, down[axis], group)
 
     def arrived(block):
         if also is not None:
@@ -224,12 +268,18 @@
     def turn(axis, part, k):
         across = two if axis == one else one
         half = 1 if axis == one else 0
-        copies = spread(along(axis, part, k, half), across)
-        corners.append((axis, part, k, half, across, copies))
+        if only is not None and half != only:
+            return
+        group = net.group()
+        spread(along(axis, part, k, half), across, group)
+        corners.append((axis, part, k, half, across, group))
 
     def own(part):
+        group = net.group()
         block = view(part, ring[0], other[0], None)
-        return {axis: spread(block, axis) for axis in (one, two)}
+        for axis in (one, two):
+            spread(block, axis, group)
+        return group
 
     crosses = [own(0)]
     if late is None:
@@ -239,142 +289,143 @@
         late.wait_recv()
         crosses.append(own(1))
         yield
-    far = []
+    far = net.group()
     for part in (0, 1):
-        order = ((0, 3), (1, 1)) if part == 0 else ((1, 1), (0, 3))
-        for n, (which, k) in enumerate(order):
+        crosses[part].wait(likes(None, 4))
+        order = (3, 1) if part == 0 else (1, 3)
+        for n, k in enumerate(order):
             for axis in (one, two):
-                crosses[part][axis][which].wait_recv()
                 block = arrived(along(axis, part, k))
                 if n == 0:
-                    on = (up, down)[part][axis]
-                    far.append((axis, part, net.send(block, block, on)))
+                    net.send(block, block, (up, down)[part][axis], far)
                 turn(axis, part, k)
         yield
-    for axis, part, copy in far:
-        copy.wait_recv()
-        arrived(along(axis, part, 2))
-        turn(axis, part, 2)
-    yield
-    last = []
-    for n, (axis, part, k, half, across, copies) in enumerate(corners):
-        for which, step_ in ((0, 3), (1, 1)):
-            copies[which].wait_recv()
+    far.wait(likes(None, 4))
+    for part in (0, 1):
+        for axis in (one, two):
+            arrived(along(axis, part, 2))
+            turn(axis, part, 2)
+    yield
+    for n, (axis, part, k, half, across, group) in enumerate(corners):
+        group.wait(likes(half, 2))
+        for which, by in ((0, 3), (1, 1)):
             if axis == one:
-                block = view(part, ring[k], other[step_], half)
+                block = view(part, ring[k], other[by], half)
                 final = view(part, ring[k], other[2], half)
             else:
-                block = view(part, ring[step_], other[k], half)
+                block = view(part, ring[by], other[k], half)
                 final = view(part, ring[2], other[k], half)
             arrived(block)
             if which == part:
-                on = (up, down)[part][across]
-                last.append((net.send(block, block, on), final))
+                net.send(block, block, (up, down)[part][across], last[half])
+                finals[half].append(final)
         if n % 4 == 3:
             yield
-    for copy, final in last:
-        copy.wait_recv()
-        arrived(final)
-
-
-def ring_reduce(net, place, axis, view, far, near, out):
-    i = place.ring(axis)
-    before, after, across = lax.rem(i + 3, 4), lax.rem(i + 1, 4), lax.rem(i + 2, 4)
-    up, down = place.step(axis, 1), place.step(axis, -1)
-    f0 = net.send(view(across, 0), far.at[0], up)
-    f1 = net.send(view(across, 1), far.at[1], down)
-    u1 = net.send(view(after, 1), near.at[1], up)
-    d0 = net.send(view(before, 0), near.at[2], down)
-    yield
-    f0.wait_recv()
-    add_refs(far.at[0], [far.at[0], view(after, 0)])
-    u0 = net.send(far.at[0], near.at[0], up)
-    f1.wait_recv()
-    add_refs(far.at[1], [far.at[1], view(before, 1)])
-    d1 = net.send(far.at[1], near.at[3], down)
-    yield
-    u1.wait_recv()
-    d0.wait_recv()
-    u0.wait_recv()
-    d1.wait_recv()
-    add_refs(out(0), [view(i, 0), near.at[0], near.at[2]])
-    add_refs(out(1), [view(i, 1), near.at[1], near.at[3]])
-
-
-def torus_gather(net, place, buf):
+    for half in (0, 1):
+        if finals[half]:
+            last[half].wait(likes(half, len(finals[half])))
+            for final in finals[half]:
+                arrived(final)
+
+
+def order_reduce(net, place, one, two, view, s, out):
+    ring = [lax.rem(place.ring(one) + k, 4) for k in range(4)]
+    other = [lax.rem(place.ring(two) + k, 4) for k in range(4)]
+    up, down = place.step(one, 1), place.step(one, -1)
+    order = (2, 1, 3, 0)
+    fars = {k: net.group() for k in order}
+    nears = {k: net.group() for k in order}
+    others = net.group()
+    for k in order:
+        net.send(view(0, ring[2], other[k]), s.far.at[k, 0], up, fars[k])
+        net.send(view(1, ring[2], other[k]), s.far.at[k, 1], down, fars[k])
+    for k in order:
+        net.send(view(1, ring[1], other[k]), s.near.at[k, 1], up, nears[k])
+        net.send(view(0, ring[3], other[k]), s.near.at[k, 2], down, nears[k])
+    yield
+    for k in order:
+        fars[k].wait(s.far.at[k])
+        add_refs(s.far.at[k, 0], [s.far.at[k, 0], view(0, ring[1], other[k])])
+        net.send(s.far.at[k, 0], s.near.at[k, 0], up, nears[k])
+        add_refs(s.far.at[k, 1], [s.far.at[k, 1], view(1, ring[3], other[k])])
+        net.send(s.far.at[k, 1], s.near.at[k, 3], down, nears[k])
+        if k != 1:
+            yield
+    for k in order:
+        nears[k].wait(s.near.at[k])
+        for p in (0, 1):
+            add_refs(
+                s.mid.at[k, p],
+                [view(p, ring[0], other[k]), s.near.at[k, p], s.near.at[k, 2 + p]],
+            )
+        if k:
+            net.send(s.mid.at[k], s.last.at[k - 1], place.step(two, k), others)
+        if k != 1:
+            yield
+    others.wait(s.last)
+    for p in (0, 1):
+        add_refs(out(p), [s.mid.at[0, p]] + [s.last.at[k, p] for k in range(3)])
+
+
+def order_buffers(rows, columns):
+    return dict(
+        far=pltpu.VMEM((4, 2, rows, columns), BF),
+        near=pltpu.VMEM((4, 4, rows, columns), BF),
+        mid=pltpu.VMEM((4, 2, rows, columns), BF),
+        last=pltpu.VMEM((3, 2, rows, columns), BF),
+    )
+
+
+def torus_gather(net, place, buf, only=None):
     c = place.c
     other = place.core()
-    swaps = []
+    swaps = net.group()
 
     def also(block):
-        swaps.append(net.send(block, block, other))
+        net.send(block, block, other, swaps)
+
+    def rows(half):
+        return pl.ds(0, 32) if half is None or only is not None else pl.ds(half * 16, 16)
 
     def view(part, i, j, half):
-        rows = pl.ds(0, 32) if half is None else pl.ds(half * 16, 16)
-        return buf.at[i, j, c, rows, pl.ds(part * 1024, 1024)]
+        return buf.at[i, j, c, rows(half), pl.ds(part * 1024, 1024)]
+
+    def likes(half, n):
+        return buf.at[pl.ds(0, 2), pl.ds(0, n // 2), 0, rows(half), pl.ds(0, 1024)]
 
     also(buf.at[place.z, place.x, c])
-    yield from cross_gather(net, place, "z", "x", view, also=also)
-    yield
-    for swap in swaps:
-        swap.wait_recv()
+    yield from cross_gather(net, place, "z", "x", view, likes, also=also, only=only)
+    yield
+    swaps.wait(buf.at[:, :, 1 - c])
 
 
 def torus_buffers():
     return dict(
         both=pltpu.VMEM((4, 4, 32, 2048), BF),
-        far_a=pltpu.VMEM((2, 4, 16, 1024), BF),
-        near_a=pltpu.VMEM((4, 4, 16, 1024), BF),
-        mid_a=pltpu.VMEM((2, 4, 16, 1024), BF),
-        far_a2=pltpu.VMEM((2, 16, 1024), BF),
-        near_a2=pltpu.VMEM((4, 16, 1024), BF),
-        far_b=pltpu.VMEM((2, 4, 16, 1024), BF),
-        near_b=pltpu.VMEM((4, 4, 16, 1024), BF),
-        mid_b=pltpu.VMEM((2, 4, 16, 1024), BF),
-        far_b2=pltpu.VMEM((2, 16, 1024), BF),
-        near_b2=pltpu.VMEM((4, 16, 1024), BF),
+        halves=[order_buffers(16, 1024), order_buffers(16, 1024)],
         total=pltpu.VMEM((32, 2048), F32),
     )
 
 
 def torus_reduce(net, place, src, swaps, s):
-    x, z, c = place.x, place.z, place.c
-    both, out = s.both, s.total
+    c = place.c
     for k, swap in enumerate(swaps):
         swap.wait_recv()
-        add_refs(both.at[k], [both.at[k], src.at[k, :, c]])
-
-    def first():
-        mid = s.mid_a
-        yield from ring_reduce(
-            net, place, "z",
-            lambda i, p: both.at[i, :, pl.ds(0, 16), pl.ds(p * 1024, 1024)],
-            s.far_a, s.near_a, lambda p: mid.at[p],
-        )
-        yield
-        yield from ring_reduce(
-            net, place, "x",
-            lambda i, p: mid.at[p, i],
-            s.far_a2, s.near_a2,
-            lambda p: out.at[pl.ds(0, 16), pl.ds(p * 1024, 1024)],
-        )
-
-    def second():
-        mid = s.mid_b
-        yield from ring_reduce(
-            net, place, "x",
-            lambda i, p: both.at[:, i, pl.ds(16, 16), pl.ds(p * 1024, 1024)],
-            s.far_b, s.near_b, lambda p: mid.at[p],
-        )
-        yield
-        yield from ring_reduce(
-            net, place, "z",
-            lambda i, p: mid.at[p, i],
-            s.far_b2, s.near_b2,
-            lambda p: out.at[pl.ds(16, 16), pl.ds(p * 1024, 1024)],
-        )
-
-    yield from together(first(), second())
+        add_refs(s.both.at[k], [s.both.at[k], src.at[k, :, c]])
+
+    def part_of(half, part):
+        return pl.ds(half * 16, 16), pl.ds(part * 1024, 1024)
+
+    yield from together(
+        order_reduce(
+            net, place, "z", "x", lambda p, i, j: s.both.at[(i, j) + part_of(0, p)],
+            s.halves[0], lambda p: s.total.at[part_of(0, p)],
+        ),
+        order_reduce(
+            net, place, "x", "z", lambda p, i, j: s.both.at[(j, i) + part_of(1, p)],
+            s.halves[1], lambda p: s.total.at[part_of(1, p)],
+        ),
+    )
 
 
 def quad_gather(net, place, buf):
@@ -450,13 +501,14 @@
     return lax.rsqrt(jnp.mean(v * v, axis=-1, keepdims=True) + EPS)
 
 
-N_COPIES = 420
-N_LOCAL = 8
+N_SENDS = 64
+N_GROUPS = 190
+N_LOCAL = 13
 
 
 def input_plan():
     return dict(
-        tokens=VM, cot=VM, small=VM, cos=VM, sin=VM,
+        tokens=ANY, cot=ANY, small=ANY, cos=ANY, sin=ANY,
         wq=ANY, wk=ANY, wv=ANY, wo=ANY, wg=ANY, wu=ANY, wd=ANY,
     )
 
@@ -471,18 +523,12 @@
     )
 
 
-def slice_buffers(n):
-    return dict(
-        far=pltpu.VMEM((2, 4, 64, n), BF),
-        near=pltpu.VMEM((4, 4, 64, n), BF),
-        mid=pltpu.VMEM((2, 4, 64, n), BF),
-        far2=pltpu.VMEM((2, 64, n), BF),
-        near2=pltpu.VMEM((4, 64, n), BF),
-    )
-
-
 def scratch_plan():
     return dict(
+        tok=pltpu.VMEM((128, 2048), BF),
+        small_in=pltpu.VMEM((16, 128), BF),
+        cos_in=pltpu.VMEM((128, 128), F32),
+        sin_in=pltpu.VMEM((128, 128), F32),
         att=pltpu.VMEM((2, 4, 4, 64, 1280), BF),
         gains=pltpu.VMEM((2, 4, 4, 16, 128), BF),
         ffn=pltpu.VMEM((3, 2, 4, 4, 64, 256), BF),
@@ -505,9 +551,9 @@
         du=pltpu.VMEM((4, 256, 256), BF),
         dxn2_part=pltpu.VMEM((4, 4, 2, 32, 2048), BF),
         ffn_part=pltpu.VMEM((3, 2, 4, 4, 64, 256), BF),
-        ffn_far=pltpu.VMEM((2, 3, 4, 64, 256), BF),
-        ffn_near=pltpu.VMEM((4, 3, 4, 64, 256), BF),
-        ffn_mid=pltpu.VMEM((2, 3, 4, 64, 256), BF),
+        ffn_far=pltpu.VMEM((4, 2, 3, 64, 256), BF),
+        ffn_near=pltpu.VMEM((4, 4, 3, 64, 256), BF),
+        ffn_mid=pltpu.VMEM((4, 2, 3, 64, 256), BF),
         dh=pltpu.VMEM((32, 2048), F32),
         dhb=pltpu.VMEM((128, 2048), BF),
         ffn_gain_grad=pltpu.VMEM((1, 2048), F32),
@@ -518,13 +564,15 @@
         dxn_zl=pltpu.VMEM((32, 2048), BF),
         dxn_tmp=pltpu.VMEM((32, 2048), BF),
         both_z=pltpu.VMEM((2, 64, 1280), BF),
-        other_z=pltpu.VMEM((64, 1280), BF),
-        gain_in=pltpu.VMEM((7, 8, 640), F32),
+        from_z=pltpu.VMEM((2, 2, 64, 1280), BF),
+        gain_quad=pltpu.VMEM((4, 8, 640), F32),
+        gain_y=pltpu.VMEM((4, 8, 640), F32),
+        gain_xz=pltpu.VMEM((8, 8, 640), F32),
         dxn2_sum=torus_buffers(),
         out_sum=torus_buffers(),
-        slices=[slice_buffers(n) for _, n, _ in ATT_SLICES],
-        send_sems=pltpu.SemaphoreType.DMA((N_COPIES,)),
-        recv_sems=pltpu.SemaphoreType.DMA((N_COPIES,)),
+        slices=[order_buffers(64, n) for _, n, _ in ATT_SLICES],
+        send_sems=pltpu.SemaphoreType.DMA((N_SENDS,)),
+        recv_sems=pltpu.SemaphoreType.DMA((N_GROUPS,)),
         sems=pltpu.SemaphoreType.DMA((N_LOCAL,)),
     )
 
@@ -547,36 +595,48 @@
     send_sems, recv_sems, sems = s.send_sems, s.recv_sems, s.sems
     me = Place()
     zh, y, x, c, zl, z = me.zh, me.y, me.x, me.c, me.zl, me.z
+    net = Net(send_sems, recv_sems)
+    att, ffn = s.att, s.ffn
+    rows = pl.ds(c * 64 + zl * 32, 32)
+
+
+    def piece(k):
+        return pl.ds(pl.multiple_of(k * 512 + c * 256, 256), 256)
+
+    def load(pairs):
+        started = []
+        for src, dst in pairs:
+            started.append(pltpu.make_async_copy(src, dst, sems.at[len(loads)]))
+            loads.append(started[-1])
+            started[-1].start()
+        return started
+
+    loads = []
+    own = att.at[zh, y, x]
+    wide = pl.ds(pl.multiple_of(zl * 512, 512), 512)
+    narrow = pl.ds(pl.multiple_of(zl * 128, 128), 128)
+    mine = zh * 4 + x
+    att_copies = load(
+        [
+            (s.wq.at[:, wide], own.at[:, pl.ds(0, 512)]),
+            (s.wk.at[:, narrow], own.at[:, pl.ds(512, 128)]),
+            (s.wv.at[:, narrow], own.at[:, pl.ds(640, 128)]),
+            (s.wo.at[:, wide], own.at[:, pl.ds(768, 512)]),
+        ]
+    )
+    (small_copy,) = load([(s.small, s.small_in)])
+    (cots_copy,) = load([(s.cot.at[rows], s.cots.at[z, x, c])])
+    ffn_copies = load(
+        [(w.at[:, piece(mine)], ffn.at[m, zh, y, x]) for m, w in enumerate((s.wg, s.wu, s.wd))]
+    )
+    other_copies = load([(s.tokens, s.tok), (s.cos, s.cos_in), (s.sin, s.sin_in)])
     greet(
         [me.step("x", 1), me.step("x", 2), me.step("x", -1)]
         + [me.step("y", 1), me.step("y", 2), me.step("y", -1)]
         + [me.step("z", 1), me.step("z", 2), me.step("z", -1)]
-        + [me.core()]
+        + [me.core(), me.at(c=1 - c, zl=1 - zl)]
         + [me.at(zh=1 - zh, x=lax.rem(x + k, 4)) for k in (1, 2, 3)]
     )
-    net = Net(send_sems, recv_sems)
-    att, ffn = s.att, s.ffn
-    rows = pl.ds(c * 64 + zl * 32, 32)
-
-
-    def piece(k):
-        return pl.ds(pl.multiple_of(k * 512 + c * 256, 256), 256)
-
-    own = att.at[zh, y, x]
-    wide = pl.ds(pl.multiple_of(zl * 512, 512), 512)
-    narrow = pl.ds(pl.multiple_of(zl * 128, 128), 128)
-    mine = zh * 4 + x
-    pairs = [
-        (s.wq.at[:, wide], own.at[:, pl.ds(0, 512)]),
-        (s.wk.at[:, narrow], own.at[:, pl.ds(512, 128)]),
-        (s.wv.at[:, narrow], own.at[:, pl.ds(640, 128)]),
-        (s.wo.at[:, wide], own.at[:, pl.ds(768, 512)]),
-    ] + [(w.at[:, piece(mine)], ffn.at[m, zh, y, x]) for m, w in enumerate((s.wg, s.wu, s.wd))]
-    copies = [pltpu.make_async_copy(a, b, sems.at[k]) for k, (a, b) in enumerate(pairs)]
-    for copy in copies:
-        copy.start()
-    s.cots[z, x, c] = s.cot[rows, :]
-    s.gains[zh, y, x] = s.small[...]
 
     def gather_attention():
         swap = net.send(own, own, me.zh_pair())
@@ -589,10 +649,14 @@
             block = att.at[1 - zh if part else zh, i, j]
             return block if half is None else block.at[:, halves[half]]
 
-        yield from cross_gather(net, me, "y", "x", view, late=swap)
+        def likes(half, n):
+            cols = slice(None) if half is None else halves[half]
+            return att.at[:, 0, pl.ds(0, n // 2), :, cols]
+
+        yield from cross_gather(net, me, "y", "x", view, likes, late=swap)
 
     def gather_ffn():
-        arrivals = []
+        arrivals = [net.group(), net.group()]
         for dz in (0, 1):
             for dx in range(4):
                 if dz == 0 and dx == 0:
@@ -600,33 +664,38 @@
                 tx = lax.rem(x + dx, 4)
                 tz = 1 - zh if dz else zh
                 for m, w in enumerate((s.wg, s.wu, s.wd)):
-                    arrivals.append(
-                        net.send(
-                            w.at[:, piece(tz * 4 + tx)],
-                            ffn.at[m, zh, y, x],
-                            me.at(zh=tz, x=tx),
-                        )
+                    net.send(
+                        w.at[:, piece(tz * 4 + tx)],
+                        ffn.at[m, zh, y, x],
+                        me.at(zh=tz, x=tx),
+                        arrivals[dz],
                     )
         yield
-        for copy in copies[4:]:
+        arrivals[0].wait(s.ffn_part.at[:, 0, 0, pl.ds(0, 3)])
+        arrivals[1].wait(s.ffn_part.at[:, 0, 0])
+        for copy in ffn_copies:
             copy.wait()
-        for copy in arrivals:
-            copy.wait_recv()
-        yield from ring_gather(net, me, "y", lambda i, p: ffn.at[:, p, i])
+        yield from ring_gather(
+            net, me, "y", lambda i, p: ffn.at[:, p, i], s.ffn_part.at[:, 0]
+        )
 
     def gather_gains():
-        gains = s.gains
-        steps = [
-            (gains.at[zh, y, x], me.zh_pair()),
-            (gains.at[:, y, x], me.at(x=x + 1 - 2 * lax.rem(x, 2))),
-            (gains.at[:, y, pl.ds(2 * lax.div(x, 2), 2)], me.step("x", 2)),
-            (gains.at[:, y], me.at(y=y + 1 - 2 * lax.rem(y, 2))),
-            (gains.at[:, pl.ds(2 * lax.div(y, 2), 2)], me.step("y", 2)),
-        ]
-        for block, device in steps:
-            copy = net.send(block, block, device)
-            yield
-            copy.wait_recv()
+        own_gain = s.gains.at[zh, y, x]
+        near, far = net.group(), net.group()
+        for k in range(4):
+            device = lax.rem(x + k, 4)
+            if k:
+                net.send(own_gain, own_gain, me.at(x=device), near)
+            net.send(own_gain, own_gain, me.at(zh=1 - zh, x=device), far)
+        yield
+        near.wait(s.gains.at[0, 0, pl.ds(0, 3)])
+        far.wait(s.gains.at[0, 0])
+        row = s.gains.at[:, y]
+        group = net.group()
+        for k in (1, -1, 2):
+            net.send(row, row, me.step("y", k), group)
+        yield
+        group.wait(s.gains.at[:, pl.ds(0, 3)])
 
     def gain_row(k):
         blocks = []
@@ -639,23 +708,28 @@
             blocks.append(total[k:k + 1, :])
         return jnp.concatenate(blocks, axis=1)
 
-    for copy in copies[:4]:
+    for copy in att_copies:
         copy.wait()
     attention = gather_attention()
+    gains = gather_gains()
+    weights = gather_ffn()
+    cots = torus_gather(net, me, s.cots, only=0)
     step(attention)
-    gains = gather_gains()
-    step(gains, attention)
-    weights = gather_ffn()
-    step(weights)
-    for _ in range(2):
-        step(gains, attention)
+    small_copy.wait()
+    small = s.small_in[...].astype(F32)
+    s.gains[zh, y, x] = jnp.where(lax.rem(x, 2) == 1, pltpu.roll(small, 64, 1), small).astype(BF)
+    step(gains, attention, attention, gains, attention)
+    cots_copy.wait()
+    step(cots, attention, weights, attention, cots)
     finish(gains)
-    t = s.tokens[...].astype(F32)
+    for copy in other_copies:
+        copy.wait()
+    t = s.tok[...].astype(F32)
     s.xn[...] = (t * rows_rms(t) * gain_row(0)).astype(BF)
+    step(attention, attention, cots, attention, attention, cots)
     finish(attention)
 
 
-    cots = torus_gather(net, me, s.cots)
     step(weights, cots)
     raw = nn(s.xn[...], att[:, :, :, :, 0:768].reshape(2048, 768))
     z_raw = raw[:, 0:640]
@@ -663,14 +737,14 @@
     v = raw[:, 640:768].astype(BF)
     s.v[...] = v
     step(cots)
-    both_gains = s.small[...].astype(F32)[2:3, :]
+    both_gains = small[2:3, :]
     turned = pltpu.roll(both_gains, 64, 1)
     low = lanes((1, 128)) < 64
     gain_q = jnp.where(low, both_gains, turned)
     gain_k = jnp.where(low, turned, both_gains)
     head_gain = jnp.concatenate([gain_q] * 4 + [gain_k], axis=1)
-    cos = jnp.concatenate([s.cos[...]] * 5, axis=1)
-    sin = jnp.concatenate([s.sin[...]] * 5, axis=1)
+    cos = jnp.concatenate([s.cos_in[...]] * 5, axis=1)
+    sin = jnp.concatenate([s.sin_in[...]] * 5, axis=1)
     n = z_raw * lax.rsqrt(head_mean(z_raw * z_raw) + EPS) * head_gain
     s.qk[...] = (n * cos + partner(n) * sin).astype(BF)
     step(cots)
@@ -697,17 +771,15 @@
     )
     step(quad, cots)
     finish(quad)
-    hidden = s.tokens[rows, :].astype(F32)
+    hidden = s.tok[rows, :].astype(F32)
     hidden = hidden + quad_total(me, s.branch, s.branch_core, s.branch_zl)
     s.hidden[...] = hidden
     s.xn2[z, x, c] = (hidden * rows_rms(hidden) * gain_row(1)).astype(BF)
     normed_net = Tagged(net)
     normed = torus_gather(normed_net, me, s.xn2)
-    step(normed, weights)
-    for _ in range(3):
-        step(normed, cots)
+    step(normed, normed, weights, normed)
     finish(cots)
-    step(normed)
+    step(normed, normed)
     finish(weights)
 
 
@@ -739,50 +811,54 @@
     dxn2 = torus_reduce(net, me, s.dxn2_part, swaps, s.dxn2_sum)
     step(dxn2)
 
-    def weight_grads(first, last):
-        def one(d, carry):
-            cols = pl.ds(pl.multiple_of(d * 256, 256), 256)
-            at = (lax.div(d, 4), lax.rem(d, 4))
+    def weight_grads(k):
+        yk = lax.rem(y + k, 4)
+
+        def one(p, carry):
+            cols = pl.ds(pl.multiple_of((p * 4 + yk) * 256, 256), 256)
             xd = s.xn2[:, :, :, :, cols].reshape(1024, 256)
             dyd = s.cots[:, :, :, :, cols].reshape(1024, 256)
             for m, left, right in ((0, xd, s.dg), (1, xd, s.du), (2, dyd, s.ab)):
                 grad = tn(left, right[...].reshape(1024, 256))
-                s.ffn_part[(m,) + at] = grad.astype(BF).reshape(4, 64, 256)
+                s.ffn_part[m, p, yk] = grad.astype(BF).reshape(4, 64, 256)
             return carry
 
-        lax.fori_loop(first, last, one, 0)
+        lax.fori_loop(0, 2, one, 0)
 
     def reduce_ffn_grads():
-        part, mid, grads = s.ffn_part, s.ffn_mid, s.ffn_grads
-        yield from ring_reduce(
-            net, me, "y", lambda i, p: part.at[:, p, i],
-            s.ffn_far, s.ffn_near, lambda p: mid.at[p],
-        )
-        arrivals = []
-        for dz in (0, 1):
-            for dx in range(4):
-                if dz == 0 and dx == 0:
-                    continue
-                tx = lax.rem(x + dx, 4)
-                tz = 1 - zh if dz else zh
-                arrivals.append(
-                    net.send(mid.at[tz, :, tx], grads.at[:, mine, c], me.at(zh=tz, x=tx))
-                )
-        keep = pltpu.make_async_copy(mid.at[zh, :, x], grads.at[:, mine, c], sems.at[7])
-        keep.start()
-        yield
+        part, grads = s.ffn_part, s.ffn_grads
+        arrivals = [net.group(), net.group()]
+        dst = grads.at[:, mine, c]
+        keep = pltpu.make_async_copy(s.ffn_mid.at[0, zh], dst, sems.at[N_LOCAL - 1])
+
+        def block(k):
+            xk = lax.rem(x + k, 4)
+            far, near, mid = (ref.at[k] for ref in (s.ffn_far, s.ffn_near, s.ffn_mid))
+            yield from ring_reduce(
+                net, me, "y", lambda i, p: part.at[:, p, i, xk], far, near, lambda p: mid.at[p]
+            )
+            if k:
+                net.send(mid.at[zh], dst, me.at(x=xk), arrivals[0])
+            else:
+                keep.start()
+            net.send(mid.at[1 - zh], dst, me.at(zh=1 - zh, x=xk), arrivals[1])
+
+        yield from together(*[block(k) for k in (2, 1, 3, 0)])
         keep.wait()
-        for copy in arrivals:
-            copy.wait_recv()
+        arrivals[0].wait(s.ffn_part.at[:, 0, 0, pl.ds(0, 3)])
+        arrivals[1].wait(s.ffn_part.at[:, 0, 0])
         swap = net.send(grads.at[:, :, c], grads.at[:, :, c], me.core())
         yield
         swap.wait_recv()
 
-    weight_grads(0, 4)
+    ffn_grads = reduce_ffn_grads()
+    weight_grads(2)
+    step(ffn_grads)
+    weight_grads(1)
+    weight_grads(3)
+    step(ffn_grads, dxn2, dxn2)
+    weight_grads(0)
     step(dxn2)
-    weight_grads(4, 8)
-    ffn_grads = reduce_ffn_grads()
-    step(ffn_grads, dxn2)
     swaps = []
     normed_net.drain()
     for k in range(4):
@@ -791,7 +867,6 @@
         swaps.append(net.send(s.xn2.at[k, :, 1 - c], s.out_sum.both.at[k], me.core()))
         if k % 2 == 1:
             step(dxn2)
-    step(ffn_grads)
     finish(dxn2)
     hidden = s.hidden[...]
     r = rows_rms(hidden)
@@ -799,7 +874,7 @@
     d = s.dxn2_sum.total[...]
     s.ffn_gain_grad[...] = jnp.sum(d * hat, axis=0, keepdims=True)
     scaled = d * gain_row(1)
-    dh = s.cot[rows, :].astype(F32)
+    dh = s.cots[z, x, c].astype(F32)
     dh = dh + r * (scaled - hat * jnp.mean(scaled * hat, axis=-1, keepdims=True))
     s.dh[...] = dh
     s.dhb[rows, :] = dh.astype(BF)
@@ -812,37 +887,35 @@
         yield from quad_gather(net, me, s.out)
 
     output = finish_output()
-    step(spread)
-    step(output)
+    step(spread, output)
     finish(spread)
 
 
     def reduce_att_grads(k):
         start, width, order = ATT_SLICES[k]
         cols = pl.ds(start, width)
-        part, mid, both_z = s.att_part, s.slices[k].mid, s.both_z
-        one, two = order
-        if one == "y":
-            view = lambda i, p: part.at[p, i, :, :, cols]
-        else:
-            view = lambda i, p: part.at[p, :, i, :, cols]
-        yield from ring_reduce(
-            net, me, one, view, s.slices[k].far, s.slices[k].near, lambda p: mid.at[p]
+        part, both_z = s.att_part, s.both_z
+
+        def view(p, i, j):
+            yi, xi = (i, j) if order == "yx" else (j, i)
+            return part.at[p, yi, xi, :, cols]
+
+        yield from order_reduce(
+            net, me, order[0], order[1], view, s.slices[k], lambda p: both_z.at[p, :, cols]
         )
+        arrivals = net.group()
+        mine_z = both_z.at[zh, :, cols]
+        theirs = both_z.at[1 - zh, :, cols]
+        net.send(theirs, s.from_z.at[zl, 1, :, cols], me.at(zh=1 - zh), arrivals)
+        net.send(theirs, s.from_z.at[zl, 1, :, cols], me.at(zh=1 - zh, zl=1 - zl), arrivals)
+        net.send(mine_z, s.from_z.at[zl, 0, :, cols], me.at(zl=1 - zl), arrivals)
         yield
-        yield from ring_reduce(
-            net, me, two, lambda i, p: mid.at[p, i],
-            s.slices[k].far2, s.slices[k].near2, lambda p: both_z.at[p, :, cols],
+        arrivals.wait(s.slices[k].last.at[:, 0])
+        add_refs(s.att_grads.at[zl, :, cols], [mine_z, s.from_z.at[zl, 1, :, cols]])
+        add_refs(
+            s.att_grads.at[1 - zl, :, cols],
+            [s.from_z.at[1 - zl, 0, :, cols], s.from_z.at[1 - zl, 1, :, cols]],
         )
-        other = s.other_z.at[:, cols]
-        swap = net.send(both_z.at[1 - zh, :, cols], other, me.zh_pair())
-        yield
-        swap.wait_recv()
-        done = s.att_grads.at[zl, :, cols]
-        add_refs(done, [both_z.at[zh, :, cols], other])
-        swap = net.send(done, done, me.zl_pair())
-        yield
-        swap.wait_recv()
 
     dhb = s.dhb[...]
     grad = tn(dhb, s.o[...]).astype(BF)
@@ -850,7 +923,7 @@
     slices = [reduce_att_grads(k) for k in range(4)]
     step(slices[2], slices[3])
     do = nn(dhb, att[:, :, :, :, 768:1280].reshape(2048, 512)).astype(BF)
-    step(output, ffn_grads)
+    step(output)
     v = s.v[...]
     k = s.qk[:, 512:640]
     k_at = {True: k, False: swap_halves(k)}
@@ -889,19 +962,19 @@
     dz = dn * head_gain
     dz = r * (dz - zhat * head_mean(dz * zhat))
     low_grads = jnp.concatenate([dz.astype(BF), dvb], axis=1)
+    grad = tn(s.xn[...], low_grads).astype(BF)
+    s.att_part[:, :, :, :, 0:768] = grad.reshape(2, 4, 4, 64, 768)
+    step(slices[0], slices[1])
     back = nt(low_grads, att[:, :, :, :, 0:768].reshape(2048, 768))
     s.dxn_part[...] = back.astype(BF)
     quad = quad_reduce(net, me, s.dxn_part, s.dxn_core, s.dxn_zl, s.dxn_tmp)
-    step(quad, output, ffn_grads)
-    grad = tn(s.xn[...], low_grads).astype(BF)
-    s.att_part[:, :, :, :, 0:768] = grad.reshape(2, 4, 4, 64, 768)
-    step(slices[0], slices[1])
+    step(quad, output)
 
 
     def tokens_and_gains():
         yield from quad
         d = quad_total(me, s.dxn_part, s.dxn_core, s.dxn_zl)
-        t = s.tokens[rows, :].astype(F32)
+        t = s.tok[rows, :].astype(F32)
         r = rows_rms(t)
         hat = t * r
         scaled = d * gain_row(0)
@@ -919,25 +992,33 @@
         sums[:, 512:640] = jnp.where(row == 0, head_grad, 0.0)
         spread = quad_gather(net, me, s.dx)
         step(spread)
-        devices = [
-            me.core(),
-            me.zl_pair(),
-            me.zh_pair(),
-            me.at(x=x + 1 - 2 * lax.rem(x, 2)),
-            me.step("x", 2),
-            me.at(y=y + 1 - 2 * lax.rem(y, 2)),
-            me.step("y", 2),
-        ]
-        for k, device in enumerate(devices):
-            copy = net.send(sums, s.gain_in.at[k], device)
+
+        def total(buf, own, devices):
+            group = net.group()
+            for device in devices:
+                net.send(buf.at[own], buf.at[own], device, group)
             yield
-            copy.wait_recv()
-            net.wait_send(copy)
-            sums[...] = sums[...] + s.gain_in[k]
+            group.wait(buf.at[pl.ds(0, len(devices))])
             step(spread)
+            sums[...] = sum(buf[k] for k in range(1, len(devices) + 1)) + buf[0]
+
+        s.gain_quad[c * 2 + zl] = sums[...]
+        yield from total(
+            s.gain_quad, c * 2 + zl, [me.core(), me.zl_pair(), me.at(c=1 - c, zl=1 - zl)]
+        )
+        s.gain_y[y] = sums[...]
+        yield from total(s.gain_y, y, [me.step("y", k) for k in (1, 2, 3)])
+        s.gain_xz[mine] = sums[...]
+        yield from total(
+            s.gain_xz,
+            mine,
+            [me.step("x", k) for k in (1, 2, 3)]
+            + [me.at(zh=1 - zh, x=lax.rem(x + k, 4)) for k in range(4)],
+        )
+        finish(spread)
 
     rest = tokens_and_gains()
-    finish(rest, slices[2], slices[3], slices[0], slices[1], output, ffn_grads)
+    finish(rest, slices[2], slices[3], output, ffn_grads, slices[0], slices[1])
     net.drain()
 
 
@@ -1024,13 +1105,9 @@
     w_gate, w_up, w_down, cotangent,
 ):
     cos, sin = (jnp.asarray(t) for t in rotary_tables())
-    dp = lax.axis_index("dp")
-    odd = lax.rem(dp, 2)
-    lane = lax.broadcasted_iota(jnp.int32, (2, 128), 1)
-    two = jnp.stack([gain_attn, gain_ffn])
-    placed = jnp.where(lax.div(lane, 64) == odd, jnp.concatenate([two, two], axis=1), 0)
-    heads = jnp.concatenate([gain_query, gain_key]).reshape(1, 128)
-    small = jnp.concatenate([placed.astype(BF), heads, jnp.zeros((13, 128), BF)], axis=0)
+    rows = [jnp.pad(v, (0, 64)).reshape(1, 128) for v in (gain_attn, gain_ffn)]
+    rows.append(jnp.concatenate([gain_query, gain_key]).reshape(1, 128))
+    small = jnp.pad(jnp.concatenate(rows, axis=0), ((0, 13), (0, 0)))
     r = everything(
         tokens=tokens, cot=cotangent, small=small, cos=cos, sin=sin,
         wq=w_query, wk=w_key, wv=w_value, wo=w_out, wg=w_gate, wu=w_up, wd=w_down,

time: 210 us -> 187 us (0.89)
  Pallas kernels: 207 us -> 184 us
    pallas_call x1, Pallas kernels: 202 us -> 179 us  [everything(): pl.pallas_call(kernel, out_shape=tuple(out_shapes), in_specs=in_specs, ou...]
where the time goes in v3:
time: 187 us; the launch traced here: 186 us
  Pallas kernels  184 us (98%)
    pallas_call x1, Pallas kernels, everything(): pl.pallas_call(kernel, out_shape=tuple(out_shapes), in_specs=in_specs, ou...  179 us
    pallas_call x1, Pallas kernels, finished(): pl.pallas_call(finish_kernel, grid=(4,), out_shape=(jax.ShapeDtypeStruct(...  4.71 us

profile of v3, /device:TPU:0, one launch (start us, length us, event | category | flops | bytes accessed | tf_op | source)
XLA Modules:
  0.0 186.4 jit_solution(5777095792530497465)
XLA Ops:
  0.6 0.7 pad_bitcast_fusion.1
  1.3 0.8 maximum_bitcast_fusion
  2.1 0.6 fusion.4.refs_3_
  2.7 178.9 %everything.1 = (bf16[2,64,1280]{2,1,0:T(8,128)(2,1)}, bf16[128,2048]{1,0:T(8,128)(2,1)}, bf16[3,8,2,64,256]{4,3,2,1,0:T(8,128)(2,1)}, f32[8,640]{1,0:T(8,128)}, bf16[128,2048]{1,0:T(8,128)(2,1)}) custom-call(f32[128,128]{1,0:T(8,128)} %constant.7.clone.refs_0_, bf16[128,2048]{1,0:T(8,128)(2,1)} %refs_1_.1, f32[128,128]{1,0:T(8,128)} %constant.8.clone.refs_2_, ...), custom_call_target="tpu_custom_call" | custom-call | tf_op jit(solution)/shard_map/everything/pallas_call | solution.py:1028
  181.5 4.7 %finished.1 = (bf16[128,2048]{1,0:T(8,128)(2,1)}, f32[128,2048]{1,0:T(8,128)}, f32[64,1024]{1,0:T(8,128)}, f32[64,256]{1,0:T(8,128)}, f32[64,256]{1,0:T(8,128)},...) custom-call(bf16[128,2048]{1,0:T(8,128)(2,1)} %get-tuple-element.31., ...), custom_call_target="tpu_custom_call" | custom-call | tf_op jit(solution)/shard_map/finished/pallas_call | solution.py:1079

commit v4 on v3

--- a/solution.py
+++ b/solution.py
@@ -14,8 +14,7 @@
 EPS = 1e-05
 THETA = 1000000.0
 VMEM_BYTES = 62 << 20
-ATT_GATHER_SPLIT = 896
-ATT_SLICES = ((0, 384, "yx"), (384, 384, "xy"), (768, 256, "yx"), (1024, 256, "xy"))
+ATT_SLICES = ((0, 384), (384, 256))
 
 
 def nn(a, b):
@@ -38,6 +37,7 @@
         self.zh = lax.div(dp, 16)
         self.y = lax.rem(lax.div(dp, 4), 4)
         self.x = lax.rem(dp, 4)
+        self.odd = lax.rem(self.y, 2)
         self.z = self.zh * 2 + self.zl
 
     def at(self, zh=None, y=None, x=None, c=None, zl=None):
@@ -59,6 +59,9 @@
 
     def zl_pair(self):
         return self.at(zl=1 - self.zl)
+
+    def y_pair(self):
+        return self.at(y=self.y + 1 - 2 * self.odd)
 
     def zh_pair(self):
         return self.at(zh=1 - self.zh)
@@ -328,7 +331,7 @@
                 arrived(final)
 
 
-def order_reduce(net, place, one, two, view, s, out):
+def order_reduce(net, place, one, two, view, s, out, other_out=None):
     ring = [lax.rem(place.ring(one) + k, 4) for k in range(4)]
     other = [lax.rem(place.ring(two) + k, 4) for k in range(4)]
     up, down = place.step(one, 1), place.step(one, -1)
@@ -364,7 +367,11 @@
             yield
     others.wait(s.last)
     for p in (0, 1):
-        add_refs(out(p), [s.mid.at[0, p]] + [s.last.at[k, p] for k in range(3)])
+        if other_out is None:
+            add_refs(out(p), [s.mid.at[0, p]] + [s.last.at[k, p] for k in range(3)])
+        else:
+            add_refs(out(p), [s.mid.at[0, p], s.last.at[1, p]])
+            add_refs(other_out(p), [s.last.at[0, p], s.last.at[2, p]])
 
 
 def order_buffers(rows, columns):
@@ -407,25 +414,26 @@
     )
 
 
-def torus_reduce(net, place, src, swaps, s):
-    c = place.c
-    for k, swap in enumerate(swaps):
-        swap.wait_recv()
-        add_refs(s.both.at[k], [s.both.at[k], src.at[k, :, c]])
-
-    def part_of(half, part):
-        return pl.ds(half * 16, 16), pl.ds(part * 1024, 1024)
-
-    yield from together(
-        order_reduce(
-            net, place, "z", "x", lambda p, i, j: s.both.at[(i, j) + part_of(0, p)],
-            s.halves[0], lambda p: s.total.at[part_of(0, p)],
-        ),
-        order_reduce(
-            net, place, "x", "z", lambda p, i, j: s.both.at[(j, i) + part_of(1, p)],
-            s.halves[1], lambda p: s.total.at[part_of(1, p)],
-        ),
-    )
+def core_sum(place, src, swap, s, k):
+    swap.wait_recv()
+    add_refs(s.both.at[k], [s.both.at[k], src.at[k, :, place.c]])
+
+
+def torus_reduce(net, place, s, orders):
+    def half(k):
+        def at(part):
+            return pl.ds(k * 16, 16), pl.ds(part * 1024, 1024)
+
+        def view(p, i, j):
+            zi, xi = (i, j) if orders[k] == "z" else (j, i)
+            return s.both.at[(zi, xi) + at(p)]
+
+        second = "x" if orders[k] == "z" else "z"
+        return order_reduce(
+            net, place, orders[k], second, view, s.halves[k], lambda p: s.total.at[at(p)]
+        )
+
+    yield from together(half(0), half(1))
 
 
 def quad_gather(net, place, buf):
@@ -440,23 +448,75 @@
     two.wait_recv()
 
 
-def quad_reduce(net, place, src, from_core, from_zl, tmp):
+def oct_reduce(net, place, src, b):
+    c, zl, q = place.c, place.zl, place.odd
+    one = net.send(src.at[:, pl.ds((1 - c) * 64, 64)], b.core, place.core())
+    yield
+    one.wait_recv()
+    b.for_y[...] = (
+        src[1 - q, pl.ds(c * 64, 64), :].astype(F32) + b.core[1 - q].astype(F32)
+    ).astype(BF)
+    far, near = pl.ds((1 - zl) * 32, 32), pl.ds(zl * 32, 32)
+    two = [net.send(b.for_y.at[r], b.y.at[r], place.y_pair()) for r in (far, near)]
+    yield
+    two[0].wait_recv()
+    theirs = src[q, pl.ds(c * 64 + (1 - zl) * 32, 32), :].astype(F32)
+    theirs = theirs + b.core[q, far, :].astype(F32) + b.y[far, :].astype(F32)
+    b.for_zl[...] = theirs.astype(BF)
+    three = net.send(b.for_zl, b.zl, place.zl_pair())
+    yield
+    two[1].wait_recv()
+    three.wait_recv()
+
+
+def oct_total(place, src, b):
+    c, zl, q = place.c, place.zl, place.odd
+    near = pl.ds(zl * 32, 32)
+    total = src[q, pl.ds(c * 64 + zl * 32, 32), :].astype(F32) + b.core[q, near, :].astype(F32)
+    return total + b.y[near, :].astype(F32) + b.zl[...].astype(F32)
+
+
+def oct_buffers():
+    return dict(
+        core=pltpu.VMEM((2, 64, 2048), BF),
+        for_y=pltpu.VMEM((64, 2048), BF),
+        y=pltpu.VMEM((64, 2048), BF),
+        for_zl=pltpu.VMEM((32, 2048), BF),
+        zl=pltpu.VMEM((32, 2048), BF),
+    )
+
+
+def quad_gather(net, place, buf):
     c, zl = place.c, place.zl
-    one = net.send(src.at[pl.ds((1 - c) * 64, 64)], from_core, place.core())
+    own = buf.at[pl.ds(c * 64 + zl * 32, 32)]
+    one = net.send(own, own, place.zl_pair())
     yield
     one.wait_recv()
-    theirs = src[pl.ds(c * 64 + (1 - zl) * 32, 32), :].astype(F32)
-    tmp[...] = (theirs + from_core[pl.ds((1 - zl) * 32, 32), :].astype(F32)).astype(BF)
-    two = net.send(tmp, from_zl, place.zl_pair())
+    half = buf.at[pl.ds(c * 64, 64)]
+    two = net.send(half, half, place.core())
     yield
     two.wait_recv()
 
 
-def quad_total(place, src, from_core, from_zl):
-    c, zl = place.c, place.zl
-    mine = src[pl.ds(c * 64 + zl * 32, 32), :].astype(F32)
-    mine = mine + from_core[pl.ds(zl * 32, 32), :].astype(F32)
-    return mine + from_zl[...].astype(F32)
+def oct_gather(net, place, buf):
+    c, zl, q = place.c, place.zl, place.odd
+    own = buf.at[q, pl.ds(c * 64 + zl * 32, 32)]
+    from_zl = net.send(own, own, place.zl_pair())
+    from_y = [net.send(own, own, place.y_pair())]
+    yield
+    from_zl.wait_recv()
+    other = buf.at[q, pl.ds(c * 64 + (1 - zl) * 32, 32)]
+    from_y.append(net.send(other, other, place.y_pair()))
+    half = buf.at[q, pl.ds(c * 64, 64)]
+    from_core = [net.send(half, half, place.core())]
+    yield
+    for copy in from_y:
+        copy.wait_recv()
+    half = buf.at[1 - q, pl.ds(c * 64, 64)]
+    from_core.append(net.send(half, half, place.core()))
+    yield
+    for copy in from_core:
+        copy.wait_recv()
 
 
 def sem_scratch(n):
@@ -501,9 +561,9 @@
     return lax.rsqrt(jnp.mean(v * v, axis=-1, keepdims=True) + EPS)
 
 
-N_SENDS = 64
-N_GROUPS = 190
-N_LOCAL = 13
+N_SENDS = 48
+N_GROUPS = 147
+N_LOCAL = 17
 
 
 def input_plan():
@@ -517,7 +577,7 @@
     return dict(
         out=jax.ShapeDtypeStruct((128, 2048), BF),
         dx=jax.ShapeDtypeStruct((128, 2048), BF),
-        att_grads=jax.ShapeDtypeStruct((2, 64, 1280), BF),
+        att_grads=jax.ShapeDtypeStruct((2, 2, 64, 640), BF),
         ffn_grads=jax.ShapeDtypeStruct((3, 8, 2, 64, 256), BF),
         gain_sums=jax.ShapeDtypeStruct((8, 640), F32),
     )
@@ -525,26 +585,26 @@
 
 def scratch_plan():
     return dict(
-        tok=pltpu.VMEM((128, 2048), BF),
+        tok=pltpu.VMEM((2, 128, 2048), BF),
+        kv_in=pltpu.VMEM((2, 64, 128), BF),
+        shard=pltpu.VMEM((2, 2, 64, 640), BF),
         small_in=pltpu.VMEM((16, 128), BF),
         cos_in=pltpu.VMEM((128, 128), F32),
         sin_in=pltpu.VMEM((128, 128), F32),
-        att=pltpu.VMEM((2, 4, 4, 64, 1280), BF),
+        att=pltpu.VMEM((2, 4, 4, 64, 640), BF),
         gains=pltpu.VMEM((2, 4, 4, 16, 128), BF),
         ffn=pltpu.VMEM((3, 2, 4, 4, 64, 256), BF),
         cots=pltpu.VMEM((4, 4, 2, 32, 2048), BF),
         xn2=pltpu.VMEM((4, 4, 2, 32, 2048), BF),
-        xn=pltpu.VMEM((128, 2048), BF),
-        z=pltpu.VMEM((128, 640), F32),
-        qk=pltpu.VMEM((128, 640), BF),
-        v=pltpu.VMEM((128, 128), BF),
+        xn=pltpu.VMEM((256, 2048), BF),
+        z=pltpu.VMEM((256, 384), F32),
+        qk=pltpu.VMEM((256, 384), BF),
         p=pltpu.VMEM((8, 128, 128), F32),
-        o=pltpu.VMEM((128, 512), BF),
-        branch=pltpu.VMEM((128, 2048), BF),
+        o=pltpu.VMEM((256, 256), BF),
+        branch=pltpu.VMEM((2, 128, 2048), BF),
+        branch_sum=oct_buffers(),
+        dxn_sum=oct_buffers(),
         hidden=pltpu.VMEM((32, 2048), F32),
-        branch_core=pltpu.VMEM((64, 2048), BF),
-        branch_zl=pltpu.VMEM((32, 2048), BF),
-        branch_tmp=pltpu.VMEM((32, 2048), BF),
         da=pltpu.VMEM((4, 256, 256), F32),
         ab=pltpu.VMEM((4, 256, 256), BF),
         dg=pltpu.VMEM((4, 256, 256), BF),
@@ -555,22 +615,19 @@
         ffn_near=pltpu.VMEM((4, 4, 3, 64, 256), BF),
         ffn_mid=pltpu.VMEM((4, 2, 3, 64, 256), BF),
         dh=pltpu.VMEM((32, 2048), F32),
-        dhb=pltpu.VMEM((128, 2048), BF),
+        dhb=pltpu.VMEM((2, 128, 2048), BF),
         ffn_gain_grad=pltpu.VMEM((1, 2048), F32),
-        d_heads=pltpu.VMEM((128, 640), F32),
-        att_part=pltpu.VMEM((2, 4, 4, 64, 1280), BF),
-        dxn_part=pltpu.VMEM((128, 2048), BF),
-        dxn_core=pltpu.VMEM((64, 2048), BF),
-        dxn_zl=pltpu.VMEM((32, 2048), BF),
-        dxn_tmp=pltpu.VMEM((32, 2048), BF),
-        both_z=pltpu.VMEM((2, 64, 1280), BF),
-        from_z=pltpu.VMEM((2, 2, 64, 1280), BF),
+        d_heads=pltpu.VMEM((256, 384), F32),
+        att_part=pltpu.VMEM((2, 4, 4, 64, 640), BF),
+        dxn_part=pltpu.VMEM((2, 128, 2048), BF),
+        both_z=pltpu.VMEM((2, 2, 64, 640), BF),
+        from_z=pltpu.VMEM((2, 2, 2, 64, 640), BF),
         gain_quad=pltpu.VMEM((4, 8, 640), F32),
         gain_y=pltpu.VMEM((4, 8, 640), F32),
         gain_xz=pltpu.VMEM((8, 8, 640), F32),
         dxn2_sum=torus_buffers(),
         out_sum=torus_buffers(),
-        slices=[order_buffers(64, n) for _, n, _ in ATT_SLICES],
+        slices=[order_buffers(64, n) for _, n in ATT_SLICES],
         send_sems=pltpu.SemaphoreType.DMA((N_SENDS,)),
         recv_sems=pltpu.SemaphoreType.DMA((N_GROUPS,)),
         sems=pltpu.SemaphoreType.DMA((N_LOCAL,)),
@@ -594,7 +651,7 @@
         vars(s).update(vars(named(part)))
     send_sems, recv_sems, sems = s.send_sems, s.recv_sems, s.sems
     me = Place()
-    zh, y, x, c, zl, z = me.zh, me.y, me.x, me.c, me.zl, me.z
+    zh, y, x, c, zl, z, odd = me.zh, me.y, me.x, me.c, me.zl, me.z, me.odd
     net = Net(send_sems, recv_sems)
     att, ffn = s.att, s.ffn
     rows = pl.ds(c * 64 + zl * 32, 32)
@@ -612,24 +669,25 @@
         return started
 
     loads = []
-    own = att.at[zh, y, x]
-    wide = pl.ds(pl.multiple_of(zl * 512, 512), 512)
     narrow = pl.ds(pl.multiple_of(zl * 128, 128), 128)
     mine = zh * 4 + x
-    att_copies = load(
-        [
-            (s.wq.at[:, wide], own.at[:, pl.ds(0, 512)]),
-            (s.wk.at[:, narrow], own.at[:, pl.ds(512, 128)]),
-            (s.wv.at[:, narrow], own.at[:, pl.ds(640, 128)]),
-            (s.wo.at[:, wide], own.at[:, pl.ds(768, 512)]),
-        ]
-    )
+    att_copies = load([(w.at[:, narrow], s.kv_in.at[k]) for k, w in enumerate((s.wk, s.wv))])
+    for parity in range(2):
+        wide = pl.ds(pl.multiple_of(zl * 512 + parity * 256, 256), 256)
+        block = s.shard.at[0, parity]
+        att_copies += load(
+            [
+                (s.wq.at[:, wide], block.at[:, pl.ds(0, 256)]),
+                (s.wo.at[:, wide], block.at[:, pl.ds(384, 256)]),
+            ]
+        )
     (small_copy,) = load([(s.small, s.small_in)])
     (cots_copy,) = load([(s.cot.at[rows], s.cots.at[z, x, c])])
     ffn_copies = load(
         [(w.at[:, piece(mine)], ffn.at[m, zh, y, x]) for m, w in enumerate((s.wg, s.wu, s.wd))]
     )
-    other_copies = load([(s.tokens, s.tok), (s.cos, s.cos_in), (s.sin, s.sin_in)])
+    (tok_copy,) = load([(s.tokens, s.tok.at[odd])])
+    other_copies = load([(s.cos, s.cos_in), (s.sin, s.sin_in)])
     greet(
         [me.step("x", 1), me.step("x", 2), me.step("x", -1)]
         + [me.step("y", 1), me.step("y", 2), me.step("y", -1)]
@@ -639,21 +697,62 @@
     )
 
     def gather_attention():
-        swap = net.send(own, own, me.zh_pair())
-        halves = (
-            pl.ds(0, ATT_GATHER_SPLIT),
-            pl.ds(ATT_GATHER_SPLIT, 1280 - ATT_GATHER_SPLIT),
-        )
-
-        def view(part, i, j, half):
-            block = att.at[1 - zh if part else zh, i, j]
-            return block if half is None else block.at[:, halves[half]]
-
-        def likes(half, n):
-            cols = slice(None) if half is None else halves[half]
-            return att.at[:, 0, pl.ds(0, n // 2), :, cols]
-
-        yield from cross_gather(net, me, "y", "x", view, likes, late=swap)
+        shard = s.shard
+
+        def plane(p):
+            return 1 - zh if p else zh
+
+        def blocks(n):
+            return att.at[0, 0, pl.ds(0, n)]
+
+        rings = {}
+        last = net.group()
+
+        def set_off(p, k):
+            block = att.at[plane(p), lax.rem(y + k, 4), x]
+            rings[p, k] = net.group()
+            net.send(block, block, me.step("x", 1), rings[p, k])
+            net.send(block, block, me.step("x", -1), rings[p, k])
+
+        def along_y(p):
+            group = net.group()
+            for k in (1, 3, 2):
+                parity = odd if k == 2 else 1 - odd
+                dst = att.at[plane(p), y, x]
+                net.send(shard.at[p, parity], dst, me.step("y", k), group)
+            s.att[plane(p), y, x] = shard[p, odd]
+            set_off(p, 0)
+            return group
+
+        swap = net.send(shard.at[0], shard.at[1], me.zh_pair())
+        groups = [along_y(0)]
+        yield
+        swap.wait_recv()
+        groups.append(along_y(1))
+        yield
+        for p in (0, 1):
+            groups[p].wait(blocks(3))
+            for k in (1, 3, 2):
+                set_off(p, k)
+            yield
+        for k in (0, 1, 3, 2):
+            for p in (0, 1):
+                rings[p, k].wait(blocks(2))
+                by = 1 if p else 3
+                block = att.at[plane(p), lax.rem(y + k, 4), lax.rem(x + by, 4)]
+                net.send(block, block, me.step("x", -1 if p else 1), last)
+            yield
+        last.wait(att.at[:, 0])
+
+    def gather_tokens():
+        half = s.tok.at[odd, pl.ds(c * 64, 64)]
+        copy = net.send(half, half, me.y_pair())
+        yield
+        copy.wait_recv()
+        half = s.tok.at[1 - odd, pl.ds(c * 64, 64)]
+        copy = net.send(half, half, me.core())
+        yield
+        copy.wait_recv()
 
     def gather_ffn():
         arrivals = [net.group(), net.group()]
@@ -710,77 +809,83 @@
 
     for copy in att_copies:
         copy.wait()
+    key, value = s.kv_in[0], s.kv_in[1]
+    low_half = lanes((64, 128)) < 64
+    s.shard[0, 0, :, 256:384] = jnp.where(low_half, key, swap_halves(value))
+    s.shard[0, 1, :, 256:384] = jnp.where(low_half, swap_halves(key), value)
     attention = gather_attention()
     gains = gather_gains()
     weights = gather_ffn()
     cots = torus_gather(net, me, s.cots, only=0)
+    pair_tokens = gather_tokens()
     step(attention)
     small_copy.wait()
     small = s.small_in[...].astype(F32)
     s.gains[zh, y, x] = jnp.where(lax.rem(x, 2) == 1, pltpu.roll(small, 64, 1), small).astype(BF)
-    step(gains, attention, attention, gains, attention)
-    cots_copy.wait()
-    step(cots, attention, weights, attention, cots)
+    step(gains, weights, attention, attention, gains, attention)
+    tok_copy.wait()
+    step(pair_tokens, attention)
     finish(gains)
     for copy in other_copies:
         copy.wait()
-    t = s.tok[...].astype(F32)
+    step(pair_tokens, attention, weights)
+    cots_copy.wait()
+    step(attention, cots)
+    finish(pair_tokens)
+    t = s.tok[...].reshape(256, 2048).astype(F32)
     s.xn[...] = (t * rows_rms(t) * gain_row(0)).astype(BF)
-    step(attention, attention, cots, attention, attention, cots)
+    step(attention, cots)
     finish(attention)
 
 
+    step(cots)
+    raw = nn(s.xn[...], att[:, :, :, :, 0:384].reshape(2048, 384))
+    s.z[...] = raw
     step(weights, cots)
-    raw = nn(s.xn[...], att[:, :, :, :, 0:768].reshape(2048, 768))
-    z_raw = raw[:, 0:640]
-    s.z[...] = z_raw
-    v = raw[:, 640:768].astype(BF)
-    s.v[...] = v
-    step(cots)
     both_gains = small[2:3, :]
     turned = pltpu.roll(both_gains, 64, 1)
     low = lanes((1, 128)) < 64
     gain_q = jnp.where(low, both_gains, turned)
-    gain_k = jnp.where(low, turned, both_gains)
-    head_gain = jnp.concatenate([gain_q] * 4 + [gain_k], axis=1)
-    cos = jnp.concatenate([s.cos_in[...]] * 5, axis=1)
-    sin = jnp.concatenate([s.sin_in[...]] * 5, axis=1)
-    n = z_raw * lax.rsqrt(head_mean(z_raw * z_raw) + EPS) * head_gain
-    s.qk[...] = (n * cos + partner(n) * sin).astype(BF)
+    head_gain = jnp.concatenate([gain_q, gain_q, turned], axis=1)
+    cos, sin = (
+        jnp.concatenate([jnp.concatenate([ref[...]] * 3, axis=1)] * 2, axis=0)
+        for ref in (s.cos_in, s.sin_in)
+    )
+    is_value = lanes((256, 384)) >= 320
+    n = raw * lax.rsqrt(head_mean(raw * raw) + EPS) * head_gain
+    s.qk[...] = jnp.where(is_value, raw, n * cos + partner(n) * sin).astype(BF)
     step(cots)
-    k = s.qk[:, 512:640]
-    k_at = {True: k, False: swap_halves(k)}
-    v_at = {True: v, False: swap_halves(v)}
     causal = lax.broadcasted_iota(jnp.int32, (128, 128), 0) >= lanes((128, 128))
-    for block in range(4):
-        out = None
-        for side in range(2):
-            h = 2 * block + side
-            same = side == h // 4
-            q = half_of(s.qk[:, block * 128:(block + 1) * 128], side)
-            score = jnp.where(causal, nt(q, k_at[same]) * 0.125, -1e30)
-            e = jnp.exp(score - jnp.max(score, axis=-1, keepdims=True))
-            p = e / jnp.sum(e, axis=-1, keepdims=True)
-            s.p[h] = p
-            part = nn(p.astype(BF), half_of(v_at[same], side))
-            out = part if out is None else out + part
-        s.o[:, block * 128:(block + 1) * 128] = out.astype(BF)
-    s.branch[...] = nt(s.o[...], att[:, :, :, :, 768:1280].reshape(2048, 512)).astype(BF)
-    quad = quad_reduce(
-        net, me, s.branch, s.branch_core, s.branch_zl, s.branch_tmp
-    )
-    step(quad, cots)
-    finish(quad)
-    hidden = s.tok[rows, :].astype(F32)
-    hidden = hidden + quad_total(me, s.branch, s.branch_core, s.branch_zl)
+    for q in range(2):
+        at = slice(q * 128, (q + 1) * 128)
+        kv = s.qk[at, 256:384]
+        sides = (kv, swap_halves(kv))
+        for block in range(2):
+            cols = slice(block * 128, (block + 1) * 128)
+            out = None
+            for side in range(2):
+                query = half_of(s.qk[at, cols], side)
+                score = jnp.where(causal, nt(query, sides[side]) * 0.125, -1e30)
+                e = jnp.exp(score - jnp.max(score, axis=-1, keepdims=True))
+                p = e / jnp.sum(e, axis=-1, keepdims=True)
+                s.p[q * 4 + 2 * block + side] = p
+                part = nn(p.astype(BF), half_of(sides[1 - side], side))
+                out = part if out is None else out + part
+            s.o[at, cols] = out.astype(BF)
+    branch = nt(s.o[...], att[:, :, :, :, 384:640].reshape(2048, 256)).astype(BF)
+    s.branch[...] = branch.reshape(2, 128, 2048)
+    summed = oct_reduce(net, me, s.branch, s.branch_sum)
+    step(summed, cots)
+    finish(summed)
+    hidden = s.tok[odd, rows, :].astype(F32)
+    hidden = hidden + oct_total(me, s.branch, s.branch_sum)
     s.hidden[...] = hidden
     s.xn2[z, x, c] = (hidden * rows_rms(hidden) * gain_row(1)).astype(BF)
     normed_net = Tagged(net)
     normed = torus_gather(normed_net, me, s.xn2)
-    step(normed, normed, weights, normed)
-    finish(cots)
+    step(normed, normed, normed)
+    finish(cots, weights)
     step(normed, normed)
-    finish(weights)
 
 
     def weight(m):
@@ -806,10 +911,11 @@
         swaps.append(
             net.send(s.dxn2_part.at[k, :, 1 - c], s.dxn2_sum.both.at[k], me.core())
         )
-
-
-    dxn2 = torus_reduce(net, me, s.dxn2_part, swaps, s.dxn2_sum)
-    step(dxn2)
+        if k:
+            core_sum(me, s.dxn2_part, swaps[k - 1], s.dxn2_sum, k - 1)
+
+
+    dxn2 = torus_reduce(net, me, s.dxn2_sum, "zx")
 
     def weight_grads(k):
         yk = lax.rem(y + k, 4)
@@ -854,6 +960,8 @@
     ffn_grads = reduce_ffn_grads()
     weight_grads(2)
     step(ffn_grads)
+    core_sum(me, s.dxn2_part, swaps[3], s.dxn2_sum, 3)
+    step(dxn2)
     weight_grads(1)
     weight_grads(3)
     step(ffn_grads, dxn2, dxn2)
@@ -877,111 +985,103 @@
     dh = s.cots[z, x, c].astype(F32)
     dh = dh + r * (scaled - hat * jnp.mean(scaled * hat, axis=-1, keepdims=True))
     s.dh[...] = dh
-    s.dhb[rows, :] = dh.astype(BF)
-    spread = quad_gather(net, me, s.dhb)
+    s.dhb[odd, rows, :] = dh.astype(BF)
+    spread = oct_gather(net, me, s.dhb)
     step(spread)
 
     def finish_output():
-        yield from torus_reduce(net, me, s.xn2, swaps, s.out_sum)
+        for k in range(4):
+            core_sum(me, s.xn2, swaps[k], s.out_sum, k)
+        yield from torus_reduce(net, me, s.out_sum, "zz")
         s.out[rows, :] = (s.hidden[...] + s.out_sum.total[...]).astype(BF)
         yield from quad_gather(net, me, s.out)
 
     output = finish_output()
-    step(spread, output)
+    step(spread, output, spread)
     finish(spread)
+    step(ffn_grads)
 
 
     def reduce_att_grads(k):
-        start, width, order = ATT_SLICES[k]
+        start, width = ATT_SLICES[k]
         cols = pl.ds(start, width)
-        part, both_z = s.att_part, s.both_z
-
-        def view(p, i, j):
-            yi, xi = (i, j) if order == "yx" else (j, i)
-            return part.at[p, yi, xi, :, cols]
-
+        both_z = s.both_z
         yield from order_reduce(
-            net, me, order[0], order[1], view, s.slices[k], lambda p: both_z.at[p, :, cols]
+            net, me, "x", "y", lambda p, i, j: s.att_part.at[p, j, i, :, cols], s.slices[k],
+            lambda p: both_z.at[p, odd, :, cols], lambda p: both_z.at[p, 1 - odd, :, cols],
         )
         arrivals = net.group()
-        mine_z = both_z.at[zh, :, cols]
-        theirs = both_z.at[1 - zh, :, cols]
-        net.send(theirs, s.from_z.at[zl, 1, :, cols], me.at(zh=1 - zh), arrivals)
-        net.send(theirs, s.from_z.at[zl, 1, :, cols], me.at(zh=1 - zh, zl=1 - zl), arrivals)
-        net.send(mine_z, s.from_z.at[zl, 0, :, cols], me.at(zl=1 - zl), arrivals)
+        mine_z = both_z.at[zh, :, :, cols]
+        theirs = both_z.at[1 - zh, :, :, cols]
+        dst = s.from_z.at[zl, 1, :, :, cols]
+        net.send(theirs, dst, me.at(zh=1 - zh), arrivals)
+        net.send(theirs, dst, me.at(zh=1 - zh, zl=1 - zl), arrivals)
+        net.send(mine_z, s.from_z.at[zl, 0, :, :, cols], me.at(zl=1 - zl), arrivals)
         yield
-        arrivals.wait(s.slices[k].last.at[:, 0])
-        add_refs(s.att_grads.at[zl, :, cols], [mine_z, s.from_z.at[zl, 1, :, cols]])
+        arrivals.wait(s.slices[k].last)
+        add_refs(s.att_grads.at[zl, :, :, cols], [mine_z, s.from_z.at[zl, 1, :, :, cols]])
         add_refs(
-            s.att_grads.at[1 - zl, :, cols],
-            [s.from_z.at[1 - zl, 0, :, cols], s.from_z.at[1 - zl, 1, :, cols]],
+            s.att_grads.at[1 - zl, :, :, cols],
+            [s.from_z.at[1 - zl, 0, :, :, cols], s.from_z.at[1 - zl, 1, :, :, cols]],
         )
 
-    dhb = s.dhb[...]
+    dhb = s.dhb[...].reshape(256, 2048)
     grad = tn(dhb, s.o[...]).astype(BF)
-    s.att_part[:, :, :, :, 768:1280] = grad.reshape(2, 4, 4, 64, 512)
-    slices = [reduce_att_grads(k) for k in range(4)]
-    step(slices[2], slices[3])
-    do = nn(dhb, att[:, :, :, :, 768:1280].reshape(2048, 512)).astype(BF)
+    s.att_part[:, :, :, :, 384:640] = grad.reshape(2, 4, 4, 64, 256)
+    slices = [reduce_att_grads(k) for k in range(2)]
+    step(slices[1])
+    do = nn(dhb, att[:, :, :, :, 384:640].reshape(2048, 256)).astype(BF)
     step(output)
-    v = s.v[...]
-    k = s.qk[:, 512:640]
-    k_at = {True: k, False: swap_halves(k)}
-    v_at = {True: v, False: swap_halves(v)}
-    zero = jnp.zeros((128, 128), F32)
-    dk = {True: zero, False: zero}
-    dv = {True: zero, False: zero}
-    for block in range(4):
-        dq = None
-        for side in range(2):
-            h = 2 * block + side
-            same = side == h // 4
-            p = s.p[h]
-            dob = half_of(do[:, block * 128:(block + 1) * 128], side)
-            q = half_of(s.qk[:, block * 128:(block + 1) * 128], side)
-            dp = nt(dob, v_at[same])
-            dv[same] = dv[same] + tn(p.astype(BF), dob)
-            ds = (p * (dp - jnp.sum(p * dp, axis=-1, keepdims=True))).astype(BF)
-            part = nn(ds, half_of(k_at[same], side))
-            dq = part if dq is None else dq + part
-            dk[same] = dk[same] + tn(ds, q)
-        s.d_heads[:, block * 128:(block + 1) * 128] = dq * 0.125
-    s.d_heads[:, 512:640] = (dk[True] + pltpu.roll(dk[False], 64, 1)) * 0.125
-    dvb = (dv[True] + pltpu.roll(dv[False], 64, 1)).astype(BF)
-    step(output, ffn_grads, slices[2], slices[3])
+    for q in range(2):
+        at = slice(q * 128, (q + 1) * 128)
+        kv = s.qk[at, 256:384]
+        sides = (kv, swap_halves(kv))
+        dk = [jnp.zeros((128, 128), F32)] * 2
+        dv = [jnp.zeros((128, 128), F32)] * 2
+        for block in range(2):
+            cols = slice(block * 128, (block + 1) * 128)
+            dq = None
+            for side in range(2):
+                p = s.p[q * 4 + 2 * block + side]
+                dob = half_of(do[at, cols], side)
+                query = half_of(s.qk[at, cols], side)
+                dp = nt(dob, sides[1 - side])
+                dv[side] = dv[side] + tn(p.astype(BF), dob)
+                ds = (p * (dp - jnp.sum(p * dp, axis=-1, keepdims=True))).astype(BF)
+                part = nn(ds, half_of(sides[side], side))
+                dq = part if dq is None else dq + part
+                dk[side] = dk[side] + tn(ds, query)
+            s.d_heads[at, cols] = dq * 0.125
+        dkey = (dk[0] + pltpu.roll(dk[1], 64, 1)) * 0.125
+        s.d_heads[at, 256:384] = dkey + dv[1] + pltpu.roll(dv[0], 64, 1)
+    step(output, slices[1])
     dout = s.d_heads[...]
     dn = dout * cos - partner(dout) * sin
     z_raw = s.z[...]
     r = lax.rsqrt(head_mean(z_raw * z_raw) + EPS)
     zhat = z_raw * r
     dgain = jnp.sum(dn * zhat, axis=0, keepdims=True)
-    q_pairs = dgain[:, 0:128] + dgain[:, 128:256] + dgain[:, 256:384] + dgain[:, 384:512]
+    q_pairs = dgain[:, 0:128] + dgain[:, 128:256]
     q_pairs = q_pairs + pltpu.roll(q_pairs, 64, 1)
-    k_pairs = dgain[:, 512:640]
-    k_pairs = k_pairs + pltpu.roll(k_pairs, 64, 1)
+    k_pairs = pltpu.roll(dgain[:, 256:384], 64, 1)
     dz = dn * head_gain
     dz = r * (dz - zhat * head_mean(dz * zhat))
-    low_grads = jnp.concatenate([dz.astype(BF), dvb], axis=1)
+    low_grads = jnp.where(is_value, dout, dz).astype(BF)
+    step(slices[1], ffn_grads)
     grad = tn(s.xn[...], low_grads).astype(BF)
-    s.att_part[:, :, :, :, 0:768] = grad.reshape(2, 4, 4, 64, 768)
+    s.att_part[:, :, :, :, 0:384] = grad.reshape(2, 4, 4, 64, 384)
     step(slices[0], slices[1])
-    back = nt(low_grads, att[:, :, :, :, 0:768].reshape(2048, 768))
-    s.dxn_part[...] = back.astype(BF)
-    quad = quad_reduce(net, me, s.dxn_part, s.dxn_core, s.dxn_zl, s.dxn_tmp)
-    step(quad, output)
-
-
-    def tokens_and_gains():
-        yield from quad
-        d = quad_total(me, s.dxn_part, s.dxn_core, s.dxn_zl)
-        t = s.tok[rows, :].astype(F32)
-        r = rows_rms(t)
-        hat = t * r
-        scaled = d * gain_row(0)
-        total = s.dh[...]
-        total = total + r * (scaled - hat * jnp.mean(scaled * hat, axis=-1, keepdims=True))
-        s.dx[rows, :] = total.astype(BF)
-        gain_grad = jnp.sum(d * hat, axis=0, keepdims=True)
+    gain_grad = jnp.zeros((1, 2048), F32)
+    for q in range(2):
+        at = slice(q * 128, (q + 1) * 128)
+        back = nt(low_grads[at], att[:, :, :, :, 0:384].reshape(2048, 384))
+        s.dxn_part[q] = back.astype(BF)
+        t = s.tok[q].astype(F32)
+        gain_grad = gain_grad + jnp.sum(back * (t * rows_rms(t)), axis=0, keepdims=True)
+    summed = oct_reduce(net, me, s.dxn_part, s.dxn_sum)
+    step(summed)
+
+    def gain_grads():
         sums = s.gain_sums
         for k in range(8):
             part = slice(k * 256, (k + 1) * 256)
@@ -990,8 +1090,6 @@
         row = lax.broadcasted_iota(jnp.int32, (8, 128), 0)
         head_grad = jnp.where(lanes((8, 128)) < 64, q_pairs, k_pairs)
         sums[:, 512:640] = jnp.where(row == 0, head_grad, 0.0)
-        spread = quad_gather(net, me, s.dx)
-        step(spread)
 
         def total(buf, own, devices):
             group = net.group()
@@ -999,7 +1097,6 @@
                 net.send(buf.at[own], buf.at[own], device, group)
             yield
             group.wait(buf.at[pl.ds(0, len(devices))])
-            step(spread)
             sums[...] = sum(buf[k] for k in range(1, len(devices) + 1)) + buf[0]
 
         s.gain_quad[c * 2 + zl] = sums[...]
@@ -1015,10 +1112,25 @@
             [me.step("x", k) for k in (1, 2, 3)]
             + [me.at(zh=1 - zh, x=lax.rem(x + k, 4)) for k in range(4)],
         )
-        finish(spread)
-
-    rest = tokens_and_gains()
-    finish(rest, slices[2], slices[3], output, ffn_grads, slices[0], slices[1])
+
+    gains = gain_grads()
+    step(gains, output, slices[1])
+
+
+    def input_grad():
+        yield from summed
+        d = oct_total(me, s.dxn_part, s.dxn_sum)
+        t = s.tok[odd, rows, :].astype(F32)
+        r = rows_rms(t)
+        hat = t * r
+        scaled = d * gain_row(0)
+        total = s.dh[...]
+        total = total + r * (scaled - hat * jnp.mean(scaled * hat, axis=-1, keepdims=True))
+        s.dx[rows, :] = total.astype(BF)
+        yield from quad_gather(net, me, s.dx)
+
+    rest = input_grad()
+    finish(rest, gains, slices[1], slices[0], output, ffn_grads)
     net.drain()
 
 
@@ -1046,8 +1158,15 @@
     out[...] = out_in[...]
     dx[...] = dx_in[...].astype(F32)
     for zl in range(2):
-        for ref, start, width in ((gq, 0, 512), (gk, 512, 128), (gv, 640, 128), (go, 768, 512)):
-            ref[:, zl * width:(zl + 1) * width] = att[zl, :, start:start + width].astype(F32)
+        even, odd = att[zl, 0].astype(F32), att[zl, 1].astype(F32)
+        for parity, block in enumerate((even, odd)):
+            start = zl * 512 + parity * 256
+            gq[:, start:start + 256] = block[:, 0:256]
+            go[:, start:start + 256] = block[:, 384:640]
+        even, odd = even[:, 256:384], odd[:, 256:384]
+        low = lanes(even.shape) < 64
+        gk[:, zl * 128:(zl + 1) * 128] = jnp.where(low, even, pltpu.roll(odd, 64, 1))
+        gv[:, zl * 128:(zl + 1) * 128] = jnp.where(low, pltpu.roll(even, 64, 1), odd)
     for m, ref in enumerate((gate, up, down)):
         for k in range(8):
             for c in range(2):
@@ -1072,20 +1191,20 @@
 
 
 def finished(r):
-    tall = rows_block(32, 2048)
-    full, half, wide = (rows_block(16, n) for n in (1024, 256, 4096))
+    tall = rows_block(64, 2048)
+    full, half, wide = (rows_block(32, n) for n in (1024, 256, 4096))
     one = whole_block(1, 64)
     sizes = [(64, 1024), (64, 256), (64, 256), (64, 1024)] + [(64, 4096)] * 3 + [(1, 64)] * 4
     return pl.pallas_call(
         finish_kernel,
-        grid=(4,),
+        grid=(2,),
         out_shape=(
             jax.ShapeDtypeStruct((128, 2048), BF),
             jax.ShapeDtypeStruct((128, 2048), F32),
         )
         + tuple(jax.ShapeDtypeStruct(size, F32) for size in sizes),
         in_specs=[
-            tall, tall, rows_block(2, 16, 1280), rows_block(3, 8, 2, 16, 256), whole_block(8, 640),
+            tall, tall, rows_block(2, 2, 32, 640), rows_block(3, 8, 2, 32, 256), whole_block(8, 640),
         ],
         out_specs=[tall, tall, full, half, half, full, wide, wide, wide, one, one, one, one],
         name="finished",

time: 187 us -> 182 us (0.973)
  Pallas kernels: 184 us -> 179 us
    pallas_call x1, Pallas kernels: 179 us -> 175 us  [everything(): pl.pallas_call(kernel, out_shape=tuple(out_shapes), in_specs=in_specs, ou...]
where the time goes in v4:
time: 182 us
  Pallas kernels  179 us (98%)
    pallas_call x1, Pallas kernels, everything(): pl.pallas_call(kernel, out_shape=tuple(out_shapes), in_specs=in_specs, ou...  175 us
    pallas_call x1, Pallas kernels, finished(): pl.pallas_call(finish_kernel, grid=(2,), out_shape=(jax.ShapeDtypeStruct(...  3.83 us

profile of v4, /device:TPU:0, one launch (start us, length us, event | category | flops | bytes accessed | tf_op | source)
XLA Modules:
  0.0 181.6 jit_solution(18066122586116751685)
XLA Ops:
  0.6 0.7 pad_bitcast_fusion.1
  1.3 0.8 maximum_bitcast_fusion
  2.1 0.6 fusion.4.refs_3_
  2.7 174.9 %everything.1 = (bf16[2,2,64,640]{3,2,1,0:T(8,128)(2,1)}, bf16[128,2048]{1,0:T(8,128)(2,1)}, bf16[3,8,2,64,256]{4,3,2,1,0:T(8,128)(2,1)}, f32[8,640]{1,0:T(8,128)}, bf16[128,2048]{1,0:T(8,128)(2,1)}) custom-call(f32[128,128]{1,0:T(8,128)} %constant.7.clone.refs_0_, bf16[128,2048]{1,0:T(8,128)(2,1)} %refs_1_.1, f32[128,128]{1,0:T(8,128)} %constant.8.clone.refs_2_, ...), custom_call_target="tpu_custom_call" | custom-call | tf_op jit(solution)/shard_map/everything/pallas_call | solution.py:1140
  177.6 3.8 %finished.1 = (bf16[128,2048]{1,0:T(8,128)(2,1)}, f32[128,2048]{1,0:T(8,128)}, f32[64,1024]{1,0:T(8,128)}, f32[64,256]{1,0:T(8,128)}, f32[64,256]{1,0:T(8,128)},...) custom-call(bf16[128,2048]{1,0:T(8,128)(2,1)} %get-tuple-element.31., ...), custom_call_target="tpu_custom_call" | custom-call | tf_op jit(solution)/shard_map/finished/pallas_call | solution.py:1198

commit v5 on v4

--- a/solution.py
+++ b/solution.py
@@ -450,7 +450,8 @@
 
 def oct_reduce(net, place, src, b):
     c, zl, q = place.c, place.zl, place.odd
-    one = net.send(src.at[:, pl.ds((1 - c) * 64, 64)], b.core, place.core())
+    theirs = pl.ds((1 - c) * 64, 64)
+    one = net.send(src.at[1 - q, theirs], b.core.at[1 - q], place.core())
     yield
     one.wait_recv()
     b.for_y[...] = (
@@ -459,6 +460,9 @@
     far, near = pl.ds((1 - zl) * 32, 32), pl.ds(zl * 32, 32)
     two = [net.send(b.for_y.at[r], b.y.at[r], place.y_pair()) for r in (far, near)]
     yield
+    one = net.send(src.at[q, theirs], b.core.at[q], place.core())
+    yield
+    one.wait_recv()
     two[0].wait_recv()
     theirs = src[q, pl.ds(c * 64 + (1 - zl) * 32, 32), :].astype(F32)
     theirs = theirs + b.core[q, far, :].astype(F32) + b.y[far, :].astype(F32)
@@ -508,15 +512,16 @@
     other = buf.at[q, pl.ds(c * 64 + (1 - zl) * 32, 32)]
     from_y.append(net.send(other, other, place.y_pair()))
     half = buf.at[q, pl.ds(c * 64, 64)]
-    from_core = [net.send(half, half, place.core())]
+    from_core = net.send(half, half, place.core())
+    yield
+    from_core.wait_recv()
     yield
     for copy in from_y:
         copy.wait_recv()
     half = buf.at[1 - q, pl.ds(c * 64, 64)]
-    from_core.append(net.send(half, half, place.core()))
-    yield
-    for copy in from_core:
-        copy.wait_recv()
+    from_core = net.send(half, half, place.core())
+    yield
+    from_core.wait_recv()
 
 
 def sem_scratch(n):
@@ -562,7 +567,7 @@
 
 
 N_SENDS = 48
-N_GROUPS = 147
+N_GROUPS = 149
 N_LOCAL = 17
 
 
@@ -841,7 +846,7 @@
     step(cots)
     raw = nn(s.xn[...], att[:, :, :, :, 0:384].reshape(2048, 384))
     s.z[...] = raw
-    step(weights, cots)
+    step(cots)
     both_gains = small[2:3, :]
     turned = pltpu.roll(both_gains, 64, 1)
     low = lanes((1, 128)) < 64
@@ -856,8 +861,9 @@
     s.qk[...] = jnp.where(is_value, raw, n * cos + partner(n) * sin).astype(BF)
     step(cots)
     causal = lax.broadcasted_iota(jnp.int32, (128, 128), 0) >= lanes((128, 128))
-    for q in range(2):
-        at = slice(q * 128, (q + 1) * 128)
+
+    def attend(q):
+        at = pl.ds(pl.multiple_of(q * 128, 128), 128)
         kv = s.qk[at, 256:384]
         sides = (kv, swap_halves(kv))
         for block in range(2):
@@ -872,10 +878,20 @@
                 part = nn(p.astype(BF), half_of(sides[1 - side], side))
                 out = part if out is None else out + part
             s.o[at, cols] = out.astype(BF)
-    branch = nt(s.o[...], att[:, :, :, :, 384:640].reshape(2048, 256)).astype(BF)
-    s.branch[...] = branch.reshape(2, 128, 2048)
+
+    def project(q):
+        at = pl.ds(pl.multiple_of(q * 128, 128), 128)
+        branch = nt(s.o[at, :], att[:, :, :, :, 384:640].reshape(2048, 256))
+        s.branch[q] = branch.astype(BF)
+
+    attend(1 - odd)
+    project(1 - odd)
     summed = oct_reduce(net, me, s.branch, s.branch_sum)
-    step(summed, cots)
+    step(summed)
+    attend(odd)
+    step(summed)
+    project(odd)
+    step(summed, cots, weights)
     finish(summed)
     hidden = s.tok[odd, rows, :].astype(F32)
     hidden = hidden + oct_total(me, s.branch, s.branch_sum)
@@ -998,8 +1014,6 @@
 
     output = finish_output()
     step(spread, output, spread)
-    finish(spread)
-    step(ffn_grads)
 
 
     def reduce_att_grads(k):
@@ -1025,15 +1039,9 @@
             [s.from_z.at[1 - zl, 0, :, :, cols], s.from_z.at[1 - zl, 1, :, :, cols]],
         )
 
-    dhb = s.dhb[...].reshape(256, 2048)
-    grad = tn(dhb, s.o[...]).astype(BF)
-    s.att_part[:, :, :, :, 384:640] = grad.reshape(2, 4, 4, 64, 256)
-    slices = [reduce_att_grads(k) for k in range(2)]
-    step(slices[1])
-    do = nn(dhb, att[:, :, :, :, 384:640].reshape(2048, 256)).astype(BF)
-    step(output)
-    for q in range(2):
-        at = slice(q * 128, (q + 1) * 128)
+    def attend_back(q):
+        at = pl.ds(pl.multiple_of(q * 128, 128), 128)
+        do = nn(s.dhb[q], att[:, :, :, :, 384:640].reshape(2048, 256)).astype(BF)
         kv = s.qk[at, 256:384]
         sides = (kv, swap_halves(kv))
         dk = [jnp.zeros((128, 128), F32)] * 2
@@ -1043,7 +1051,7 @@
             dq = None
             for side in range(2):
                 p = s.p[q * 4 + 2 * block + side]
-                dob = half_of(do[at, cols], side)
+                dob = half_of(do[:, cols], side)
                 query = half_of(s.qk[at, cols], side)
                 dp = nt(dob, sides[1 - side])
                 dv[side] = dv[side] + tn(p.astype(BF), dob)
@@ -1054,6 +1062,15 @@
             s.d_heads[at, cols] = dq * 0.125
         dkey = (dk[0] + pltpu.roll(dk[1], 64, 1)) * 0.125
         s.d_heads[at, 256:384] = dkey + dv[1] + pltpu.roll(dv[0], 64, 1)
+
+    attend_back(odd)
+    step(spread, ffn_grads)
+    finish(spread)
+    grad = tn(s.dhb[...].reshape(256, 2048), s.o[...]).astype(BF)
+    s.att_part[:, :, :, :, 384:640] = grad.reshape(2, 4, 4, 64, 256)
+    slices = [reduce_att_grads(k) for k in range(2)]
+    step(slices[1], output)
+    attend_back(1 - odd)
     step(output, slices[1])
     dout = s.d_heads[...]
     dn = dout * cos - partner(dout) * sin

time: 182 us -> 180 us (0.989)
  Pallas kernels: 179 us -> 177 us
where the time goes in v5:
time: 180 us
  Pallas kernels  177 us (98%)
    pallas_call x1, Pallas kernels, everything(): pl.pallas_call(kernel, out_shape=tuple(out_shapes), in_specs=in_specs, ou...  174 us
    pallas_call x1, Pallas kernels, finished(): pl.pallas_call(finish_kernel, grid=(2,), out_shape=(jax.ShapeDtypeStruct(...  3.83 us

profile of v5, /device:TPU:0, one launch (start us, length us, event | category | flops | bytes accessed | tf_op | source)
XLA Modules:
  0.0 180.2 jit_solution(15848796938895955062)
XLA Ops:
  0.6 0.7 pad_bitcast_fusion.1
  1.3 0.8 maximum_bitcast_fusion
  2.1 0.6 fusion.4.refs_3_
  2.7 173.5 %everything.1 = (bf16[2,2,64,640]{3,2,1,0:T(8,128)(2,1)}, bf16[128,2048]{1,0:T(8,128)(2,1)}, bf16[3,8,2,64,256]{4,3,2,1,0:T(8,128)(2,1)}, f32[8,640]{1,0:T(8,128)}, bf16[128,2048]{1,0:T(8,128)(2,1)}) custom-call(f32[128,128]{1,0:T(8,128)} %constant.7.clone.refs_0_, bf16[128,2048]{1,0:T(8,128)(2,1)} %refs_1_.1, f32[128,128]{1,0:T(8,128)} %constant.8.clone.refs_2_, ...), custom_call_target="tpu_custom_call" | custom-call | tf_op jit(solution)/shard_map/everything/pallas_call | solution.py:1157
  176.2 3.8 %finished.1 = (bf16[128,2048]{1,0:T(8,128)(2,1)}, f32[128,2048]{1,0:T(8,128)}, f32[64,1024]{1,0:T(8,128)}, f32[64,256]{1,0:T(8,128)}, f32[64,256]{1,0:T(8,128)},...) custom-call(bf16[128,2048]{1,0:T(8,128)(2,1)} %get-tuple-element.31., ...), custom_call_target="tpu_custom_call" | custom-call | tf_op jit(solution)/shard_map/finished/pallas_call | solution.py:1215

commit v6 on v5

--- a/solution.py
+++ b/solution.py
@@ -847,7 +847,7 @@
     raw = nn(s.xn[...], att[:, :, :, :, 0:384].reshape(2048, 384))
     s.z[...] = raw
     step(cots)
-    both_gains = small[2:3, :]
+    both_gains = small[2:3, :] + pltpu.roll(small[3:4, :], 64, 1)
     turned = pltpu.roll(both_gains, 64, 1)
     low = lanes((1, 128)) < 64
     gain_q = jnp.where(low, both_gains, turned)
@@ -1241,9 +1241,7 @@
     w_gate, w_up, w_down, cotangent,
 ):
     cos, sin = (jnp.asarray(t) for t in rotary_tables())
-    rows = [jnp.pad(v, (0, 64)).reshape(1, 128) for v in (gain_attn, gain_ffn)]
-    rows.append(jnp.concatenate([gain_query, gain_key]).reshape(1, 128))
-    small = jnp.pad(jnp.concatenate(rows, axis=0), ((0, 13), (0, 0)))
+    small = jnp.pad(jnp.stack([gain_attn, gain_ffn, gain_query, gain_key]), ((0, 12), (0, 64)))
     r = everything(
         tokens=tokens, cot=cotangent, small=small, cos=cos, sin=sin,
         wq=w_query, wk=w_key, wv=w_value, wo=w_out, wg=w_gate, wu=w_up, wd=w_down,

time: 180 us -> 180 us (level)
  no operation moved by 1% of the time
where the time goes in v6:
time: 180 us; the launch traced here: 179 us
  Pallas kernels  177 us (98%)
    pallas_call x1, Pallas kernels, everything(): pl.pallas_call(kernel, out_shape=tuple(out_shapes), in_specs=in_specs, ou...  173 us
    pallas_call x1, Pallas kernels, finished(): pl.pallas_call(finish_kernel, grid=(2,), out_shape=(jax.ShapeDtypeStruct(...  3.83 us

profile of v6, /device:TPU:0, one launch (start us, length us, event | category | flops | bytes accessed | tf_op | source)
XLA Modules:
  0.0 179.3 jit_solution(6388419086514827785)
XLA Ops:
  0.6 1.3 fusion.8.refs_3_
  2.0 173.3 %everything.1 = (bf16[2,2,64,640]{3,2,1,0:T(8,128)(2,1)}, bf16[128,2048]{1,0:T(8,128)(2,1)}, bf16[3,8,2,64,256]{4,3,2,1,0:T(8,128)(2,1)}, f32[8,640]{1,0:T(8,128)}, bf16[128,2048]{1,0:T(8,128)(2,1)}) custom-call(f32[128,128]{1,0:T(8,128)} %constant.7.clone.refs_0_, bf16[128,2048]{1,0:T(8,128)(2,1)} %refs_1_.1, f32[128,128]{1,0:T(8,128)} %constant.8.clone.refs_2_, ...), custom_call_target="tpu_custom_call" | custom-call | tf_op jit(solution)/shard_map/everything/pallas_call | solution.py:1157
  175.3 3.8 %finished.1 = (bf16[128,2048]{1,0:T(8,128)(2,1)}, f32[128,2048]{1,0:T(8,128)}, f32[64,1024]{1,0:T(8,128)}, f32[64,256]{1,0:T(8,128)}, f32[64,256]{1,0:T(8,128)},...) custom-call(bf16[128,2048]{1,0:T(8,128)(2,1)} %get-tuple-element.31., ...), custom_call_target="tpu_custom_call" | custom-call | tf_op jit(solution)/shard_map/finished/pallas_call | solution.py:1215
